TPU v7x, 128 devices: a whole 4x4x4 slice. The times are simulated.
128 devices in a mesh: cuts: 4 (over z), tile: 32 (over y, x, core).
Axes of the slice: x: 4, y: 4, z: 4, core: 2. Of those that a mesh axis runs over, the one named last changes fastest.
Arguments:
- start_states: float32 [4, 3, 512, 2048], P('cuts', None, 'tile'), may hold values from -6 to 6
Outputs:
- next_states: float32 [4, 3, 512, 2048], P('cuts', None, 'tile')
All inputs are finite; a program needn't handle non-finite values.
Results may differ from a plain program's by a relative error of at most 0.0001.
Values sent between devices are 32-bit elements; how exact they have to be, the bound alone decides.
No kernel may reach another device: no remote copies, remote signals or barrier semaphores. Data moves between devices by JAX's collectives and lax.ppermute only.
A program may use at most 128 MiB of HBM per device.

v0:
```python
import jax
import jax.numpy as jnp
from jax import lax
from jax.sharding import PartitionSpec as P

STEPS = 3


FINE_SPACING = 0.05
COARSE_SPACING = 0.1
FINE_STEP = 0.015
COARSE_STEP = 0.045


def extended(shard, sides, width):
    for axis, dim in sides:
        size, length = (lax.axis_size(axis), shard.shape[dim])
        up = [(i, (i + 1) % size) for i in range(size - 1)]
        down = [(j, i) for i, j in up]
        last = lax.slice_in_dim(shard, length - width, length, axis=dim)
        first = lax.slice_in_dim(shard, 0, width, axis=dim)
        before = lax.ppermute(last, axis, up)
        after = lax.ppermute(first, axis, down)
        shard = jnp.concatenate([before, shard, after], axis=dim)
    return shard


def passed_along(block, axis, distance):
    devices = range(lax.axis_size(axis))
    route = [(i - distance, i) for i in devices if i - distance in devices]
    return lax.ppermute(block, axis, route)


def depth_profile(columns, stride, length):
    centers = (jnp.arange(columns).astype(jnp.float32) + 0.5) * stride
    return 0.9 + 0.3 * jnp.sin(6.0 * jnp.pi * centers / length)


def along_x(values, spacing):
    padded = jnp.pad(values, [(0, 0)] * (values.ndim - 1) + [(1, 1)])
    return (padded[..., 2:] - padded[..., :-2]) / (2.0 * spacing)


def along_y(values, spacing):
    padded = jnp.pad(values, [(0, 0)] * (values.ndim - 2) + [(1, 1), (0, 0)])
    return (padded[..., 2:, :] - padded[..., :-2, :]) / (2.0 * spacing)


def second_y(values):
    padded = jnp.pad(values, [(0, 0)] * (values.ndim - 2) + [(1, 1), (0, 0)])
    return padded[..., 2:, :] - 2.0 * values + padded[..., :-2, :]


def reduce_lines(lower, middle, upper, rhs):
    length = rhs.shape[-1]
    if length == 1:
        return rhs / middle
    leading = rhs.shape[:-1]
    pairs = rhs.reshape(leading + (length // 2, 2))
    rhs_even = pairs[..., 0]
    rhs_odd = pairs[..., 1]
    lower_even = lower[0::2]
    lower_odd = lower[1::2]
    middle_even = middle[0::2]
    middle_odd = middle[1::2]
    upper_even = upper[0::2]
    upper_odd = upper[1::2]
    one_more = jnp.ones((1,), jnp.float32)
    no_more = jnp.zeros((1,), jnp.float32)
    middle_after = jnp.concatenate([middle_even[1:], one_more])
    lower_after = jnp.concatenate([lower_even[1:], no_more])
    upper_after = jnp.concatenate([upper_even[1:], no_more])
    rhs_after = jnp.concatenate(
        [rhs_even[..., 1:], jnp.zeros(leading + (1,), jnp.float32)], axis=-1
    )
    alpha = -lower_odd / middle_even
    gamma = -upper_odd / middle_after
    new_lower = alpha * lower_even
    new_middle = middle_odd + alpha * upper_even + gamma * lower_after
    new_upper = gamma * upper_after
    new_rhs = rhs_odd + alpha * rhs_even + gamma * rhs_after
    solved_odd = reduce_lines(new_lower, new_middle, new_upper, new_rhs)
    odd_before = jnp.concatenate(
        [jnp.zeros(leading + (1,), jnp.float32), solved_odd[..., :-1]], axis=-1
    )
    solved_even = (rhs_even - lower_even * odd_before - upper_even * solved_odd) / middle_even
    return jnp.stack([solved_even, solved_odd], axis=-1).reshape(leading + (length,))


def solve_lines(forcing, seabed, spacing):
    columns = forcing.shape[-1]
    coupling = seabed * seabed / (3.0 * spacing * spacing)
    below_diag = (-coupling).at[0].set(0.0)
    above_diag = (-coupling).at[columns - 1].set(0.0)
    middle = 1.0 + 2.0 * coupling
    solved = reduce_lines(below_diag, middle, above_diag, forcing)
    return solved


def wave_step(fields, seabed, spacing, time_step, inside):
    height = fields[0]
    flux_x = fields[1]
    flux_y = fields[2]
    height_new = (
        height - time_step * (along_x(flux_x, spacing) + along_y(flux_y, spacing))
    ) * inside
    forcing = jnp.stack(
        [
            flux_x - time_step * seabed * along_x(height_new, spacing),
            flux_y - time_step * seabed * along_y(height_new, spacing),
        ],
        axis=0,
    )
    trial_flux = solve_lines(forcing, seabed, spacing) * inside
    dispersion = seabed * seabed / 3.0
    weight = dispersion / (spacing * spacing + 4.0 * dispersion)
    fluxes_new = (trial_flux + weight * second_y(trial_flux - fields[1:])) * inside
    return jnp.concatenate([height_new[None], fluxes_new], axis=0)


def restrict(fields):
    planes = fields.shape[0]
    row_count = fields.shape[1]
    columns = fields.shape[2]
    blocks = fields.reshape(planes, row_count // 2, 2, columns // 2, 2)
    return 0.25 * jnp.sum(blocks, axis=(2, 4))


def prolong(coarse):
    return jnp.repeat(jnp.repeat(coarse, 2, axis=1), 2, axis=2)


def per_device(start_states):
    fields = start_states[0]
    row_count = fields.shape[1]
    columns = fields.shape[2]
    tile_count = lax.axis_size("tile")
    first_row = lax.axis_index("tile") * row_count
    total_rows = row_count * tile_count
    fine_depth = depth_profile(columns, 1.0, columns)
    coarse_depth = depth_profile(columns // 2, 2.0, columns)

    def row_mask(local_rows, margin, factor):
        offsets = (
            jnp.arange(local_rows + 2 * margin, dtype=jnp.int32) - margin + first_row // factor
        )
        return ((offsets >= 0) & (offsets < total_rows // factor)).astype(jnp.float32)[:, None]

    inside = row_mask(row_count, 3, 1)
    fine_end = fields
    for substep in range(STEPS):
        widened = extended(fine_end, (("tile", 1),), 3)
        fine_end = wave_step(widened, fine_depth, FINE_SPACING, FINE_STEP, inside)[
            :, 3 : 3 + row_count
        ]
    coarse_rows = row_count // 2
    coarse_inside = row_mask(coarse_rows, 3, 2)

    def coarse_step(values):
        widened_coarse = extended(values, (("tile", 1),), 3)
        return wave_step(widened_coarse, coarse_depth, COARSE_SPACING, COARSE_STEP, coarse_inside)[
            :, 3 : 3 + coarse_rows
        ]

    restricted_start = restrict(fields)
    restricted_end = restrict(fine_end)

    def propagate(current):
        return coarse_step(current - restricted_start)

    cut_index = lax.axis_index("cuts")
    slices = lax.axis_size("cuts")
    current = restricted_start
    for link_step in range(slices - 1):
        arrived = passed_along(propagate(current) + restricted_end, "cuts", 1)
        current = jnp.where(cut_index == link_step + 1, arrived, current)
    return (prolong(propagate(current)) + fine_end)[None]


def solution(mesh):
    in_specs = (P("cuts", None, "tile", None),)
    out_specs = P("cuts", None, "tile", None)
    return jax.shard_map(
        per_device, mesh=mesh, in_specs=in_specs, out_specs=out_specs, check_vma=False
    )
```

profile of v0, /device:TPU:16, one launch (start us, length us, event | category | flops | bytes accessed | tf_op | source)
XLA Modules:
  0.0 424.9 jit_solution(10509147231240296361)
XLA Ops:
  1.1 1.9 collective-permute-start.2
  3.0 5.8 %collective-permute-start.3 = (f32[3,3,2048]{2,1,0:T(4,128)S(1)}, f32[3,3,2048]{2,1,0:T(4,128)S(1)}, u32[]{:S(2)}, u32[]{:S(2)}) collective-permute-start(f32[3,3,2048]{2,1,0:T(4,128)S(1)} %get-tuple-element.267), channel_id=1, source_target_pairs={{1,0},{2,1},{3,2},{4,3},{5,4},{6,5},{7,6},{8,7},{9,8},{10,9},{11,1... | collective-permute-start | bytes 221192 | tf_op jit(solution)/shard_map/ppermute | solution.py:23
  8.7 28.5 %reshape_squeeze.3 = f32[3,8,2,1024,2]{4,3,2,1,0:T(8,128)} reshape(f32[1,3,16,2048]{3,2,1,0:T(8,128)} %param.29) | data formatting | bytes 786432 | tf_op jit(solution)/shard_map/reshape;squeeze | solution.py:125
  37.2 10.2 %reduce_sum.18 = f32[3,8,1024]{2,1,0:T(8,128)S(1)} reduce(f32[3,8,2,1024,2]{4,3,2,1,0:T(8,128)} %reshape_squeeze.3, f32[]{:T(128)} %constant.343.clone.1), dimensions={2,4}, to_apply=%region_0.1 | reduce | flops 73728 | bytes 491524 | tf_op jit(solution)/shard_map/reduce_sum | solution.py:126
  47.5 1.9 collective-permute-start
  49.4 6.2 %collective-permute-start.1 = (f32[3,3,1024]{2,1,0:T(4,128)S(1)}, f32[3,3,1024]{2,1,0:T(4,128)S(1)}, u32[]{:S(2)}, u32[]{:S(2)}) collective-permute-start(f32[3,3,1024]{2,1,0:T(4,128)S(1)} %get-tuple-element.319), channel_id=1, source_target_pairs={{1,0},{2,1},{3,2},{4,3},{5,4},{6,5},{7,6},{8,7},{9,8},{10,9},{11,1... | collective-permute-start | bytes 110600 | tf_op jit(solution)/shard_map/ppermute | solution.py:23
  179.9 2.1 pad_maximum_fusion.4
  196.2 2.0 copy.1606
  200.0 2.8 add_multiply_fusion.2
  202.8 2.2 copy.1365
  207.3 6.2 %collective-permute-start.5 = (f32[3,3,2048]{2,1,0:T(4,128)S(1)}, f32[3,3,2048]{2,1,0:T(4,128)S(1)}, u32[]{:S(2)}, u32[]{:S(2)}) collective-permute-start(f32[3,3,2048]{2,1,0:T(4,128)S(1)} %get-tuple-element.248), channel_id=1, source_target_pairs={{1,0},{2,1},{3,2},{4,3},{5,4},{6,5},{7,6},{8,7},{9,8},{10,9},{11,1... | collective-permute-start | bytes 221192 | tf_op jit(solution)/shard_map/ppermute | solution.py:23
  236.0 2.0 copy.1626
  239.9 2.9 add_multiply_fusion.1
  242.8 2.2 copy.1408
  247.3 5.8 %collective-permute-start.7 = (f32[3,3,2048]{2,1,0:T(4,128)S(1)}, f32[3,3,2048]{2,1,0:T(4,128)S(1)}, u32[]{:S(2)}, u32[]{:S(2)}) collective-permute-start(f32[3,3,2048]{2,1,0:T(4,128)S(1)} %get-tuple-element.243), channel_id=1, source_target_pairs={{1,0},{2,1},{3,2},{4,3},{5,4},{6,5},{7,6},{8,7},{9,8},{10,9},{11,1... | collective-permute-start | bytes 221192 | tf_op jit(solution)/shard_map/ppermute | solution.py:23
  276.2 2.0 copy.1638
  283.2 2.6 pad_maximum_fusion
  285.7 2.3 copy.1454
  288.0 27.6 %reshape.1034 = f32[3,8,2,1024,2]{4,3,2,1,0:T(8,128)} reshape(f32[3,16,2048]{2,1,0:T(8,128)S(1)} %copy.1454) | data formatting | bytes 786432 | tf_op jit(solution)/shard_map/reshape | solution.py:125
  315.7 10.2 %reduce_sum.19 = f32[3,8,1024]{2,1,0:T(8,128)S(1)} reduce(f32[3,8,2,1024,2]{4,3,2,1,0:T(8,128)} %reshape.1034, f32[]{:T(128)} %constant.343.clone.1), dimensions={2,4}, to_apply=%region_1.2 | reduce | flops 73728 | bytes 491524 | tf_op jit(solution)/shard_map/reduce_sum | solution.py:126
  326.0 3.8 collective-permute-start.8
  329.9 2.2 collective-permute-done.8
  332.1 5.0 %collective-permute-start.10 = (f32[3,3,1024]{2,1,0:T(4,128)S(1)}, f32[3,3,1024]{2,1,0:T(4,128)S(1)}, u32[]{:S(2)}, u32[]{:S(2)}) collective-permute-start(f32[3,3,1024]{2,1,0:T(4,128)S(1)} %get-tuple-element.317), channel_id=1, source_target_pairs={{1,0},{2,1},{3,2},{4,3},{5,4},{6,5},{7,6},{8,7},{9,8},{10,9},{11,1... | collective-permute-start | bytes 110600 | tf_op jit(solution)/shard_map/ppermute | solution.py:23
  339.0 5.6 %collective-permute-done.9 = f32[3,3,1024]{2,1,0:T(4,128)S(1)} collective-permute-done((f32[3,3,1024]{2,1,0:T(4,128)S(1)}, f32[3,3,1024]{2,1,0:T(4,128)S(1)}, u32[]{:S(2)}, u32[]{:S(2)}) %collective-permute-start.9) | collective-permute-done | bytes 36896 | tf_op jit(solution)/shard_map/ppermute | solution.py:22
  358.5 4.0 collective-permute-start.11
  362.5 2.2 collective-permute-done.11
  366.7 5.9 %collective-permute-start.13 = (f32[3,3,1024]{2,1,0:T(4,128)S(1)}, f32[3,3,1024]{2,1,0:T(4,128)S(1)}, u32[]{:S(2)}, u32[]{:S(2)}) collective-permute-start(f32[3,3,1024]{2,1,0:T(4,128)S(1)} %get-tuple-element.315), channel_id=1, source_target_pairs={{1,0},{2,1},{3,2},{4,3},{5,4},{6,5},{7,6},{8,7},{9,8},{10,9},{11,1... | collective-permute-start | bytes 110600 | tf_op jit(solution)/shard_map/ppermute | solution.py:23
  387.6 4.3 %collective-permute-start.14 = (f32[3,8,1024]{2,1,0:T(8,128)S(1)}, f32[3,8,1024]{2,1,0:T(8,128)S(1)}, u32[]{:S(2)}, u32[]{:S(2)}) collective-permute-start(f32[3,8,1024]{2,1,0:T(8,128)S(1)} %fusion.17), channel_id=1, source_target_pairs={{0,32},{32,64},{64,96},{1,33},{33,65},{65,97},{2,34},{34,66},{66,9... | collective-permute-start | bytes 294920 | tf_op jit(solution)/shard_map/ppermute | solution.py:31
  391.9 2.2 collective-permute-done.14
  396.1 5.8 %collective-permute-start.16 = (f32[3,3,1024]{2,1,0:T(4,128)S(1)}, f32[3,3,1024]{2,1,0:T(4,128)S(1)}, u32[]{:S(2)}, u32[]{:S(2)}) collective-permute-start(f32[3,3,1024]{2,1,0:T(4,128)S(1)} %get-tuple-element.313), channel_id=1, source_target_pairs={{1,0},{2,1},{3,2},{4,3},{5,4},{6,5},{7,6},{8,7},{9,8},{10,9},{11,1... | collective-permute-start | bytes 110600 | tf_op jit(solution)/shard_map/ppermute | solution.py:23
  419.2 2.6 add_bitcast_fusion
  421.7 3.0 copy.1573
  (1223 shorter events, 237.1 us)
Async XLA Ops:
  1.1 173.0 %collective-permute-start.2 = (f32[3,3,2048]{2,1,0:T(4,128)S(1)}, f32[3,3,2048]{2,1,0:T(4,128)S(1)}, u32[]{:S(2)}, u32[]{:S(2)}) collective-permute-start(f32[3,3,2048]{2,1,0:T(4,128)S(1)} %get-tuple-element.266), channel_id=1, source_target_pairs={{0,1},{1,2},{2,3},{3,4},{4,5},{5,6},{6,7},{7,8},{8,9},{9,10},{10,1... | collective-permute-start | bytes 221192 | tf_op jit(solution)/shard_map/ppermute | solution.py:22
  3.0 171.1 %collective-permute-start.3 = (f32[3,3,2048]{2,1,0:T(4,128)S(1)}, f32[3,3,2048]{2,1,0:T(4,128)S(1)}, u32[]{:S(2)}, u32[]{:S(2)}) collective-permute-start(f32[3,3,2048]{2,1,0:T(4,128)S(1)} %get-tuple-element.267), channel_id=1, source_target_pairs={{1,0},{2,1},{3,2},{4,3},{5,4},{6,5},{7,6},{8,7},{9,8},{10,9},{11,1... | collective-permute-start | bytes 221192 | tf_op jit(solution)/shard_map/ppermute | solution.py:23
  47.4 113.4 %copy-start.5 = (f32[3,8,1024]{2,1,0:T(8,128)}, f32[3,8,1024]{2,1,0:T(8,128)S(1)}, u32[]{:S(2)}) copy-start(f32[3,8,1024]{2,1,0:T(8,128)S(1)} %reduce_sum.18) | copy-start | bytes 294916
  47.5 111.0 %collective-permute-start = (f32[3,3,1024]{2,1,0:T(4,128)S(1)}, f32[3,3,1024]{2,1,0:T(4,128)S(1)}, u32[]{:S(2)}, u32[]{:S(2)}) collective-permute-start(f32[3,3,1024]{2,1,0:T(4,128)S(1)} %get-tuple-element.318), channel_id=1, source_target_pairs={{0,1},{1,2},{2,3},{3,4},{4,5},{5,6},{6,7},{7,8},{8,9},{9,10},{10,1... | collective-permute-start | bytes 110600 | tf_op jit(solution)/shard_map/ppermute | solution.py:22
  49.4 109.0 %collective-permute-start.1 = (f32[3,3,1024]{2,1,0:T(4,128)S(1)}, f32[3,3,1024]{2,1,0:T(4,128)S(1)}, u32[]{:S(2)}, u32[]{:S(2)}) collective-permute-start(f32[3,3,1024]{2,1,0:T(4,128)S(1)} %get-tuple-element.319), channel_id=1, source_target_pairs={{1,0},{2,1},{3,2},{4,3},{5,4},{6,5},{7,6},{8,7},{9,8},{10,9},{11,1... | collective-permute-start | bytes 110600 | tf_op jit(solution)/shard_map/ppermute | solution.py:23
  57.2 124.8 %copy-start.23 = (f32[1024]{0:T(1024)}, f32[1024]{0:T(1024)S(1)}, u32[]{:S(2)}) copy-start(f32[1024]{0:T(1024)S(1)} %get-tuple-element.182) | copy-start | bytes 12292
  57.4 135.2 %copy-start.37 = (f32[512]{0:T(512)}, f32[512]{0:T(512)S(1)}, u32[]{:S(2)}) copy-start(f32[512]{0:T(512)S(1)} %slice.2481) | copy-start | bytes 6148
  57.8 124.2 %copy-start.26 = (f32[1024]{0:T(1024)}, f32[1024]{0:T(1024)S(1)}, u32[]{:S(2)}) copy-start(f32[1024]{0:T(1024)S(1)} %get-tuple-element.184) | copy-start | bytes 12292
  58.0 134.6 %copy-start.40 = (f32[512]{0:T(512)}, f32[512]{0:T(512)S(1)}, u32[]{:S(2)}) copy-start(f32[512]{0:T(512)S(1)} %slice.2497) | copy-start | bytes 6148
  58.6 134.1 %copy-start.43 = (f32[512]{0:T(512)}, f32[512]{0:T(512)S(1)}, u32[]{:S(2)}) copy-start(f32[512]{0:T(512)S(1)} %slice.2487) | copy-start | bytes 6148
  59.1 112.4 %copy-start.29 = (f32[512]{0:T(512)}, f32[512]{0:T(512)S(1)}, u32[]{:S(2)}) copy-start(f32[512]{0:T(512)S(1)} %slice.2331) | copy-start | bytes 6148
  59.6 112.0 %copy-start.31 = (f32[512]{0:T(512)}, f32[512]{0:T(512)S(1)}, u32[]{:S(2)}) copy-start(f32[512]{0:T(512)S(1)} %slice.2343) | copy-start | bytes 6148
  60.0 111.5 %copy-start.33 = (f32[512]{0:T(512)}, f32[512]{0:T(512)S(1)}, u32[]{:S(2)}) copy-start(f32[512]{0:T(512)S(1)} %slice.2334) | copy-start | bytes 6148
  60.6 100.2 %copy-start.68 = (f32[256]{0:T(256)}, f32[256]{0:T(256)S(1)}, u32[]{:S(2)}) copy-start(f32[256]{0:T(256)S(1)} %slice.2493) | copy-start | bytes 3076
  61.0 99.9 %copy-start.54 = (f32[512]{0:T(512)}, f32[512]{0:T(512)S(1)}, u32[]{:S(2)}) copy-start(f32[512]{0:T(512)S(1)} %get-tuple-element.180) | copy-start | bytes 6148
  61.2 99.7 %copy-start.76 = (f32[256]{0:T(256)}, f32[256]{0:T(256)S(1)}, u32[]{:S(2)}) copy-start(f32[256]{0:T(256)S(1)} %slice.2509) | copy-start | bytes 3076
  61.6 99.4 %copy-start.46 = (f32[512]{0:T(512)}, f32[512]{0:T(512)S(1)}, u32[]{:S(2)}) copy-start(f32[512]{0:T(512)S(1)} %get-tuple-element.220) | copy-start | bytes 6148
  61.8 99.2 %copy-start.48 = (f32[512]{0:T(512)}, f32[512]{0:T(512)S(1)}, u32[]{:S(2)}) copy-start(f32[512]{0:T(512)S(1)} %get-tuple-element.222) | copy-start | bytes 6148
  62.1 98.8 %copy-start.72 = (f32[256]{0:T(256)}, f32[256]{0:T(256)S(1)}, u32[]{:S(2)}) copy-start(f32[256]{0:T(256)S(1)} %slice.2499) | copy-start | bytes 3076
  205.4 8.1 %collective-permute-start.4 = (f32[3,3,2048]{2,1,0:T(4,128)S(1)}, f32[3,3,2048]{2,1,0:T(4,128)S(1)}, u32[]{:S(2)}, u32[]{:S(2)}) collective-permute-start(f32[3,3,2048]{2,1,0:T(4,128)S(1)} %get-tuple-element.247), channel_id=1, source_target_pairs={{0,1},{1,2},{2,3},{3,4},{4,5},{5,6},{6,7},{7,8},{8,9},{9,10},{10,1... | collective-permute-start | bytes 221192 | tf_op jit(solution)/shard_map/ppermute | solution.py:22
  207.3 8.0 %collective-permute-start.5 = (f32[3,3,2048]{2,1,0:T(4,128)S(1)}, f32[3,3,2048]{2,1,0:T(4,128)S(1)}, u32[]{:S(2)}, u32[]{:S(2)}) collective-permute-start(f32[3,3,2048]{2,1,0:T(4,128)S(1)} %get-tuple-element.248), channel_id=1, source_target_pairs={{1,0},{2,1},{3,2},{4,3},{5,4},{6,5},{7,6},{8,7},{9,8},{10,9},{11,1... | collective-permute-start | bytes 221192 | tf_op jit(solution)/shard_map/ppermute | solution.py:23
  245.4 8.1 %collective-permute-start.6 = (f32[3,3,2048]{2,1,0:T(4,128)S(1)}, f32[3,3,2048]{2,1,0:T(4,128)S(1)}, u32[]{:S(2)}, u32[]{:S(2)}) collective-permute-start(f32[3,3,2048]{2,1,0:T(4,128)S(1)} %get-tuple-element.242), channel_id=1, source_target_pairs={{0,1},{1,2},{2,3},{3,4},{4,5},{5,6},{6,7},{7,8},{8,9},{9,10},{10,1... | collective-permute-start | bytes 221192 | tf_op jit(solution)/shard_map/ppermute | solution.py:22
  247.3 8.0 %collective-permute-start.7 = (f32[3,3,2048]{2,1,0:T(4,128)S(1)}, f32[3,3,2048]{2,1,0:T(4,128)S(1)}, u32[]{:S(2)}, u32[]{:S(2)}) collective-permute-start(f32[3,3,2048]{2,1,0:T(4,128)S(1)} %get-tuple-element.243), channel_id=1, source_target_pairs={{1,0},{2,1},{3,2},{4,3},{5,4},{6,5},{7,6},{8,7},{9,8},{10,9},{11,1... | collective-permute-start | bytes 221192 | tf_op jit(solution)/shard_map/ppermute | solution.py:23
  326.0 6.0 %collective-permute-start.8 = (f32[3,8,1024]{2,1,0:T(8,128)S(1)}, f32[3,8,1024]{2,1,0:T(8,128)S(1)}, u32[]{:S(2)}, u32[]{:S(2)}) collective-permute-start(f32[3,8,1024]{2,1,0:T(8,128)S(1)} %fusion.19), channel_id=1, source_target_pairs={{0,32},{32,64},{64,96},{1,33},{33,65},{65,97},{2,34},{34,66},{66,9... | collective-permute-start | bytes 294920 | tf_op jit(solution)/shard_map/ppermute | solution.py:31
  332.1 6.9 %collective-permute-start.10 = (f32[3,3,1024]{2,1,0:T(4,128)S(1)}, f32[3,3,1024]{2,1,0:T(4,128)S(1)}, u32[]{:S(2)}, u32[]{:S(2)}) collective-permute-start(f32[3,3,1024]{2,1,0:T(4,128)S(1)} %get-tuple-element.317), channel_id=1, source_target_pairs={{1,0},{2,1},{3,2},{4,3},{5,4},{6,5},{7,6},{8,7},{9,8},{10,9},{11,1... | collective-permute-start | bytes 110600 | tf_op jit(solution)/shard_map/ppermute | solution.py:23
  337.1 7.5 %collective-permute-start.9 = (f32[3,3,1024]{2,1,0:T(4,128)S(1)}, f32[3,3,1024]{2,1,0:T(4,128)S(1)}, u32[]{:S(2)}, u32[]{:S(2)}) collective-permute-start(f32[3,3,1024]{2,1,0:T(4,128)S(1)} %get-tuple-element.316), channel_id=1, source_target_pairs={{0,1},{1,2},{2,3},{3,4},{4,5},{5,6},{6,7},{7,8},{8,9},{9,10},{10,1... | collective-permute-start | bytes 110600 | tf_op jit(solution)/shard_map/ppermute | solution.py:22
  358.5 6.2 %collective-permute-start.11 = (f32[3,8,1024]{2,1,0:T(8,128)S(1)}, f32[3,8,1024]{2,1,0:T(8,128)S(1)}, u32[]{:S(2)}, u32[]{:S(2)}) collective-permute-start(f32[3,8,1024]{2,1,0:T(8,128)S(1)} %fusion.18), channel_id=1, source_target_pairs={{0,32},{32,64},{64,96},{1,33},{33,65},{65,97},{2,34},{34,66},{66,9... | collective-permute-start | bytes 294920 | tf_op jit(solution)/shard_map/ppermute | solution.py:31
  364.7 7.9 %collective-permute-start.12 = (f32[3,3,1024]{2,1,0:T(4,128)S(1)}, f32[3,3,1024]{2,1,0:T(4,128)S(1)}, u32[]{:S(2)}, u32[]{:S(2)}) collective-permute-start(f32[3,3,1024]{2,1,0:T(4,128)S(1)} %get-tuple-element.314), channel_id=1, source_target_pairs={{0,1},{1,2},{2,3},{3,4},{4,5},{5,6},{6,7},{7,8},{8,9},{9,10},{10,1... | collective-permute-start | bytes 110600 | tf_op jit(solution)/shard_map/ppermute | solution.py:22
  366.7 7.5 %collective-permute-start.13 = (f32[3,3,1024]{2,1,0:T(4,128)S(1)}, f32[3,3,1024]{2,1,0:T(4,128)S(1)}, u32[]{:S(2)}, u32[]{:S(2)}) collective-permute-start(f32[3,3,1024]{2,1,0:T(4,128)S(1)} %get-tuple-element.315), channel_id=1, source_target_pairs={{1,0},{2,1},{3,2},{4,3},{5,4},{6,5},{7,6},{8,7},{9,8},{10,9},{11,1... | collective-permute-start | bytes 110600 | tf_op jit(solution)/shard_map/ppermute | solution.py:23
  387.6 6.5 %collective-permute-start.14 = (f32[3,8,1024]{2,1,0:T(8,128)S(1)}, f32[3,8,1024]{2,1,0:T(8,128)S(1)}, u32[]{:S(2)}, u32[]{:S(2)}) collective-permute-start(f32[3,8,1024]{2,1,0:T(8,128)S(1)} %fusion.17), channel_id=1, source_target_pairs={{0,32},{32,64},{64,96},{1,33},{33,65},{65,97},{2,34},{34,66},{66,9... | collective-permute-start | bytes 294920 | tf_op jit(solution)/shard_map/ppermute | solution.py:31
  394.1 7.7 %collective-permute-start.15 = (f32[3,3,1024]{2,1,0:T(4,128)S(1)}, f32[3,3,1024]{2,1,0:T(4,128)S(1)}, u32[]{:S(2)}, u32[]{:S(2)}) collective-permute-start(f32[3,3,1024]{2,1,0:T(4,128)S(1)} %get-tuple-element.312), channel_id=1, source_target_pairs={{0,1},{1,2},{2,3},{3,4},{4,5},{5,6},{6,7},{7,8},{8,9},{9,10},{10,1... | collective-permute-start | bytes 110600 | tf_op jit(solution)/shard_map/ppermute | solution.py:22
  396.1 7.5 %collective-permute-start.16 = (f32[3,3,1024]{2,1,0:T(4,128)S(1)}, f32[3,3,1024]{2,1,0:T(4,128)S(1)}, u32[]{:S(2)}, u32[]{:S(2)}) collective-permute-start(f32[3,3,1024]{2,1,0:T(4,128)S(1)} %get-tuple-element.313), channel_id=1, source_target_pairs={{1,0},{2,1},{3,2},{4,3},{5,4},{6,5},{7,6},{8,7},{9,8},{10,9},{11,1... | collective-permute-start | bytes 110600 | tf_op jit(solution)/shard_map/ppermute | solution.py:23
  (206 other events, 2035.0 us)
where the time goes:
time: 433 us; the launch traced here: 425 us
  local copies, waits for them, and re-layouts  188 us (43%)
  other arithmetic  138 us (32%)
  starting transfers between devices  66.2 us (15%)
  waiting for transfers between devices  19.3 us (4%)
  between operations  13.9 us (3%)
    ppermute x7, starting transfers between devices, extended(): after = lax.ppermute(first, axis, down)  40.6 us
    another operation x132, other arithmetic, reduce_lines(): jnp.stack([solved_even, solved_odd], axis=-1).reshape(leading + (length,))  39 us
    another operation x1, local copies, waits for them, and re-layouts, restrict(): blocks = fields.reshape(planes, row_count // 2, 2, columns // 2, 2)  28.5 us
    reshape x1, local copies, waits for them, and re-layouts, restrict(): blocks = fields.reshape(planes, row_count // 2, 2, columns // 2, 2)  27.6 us
    reduce_sum x2, other arithmetic, restrict(): return 0.25 * jnp.sum(blocks, axis=(2, 4))  20.4 us
    unnamed x447, local copies, waits for them, and re-layouts  19.2 us
    another operation x66, local copies, waits for them, and re-layouts, reduce_lines(): jnp.stack([solved_even, solved_odd], axis=-1).reshape(leading + (length,))  16.3 us
    ppermute x7, starting transfers between devices, extended(): before = lax.ppermute(last, axis, up)  13.4 us
  transfers between devices with their start and end apart: 17, of which 9 were waited for; matrix products, arithmetic and copies ran while one was open for 35% of the time, Pallas kernels for 0%

commit v1 on v0

v1 whole, which is shorter than its diff:
```python
import jax
import jax.numpy as jnp
import ml_dtypes
import numpy as np
from jax import lax
from jax.experimental import pallas as pl
from jax.experimental.pallas import tpu as pltpu
from jax.sharding import PartitionSpec as P

STEPS = 3
FINE_SPACING = 0.05
COARSE_SPACING = 0.1
FINE_STEP = 0.015
COARSE_STEP = 0.045

NX = 2048
ROWS = 16
UNKNOWNS = 512
BLOCKS = 4
LANES = 128
HALO_ROWS = 32
COARSE_HALO = 9
VMEM_LIMIT = 48 * 1024 * 1024


def halves(values):
    high = values.astype(np.float32).astype(ml_dtypes.bfloat16)
    low = (values - high.astype(np.float64)).astype(np.float32).astype(ml_dtypes.bfloat16)
    return high, low


def shifted(values):
    return np.concatenate([[0.0], values[:-1]])


def eliminated(lower, middle, upper):
    lower_e, lower_o = lower[0::2], lower[1::2]
    middle_e, middle_o = middle[0::2], middle[1::2]
    upper_e, upper_o = upper[0::2], upper[1::2]
    middle_n = np.append(middle_e[1:], 1.0)
    lower_n = np.append(lower_e[1:], 0.0)
    upper_n = np.append(upper_e[1:], 0.0)
    alpha = -lower_o / middle_e
    gamma = -upper_o / middle_n
    reduced = (alpha * lower_e, middle_o + alpha * upper_e + gamma * lower_n, gamma * upper_n)
    return alpha, gamma, reduced


def operator_tables(phases, columns, spacing, time_step):
    stride = NX // columns
    centers = (np.arange(columns) + 0.5) * stride
    depth = 0.9 + 0.3 * np.sin(6.0 * np.pi * centers / NX)
    beta = depth * depth / 3.0
    coupling = beta / (spacing * spacing)
    lower = -coupling.copy()
    lower[0] = 0.0
    upper = -coupling.copy()
    upper[-1] = 0.0
    middle = 1.0 + 2.0 * coupling
    slope = time_step * depth / (2.0 * spacing)
    weight = beta / (spacing * spacing + 4.0 * beta)
    rows = {}
    for p in range(phases):
        rows["slope", p] = slope[p::phases]
        rows["weight", p] = weight[p::phases]
    alpha, gamma, first = eliminated(lower, middle, upper)
    if phases == 4:
        alpha2, gamma2, last = eliminated(*first)
        a1, a3, g1, g3 = alpha[0::2], alpha[1::2], gamma[0::2], gamma[1::2]
        rows["s0"] = alpha2 * a1
        rows["s1"] = alpha2
        rows["s2"] = a3 + alpha2 * g1
        rows["n1"] = shifted(gamma2)
        rows["n0"] = shifted(gamma2) * a1 + shifted(g3)
        rows["n2"] = shifted(gamma2) * g1
        l1, m1, u1 = (v[0::2] for v in first)
        rows["b1"] = 1.0 / m1
        rows["b0"] = a1 / m1
        rows["b2"] = g1 / m1
        rows["bp"] = -l1 / m1
        rows["b3"] = -u1 / m1
        rows["c0"] = 1.0 / middle[0::4]
        rows["cp"] = -lower[0::4] / middle[0::4]
        rows["c1"] = -upper[0::4] / middle[0::4]
        rows["d2"] = 1.0 / middle[2::4]
        rows["d1"] = -lower[2::4] / middle[2::4]
        rows["d3"] = -upper[2::4] / middle[2::4]
    else:
        last = first
        rows["s0"] = alpha
        rows["n0"] = shifted(gamma)
        rows["c0"] = 1.0 / middle[0::2]
        rows["cp"] = -lower[0::2] / middle[0::2]
        rows["c1"] = -upper[0::2] / middle[0::2]
    low, mid, up = last
    matrix = np.diag(mid) + np.diag(low[1:], -1) + np.diag(up[:-1], 1)
    inverse = np.linalg.inv(matrix)
    names = {name: i for i, name in enumerate(rows)}
    table = np.stack(list(rows.values())).reshape(-1, LANES).astype(np.float32)
    return names, table, np.stack(halves(inverse.T))


FINE_NAMES, FINE_TABLE, FINE_INVERSE = operator_tables(4, NX, FINE_SPACING, FINE_STEP)
COARSE_NAMES, COARSE_TABLE, COARSE_INVERSE = operator_tables(2, NX // 2, COARSE_SPACING, COARSE_STEP)


def phase_matrix():
    matrix = np.zeros((512, 512), np.float32)
    j = np.arange(512)
    matrix[j, (j % 4) * LANES + j // 4] = 1.0
    return matrix


PHASES = phase_matrix().astype(ml_dtypes.bfloat16)
NATURAL = phase_matrix().T.copy().astype(ml_dtypes.bfloat16)


def spread_matrix():
    matrix = np.zeros((256, 512), np.float32)
    c = np.arange(512)
    coarse = c // 2
    matrix[(coarse % 2) * LANES + coarse // 2, c] = 1.0
    return matrix


SPREAD = spread_matrix().astype(ml_dtypes.bfloat16)


def split(values):
    high = values.astype(jnp.bfloat16)
    low = (values - high.astype(jnp.float32)).astype(jnp.bfloat16)
    return high, low


def dot(a, b):
    return jnp.dot(a, b, preferred_element_type=jnp.float32)


def placed(values, matrix):
    count = values.shape[0]
    high, low = split(values)
    both = dot(jnp.concatenate([high, low], axis=0), matrix)
    return both[:count] + both[count:]


def lane_index(rows):
    return lax.broadcasted_iota(jnp.int32, (rows, LANES), 1)


def following(tiles):
    lane = lane_index(tiles[0].shape[0])
    rolled = [pltpu.roll(t, LANES - 1, 1) for t in tiles] + [jnp.zeros_like(tiles[0])]
    return [jnp.where(lane == LANES - 1, rolled[a + 1], rolled[a]) for a in range(BLOCKS)]


def preceding(tiles):
    lane = lane_index(tiles[0].shape[0])
    rolled = [jnp.zeros_like(tiles[0])] + [pltpu.roll(t, 1, 1) for t in tiles]
    return [jnp.where(lane == 0, rolled[a], rolled[a + 1]) for a in range(BLOCKS)]


def inside(first, count, total):
    row = lax.broadcasted_iota(jnp.int32, (count, LANES), 0) + first
    return jnp.where((row >= 0) & (row < total), 1.0, 0.0).astype(jnp.float32)


def wave_step(phases, names, table, inverse, ratio, height, height_new, flux, diff, windows, origin, total):
    (h0, hn), (d0, dn), (o0, on) = windows
    last = phases - 1

    def coef(name, a):
        i = names[name] * BLOCKS + a
        return table[i : i + 1, :]

    mask = inside(origin + h0, hn, total)
    rows = pl.ds(h0, hn)
    before = preceding([flux[0, last, a, rows, :] for a in range(BLOCKS)])
    after = following([flux[0, 0, a, rows, :] for a in range(BLOCKS)])
    for p in range(phases):
        for a in range(BLOCKS):
            right = after[a] if p == last else flux[0, p + 1, a, rows, :]
            left = before[a] if p == 0 else flux[0, p - 1, a, rows, :]
            down = flux[1, p, a, pl.ds(h0 + 1, hn), :]
            upper = flux[1, p, a, pl.ds(h0 - 1, hn), :]
            change = (right - left) + (down - upper)
            height_new[p, a, rows, :] = (height[p, a, rows, :] - ratio * change) * mask

    rows = pl.ds(d0, dn)
    mask = inside(origin + d0, dn, total)
    before = preceding([height_new[last, a, rows, :] for a in range(BLOCKS)])
    after = following([height_new[0, a, rows, :] for a in range(BLOCKS)])
    reduced = []
    for i in range(2):
        own, passed = [], []
        for a in range(BLOCKS):
            force = []
            for p in range(phases):
                if i == 0:
                    right = after[a] if p == last else height_new[p + 1, a, rows, :]
                    left = before[a] if p == 0 else height_new[p - 1, a, rows, :]
                    value = flux[0, p, a, rows, :] - coef(("slope", p), a) * (right - left)
                else:
                    down = height_new[p, a, pl.ds(d0 + 1, dn), :]
                    upper = height_new[p, a, pl.ds(d0 - 1, dn), :]
                    value = (flux[1, p, a, rows, :] - coef(("slope", p), a) * (down - upper)) * mask
                if p < last:
                    diff[i, p, a, rows, :] = value
                force.append(value)
            kept = force[last] + coef("s0", a) * force[0]
            sent = coef("n0", a) * force[0]
            if phases == 4:
                kept = kept + coef("s1", a) * force[1] + coef("s2", a) * force[2]
                sent = sent + coef("n1", a) * force[1] + coef("n2", a) * force[2]
            own.append(kept)
            passed.append(sent)
        arrived = following(passed)
        reduced.append(jnp.concatenate([own[a] + arrived[a] for a in range(BLOCKS)], axis=1))
    high, low = split(jnp.concatenate(reduced, axis=0))
    both = dot(jnp.concatenate([high, low], axis=0), inverse[0])
    solved = both[: 2 * dn] + both[2 * dn :] + dot(high, inverse[1])

    for i in range(2):
        ends = [solved[i * dn : (i + 1) * dn, a * LANES : (a + 1) * LANES] for a in range(BLOCKS)]
        before = preceding(ends)
        for a in range(BLOCKS):
            end, prior = ends[a], before[a]
            f0 = diff[i, 0, a, rows, :]
            if phases == 4:
                f1 = diff[i, 1, a, rows, :]
                f2 = diff[i, 2, a, rows, :]
                x1 = (
                    coef("b1", a) * f1
                    + coef("b0", a) * f0
                    + coef("b2", a) * f2
                    + coef("bp", a) * prior
                    + coef("b3", a) * end
                )
                x0 = coef("c0", a) * f0 + coef("cp", a) * prior + coef("c1", a) * x1
                x2 = coef("d2", a) * f2 + coef("d1", a) * x1 + coef("d3", a) * end
                trial = [x0, x1, x2, end]
            else:
                trial = [coef("c0", a) * f0 + coef("cp", a) * prior + coef("c1", a) * end, end]
            for p in range(phases):
                diff[i, p, a, rows, :] = trial[p] - flux[i, p, a, rows, :]

    mask = inside(origin + o0, on, total)
    rows = pl.ds(o0, on)
    for i in range(2):
        for p in range(phases):
            for a in range(BLOCKS):
                middle = diff[i, p, a, rows, :]
                down = diff[i, p, a, pl.ds(o0 + 1, on), :]
                upper = diff[i, p, a, pl.ds(o0 - 1, on), :]
                bend = coef(("weight", p), a) * (down + upper - 2.0 * middle)
                flux[i, p, a, rows, :] = (flux[i, p, a, rows, :] + middle + bend) * mask


FINE_RATIO = FINE_STEP / (2.0 * FINE_SPACING)
COARSE_RATIO = COARSE_STEP / (2.0 * COARSE_SPACING)


def pack_kernel(x, to_next, to_previous):
    for s in range(16):
        cols = slice(s * LANES, (s + 1) * LANES)
        base = s * HALO_ROWS
        for c, (start, count) in enumerate(((0, 10), (10, 11), (21, 11))):
            to_next[base + start : base + start + count, :] = x[c, ROWS - count : ROWS, cols]
            to_previous[base + start : base + start + count, :] = x[c, 0:count, cols]


def own_kernel(x, matrix, out):
    parts = []
    for a in range(BLOCKS):
        for c in range(3):
            parts.append(x[c, :, a * 512 : (a + 1) * 512])
    phased = placed(jnp.concatenate(parts, axis=0), matrix[...])
    for a in range(BLOCKS):
        for c in range(3):
            base = (a * 3 + c) * ROWS
            for p in range(4):
                out[c, p, a] = phased[base : base + ROWS, p * LANES : (p + 1) * LANES]


def fine_kernel(
    own, above, below, matrix, fine_inverse, coarse_inverse, fine_table, coarse_table,
    fine_end, u_own, u_next, u_previous, propagated,
    height, height_new, flux, diff, c_height, c_height_new, c_flux, c_diff,
):
    tile = lax.axis_index("tile")
    cut = lax.axis_index("cuts")
    tiles = lax.axis_size("tile")
    parts = []
    for a in range(BLOCKS):
        for halo in (above, below):
            parts.append(
                jnp.concatenate(
                    [halo[(4 * a + s) * HALO_ROWS : (4 * a + s + 1) * HALO_ROWS, :] for s in range(4)],
                    axis=1,
                )
            )
    phased = placed(jnp.concatenate(parts, axis=0), matrix[...])

    def field(c, p, a):
        return height.at[p, a] if c == 0 else flux.at[c - 1, p, a]

    for a in range(BLOCKS):
        for p in range(4):
            lanes = slice(p * LANES, (p + 1) * LANES)
            top = a * 2 * HALO_ROWS
            low = top + HALO_ROWS
            for c, (start, count) in enumerate(((0, 10), (10, 11), (21, 11))):
                to = field(c, p, a)
                to[16 - count : 16, :] = phased[top + start : top + start + count, lanes]
                to[16:32, :] = own[c, p, a]
                to[32 : 32 + count, :] = phased[low + start : low + start + count, lanes]

    def restricted(ref, p, a):
        total = None
        for q in (2 * p, 2 * p + 1):
            for r in (8, 9):
                part = ref(q, a)[pl.ds(r, 16, stride=2), :]
                total = part if total is None else total + part
        return 0.25 * total

    for p in range(2):
        for a in range(BLOCKS):
            c_height[p, a, 8:24, :] = restricted(lambda q, b: height.at[q, b], p, a)
            for i in range(2):
                c_flux[i, p, a, 8:24, :] = restricted(lambda q, b: flux.at[i, q, b], p, a)

    wave_step(
        2, COARSE_NAMES, coarse_table, coarse_inverse, COARSE_RATIO, c_height, c_height_new, c_flux, c_diff,
        ((8, 16), (8, 16), (8, 16)), tile * (ROWS // 2) - 12, tiles * (ROWS // 2),
    )

    origin = tile * ROWS - 16
    total = tiles * ROWS
    arguments = (4, FINE_NAMES, fine_table, fine_inverse, FINE_RATIO)
    wave_step(*arguments, height, height_new, flux, diff, ((4, 40), (4, 40), (8, 32)), origin, total)
    wave_step(*arguments, height_new, height, flux, diff, ((8, 32), (8, 32), (8, 32)), origin, total)
    wave_step(*arguments, height, height_new, flux, diff, ((12, 24), (12, 24), (12, 24)), origin, total)

    for p in range(4):
        for a in range(BLOCKS):
            fine_end[0, p, a] = height_new[p, a, 16:32, :]
            for i in range(2):
                fine_end[i + 1, p, a] = flux[i, p, a, 16:32, :]

    later = jnp.where(cut > 0, 1.0, 0.0).astype(jnp.float32)
    for c in range(3):
        for p in range(2):
            for a in range(BLOCKS):
                if c == 0:
                    end = restricted(lambda q, b: height_new.at[q, b], p, a)
                    step = c_height_new[p, a, 8:24, :]
                else:
                    end = restricted(lambda q, b: flux.at[c - 1, q, b], p, a)
                    step = c_flux[c - 1, p, a, 8:24, :]
                step = later * step
                propagated[c, p, a] = step[4:12]
                u = end - step
                c_diff[0, p, a, 8:24, :] = u
                u_own[c, p, a] = u[4:12]
                base = ((c * 2 + p) * BLOCKS + a) * COARSE_HALO
                u_next[base : base + COARSE_HALO, :] = c_diff[0, p, a, 11:20, :]
                u_previous[base : base + COARSE_HALO, :] = c_diff[0, p, a, 12:21, :]


def natural_kernel(fine_end, matrix, out):
    parts = []
    for a in range(BLOCKS):
        for c in range(3):
            parts.append(jnp.concatenate([fine_end[c, p, a] for p in range(4)], axis=1))
    natural = placed(jnp.concatenate(parts, axis=0), matrix[...])
    for a in range(BLOCKS):
        for c in range(3):
            base = (a * 3 + c) * ROWS
            out[c, :, a * 512 : (a + 1) * 512] = natural[base : base + ROWS]


def coarse_kernel(own, above, below, inverse, table, one, two, three, height, height_new, flux, diff):
    tile = lax.axis_index("tile")
    tiles = lax.axis_size("tile")
    for c in range(3):
        for p in range(2):
            for a in range(BLOCKS):
                to = height.at[p, a] if c == 0 else flux.at[c - 1, p, a]
                base = ((c * 2 + p) * BLOCKS + a) * COARSE_HALO
                to[7:16, :] = above[base : base + COARSE_HALO, :]
                to[16:24, :] = own[c, p, a]
                to[24:33, :] = below[base : base + COARSE_HALO, :]
    origin = tile * (ROWS // 2) - 16
    total = tiles * (ROWS // 2)
    arguments = (2, COARSE_NAMES, table, inverse, COARSE_RATIO)

    def keep(out, source):
        for p in range(2):
            for a in range(BLOCKS):
                out[0, p, a] = source[p, a, 16:24, :]
                for i in range(2):
                    out[i + 1, p, a] = flux[i, p, a, 16:24, :]

    wave_step(*arguments, height, height_new, flux, diff, ((8, 24), (8, 24), (8, 24)), origin, total)
    keep(one, height_new)
    wave_step(*arguments, height_new, height, flux, diff, ((8, 24), (12, 16), (12, 16)), origin, total)
    keep(two, height)
    wave_step(*arguments, height, height_new, flux, diff, ((12, 16), (12, 16), (16, 8)), origin, total)
    keep(three, height_new)


def final_kernel(fine_end, propagated, one, two, three, matrix, out, rows):
    parts = []
    for a in range(BLOCKS):
        for c in range(3):
            pair = []
            for p in range(2):
                pair.append(one[c, p, a] + two[c, p, a] + three[c, p, a] - propagated[c, p, a])
            parts.append(jnp.concatenate(pair, axis=1))
    spread = placed(jnp.concatenate(parts, axis=0), matrix[...])
    for a in range(BLOCKS):
        for c in range(3):
            base = (a * 3 + c) * 8
            for s in range(4):
                value = spread[base : base + 8, s * LANES : (s + 1) * LANES]
                rows[c, a * 4 + s, pl.ds(0, 8, stride=2), :] = value
                rows[c, a * 4 + s, pl.ds(1, 8, stride=2), :] = value
    for c in range(3):
        for s in range(16):
            cols = slice(s * LANES, (s + 1) * LANES)
            out[c, :, cols] = fine_end[c, :, cols] + rows[c, s]


def f32(*shape):
    return jax.ShapeDtypeStruct(shape, jnp.float32)


def scratch(*shape):
    return pltpu.VMEM(shape, jnp.float32)


def call(kernel, outs, scratches=(), name=None):
    return pl.pallas_call(
        kernel,
        out_shape=outs,
        scratch_shapes=scratches,
        name=name,
        compiler_params=pltpu.CompilerParams(vmem_limit_bytes=VMEM_LIMIT),
    )


def per_device(start_states):
    x = start_states[0]
    tiles = lax.axis_size("tile")
    slices = lax.axis_size("cuts")
    forward = [(i, i + 1) for i in range(tiles - 1)]
    backward = [(i + 1, i) for i in range(tiles - 1)]

    halo = f32(16 * HALO_ROWS, LANES)
    to_next, to_previous = call(pack_kernel, [halo, halo], name="pack")(x)
    above = lax.ppermute(to_next, "tile", forward)
    below = lax.ppermute(to_previous, "tile", backward)
    own = call(own_kernel, f32(3, 4, BLOCKS, ROWS, LANES), name="phases")(x, PHASES)

    coarse = f32(3, 2, BLOCKS, 8, LANES)
    coarse_halo = f32(3 * 2 * BLOCKS * COARSE_HALO, LANES)
    fine_end, u_own, u_next, u_previous, propagated = call(
        fine_kernel,
        [f32(3, 4, BLOCKS, ROWS, LANES), coarse, coarse_halo, coarse_halo, coarse],
        [
            scratch(4, BLOCKS, 48, LANES),
            scratch(4, BLOCKS, 48, LANES),
            scratch(2, 4, BLOCKS, 48, LANES),
            scratch(2, 4, BLOCKS, 48, LANES),
            scratch(2, BLOCKS, 32, LANES),
            scratch(2, BLOCKS, 32, LANES),
            scratch(2, 2, BLOCKS, 32, LANES),
            scratch(2, 2, BLOCKS, 32, LANES),
        ],
        name="fine",
    )(own, above, below, PHASES, FINE_INVERSE, COARSE_INVERSE, FINE_TABLE, COARSE_TABLE)

    u_above = lax.ppermute(u_next, "tile", forward)
    u_below = lax.ppermute(u_previous, "tile", backward)
    natural = call(natural_kernel, f32(3, ROWS, NX), name="natural")(fine_end, NATURAL)

    powers = call(
        coarse_kernel,
        [coarse, coarse, coarse],
        [
            scratch(2, BLOCKS, 48, LANES),
            scratch(2, BLOCKS, 48, LANES),
            scratch(2, 2, BLOCKS, 48, LANES),
            scratch(2, 2, BLOCKS, 48, LANES),
        ],
        name="coarse",
    )(u_own, u_above, u_below, COARSE_INVERSE, COARSE_TABLE)
    arrived = [
        lax.ppermute(power, "cuts", [(i, i + m) for i in range(slices - m)])
        for m, power in enumerate(powers, 1)
    ]
    out = call(final_kernel, f32(3, ROWS, NX), [scratch(3, 16, ROWS, LANES)], name="final")(
        natural, propagated, *arrived, SPREAD
    )
    return out[None]


def solution(mesh):
    spec = P("cuts", None, "tile", None)
    return jax.shard_map(per_device, mesh=mesh, in_specs=(spec,), out_specs=spec, check_vma=False)
```

time: 433 us -> 44 us (0.10)
  the two profiles are of different devices: /device:TPU:16 before, /device:TPU:15 now
where the time goes in v1:
time: 44 us; the launch traced here: 43.7 us
  starting transfers between devices  20 us (45%)
  waiting for transfers between devices  13.4 us (30%)
  Pallas kernels  6.76 us (15%)
  local copies, waits for them, and re-layouts  3.37 us (8%)
    ppermute x3, starting transfers between devices, per_device(): lax.ppermute(power, 'cuts', [(i, i + m) for i in range(slices - m)])  10.1 us
    ppermute x1, waiting for transfers between devices, per_device(): below = lax.ppermute(to_previous, 'tile', backward)  6.44 us
    ppermute x1, waiting for transfers between devices, per_device(): u_below = lax.ppermute(u_previous, 'tile', backward)  5.75 us
    ppermute x1, starting transfers between devices, per_device(): above = lax.ppermute(to_next, 'tile', forward)  3.68 us
    unnamed x18, local copies, waits for them, and re-layouts  3.37 us
    pallas_call x1, Pallas kernels, per_device(): call(fine_kernel, [f32(3, 4, BLOCKS, ROWS, LANES), coarse, coarse_halo, c...  3.2 us
    ppermute x1, starting transfers between devices, per_device(): u_below = lax.ppermute(u_previous, 'tile', backward)  2.41 us
    ppermute x1, starting transfers between devices, per_device(): below = lax.ppermute(to_previous, 'tile', backward)  1.92 us
  transfers between devices with their start and end apart: 7, of which 3 were waited for; matrix products, arithmetic and copies ran while one was open for 0% of the time, Pallas kernels for 2%

profile of v1, /device:TPU:15, one launch (start us, length us, event | category | flops | bytes accessed | tf_op | source)
XLA Modules:
  0.0 43.7 jit_solution(7947480719776145172)
XLA Ops:
  0.0 1.1 %copy-done.3 = f32[1,3,16,2048]{3,2,1,0:T(8,128)S(1)} copy-done((f32[1,3,16,2048]{3,2,1,0:T(8,128)S(1)}, f32[1,3,16,2048]{3,2,1,0:T(8,128)}, u32[]{:S(2)}) %copy-start.3) | copy-done | bytes 393240
  1.1 0.1 pack.1
  1.1 3.7 %collective-permute-start = (f32[512,128]{1,0:T(8,128)S(1)}, f32[512,128]{1,0:T(8,128)S(1)}, u32[]{:S(2)}, u32[]{:S(2)}) collective-permute-start(f32[512,128]{1,0:T(8,128)S(1)} %get-tuple-element.15), channel_id=1, source_target_pairs={{0,1},{1,2},{2,3},{3,4},{4,5},{5,6},{6,7},{7,8},{8,9},{9,10},{10,1... | collective-permute-start | bytes 786440 | tf_op jit(solution)/shard_map/ppermute | solution.py:460
  4.8 1.9 %collective-permute-start.1 = (f32[512,128]{1,0:T(8,128)S(1)}, f32[512,128]{1,0:T(8,128)S(1)}, u32[]{:S(2)}, u32[]{:S(2)}) collective-permute-start(f32[512,128]{1,0:T(8,128)S(1)} %get-tuple-element.16), channel_id=1, source_target_pairs={{1,0},{2,1},{3,2},{4,3},{5,4},{6,5},{7,6},{8,7},{9,8},{10,9},{11,1... | collective-permute-start | bytes 786440 | tf_op jit(solution)/shard_map/ppermute | solution.py:461
  6.8 0.0 copy-start.1
  6.8 1.0 %copy-done.1 = bf16[512,512]{1,0:T(8,128)(2,1)S(1)} copy-done((bf16[512,512]{1,0:T(8,128)(2,1)S(1)}, bf16[512,512]{1,0:T(8,128)(2,1)}, u32[]{:S(2)}) %copy-start.1) | copy-done | bytes 524312
  7.8 0.4 phases.1.own
  8.2 0.0 collective-permute-done.above
  8.2 6.4 %collective-permute-done.1.below = f32[512,128]{1,0:T(8,128)S(1)} collective-permute-done((f32[512,128]{1,0:T(8,128)S(1)}, f32[512,128]{1,0:T(8,128)S(1)}, u32[]{:S(2)}, u32[]{:S(2)}) %collective-permute-start.1) | collective-permute-done | bytes 262176 | tf_op jit(solution)/shard_map/ppermute | solution.py:461
  14.6 0.0 copy-done
  14.6 0.0 copy-done.2
  14.6 0.0 copy-done.7
  14.6 0.0 copy-done.8
  14.7 0.0 copy-start.4
  14.7 1.2 %copy-done.4 = bf16[2,512,512]{2,1,0:T(8,128)(2,1)S(1)} copy-done((bf16[2,512,512]{2,1,0:T(8,128)(2,1)S(1)}, bf16[2,512,512]{2,1,0:T(8,128)(2,1)}, u32[]{:S(2)}) %copy-start.4) | copy-done | bytes 1048600
  15.9 3.2 %fine.1 = (f32[3,4,4,16,128]{4,3,2,1,0:T(8,128)S(1)}, f32[3,2,4,8,128]{4,3,2,1,0:T(8,128)S(1)}, f32[216,128]{1,0:T(8,128)S(1)}, f32[216,128]{1,0:T(8,128)S(1)}, f32[3,2,4,8,128]{4,3,2,1,0:T(8,128)S(1)}) custom-call(f32[3,4,4,16,128]{4,3,2,1,0:T(8,128)S(1)} %phases.1.own, f32[512,128]{1,0:T(8,128)S(1)} %collective-permute-done.above, ...), custom_call_target="tpu_custom_call" | custom-call | tf_op jit(solution)/shard_map/fine/pallas_call | solution.py:466
  19.1 1.9 %collective-permute-start.2 = (f32[216,128]{1,0:T(8,128)S(1)}, f32[216,128]{1,0:T(8,128)S(1)}, u32[]{:S(2)}, u32[]{:S(2)}) collective-permute-start(f32[216,128]{1,0:T(8,128)S(1)} %get-tuple-element.20), channel_id=1, source_target_pairs={{0,1},{1,2},{2,3},{3,4},{4,5},{5,6},{6,7},{7,8},{8,9},{9,10},{10,1... | collective-permute-start | bytes 331784 | tf_op jit(solution)/shard_map/ppermute | solution.py:482
  21.0 2.4 %collective-permute-start.3 = (f32[216,128]{1,0:T(8,128)S(1)}, f32[216,128]{1,0:T(8,128)S(1)}, u32[]{:S(2)}, u32[]{:S(2)}) collective-permute-start(f32[216,128]{1,0:T(8,128)S(1)} %get-tuple-element.21), channel_id=1, source_target_pairs={{1,0},{2,1},{3,2},{4,3},{5,4},{6,5},{7,6},{8,7},{9,8},{10,9},{11,1... | collective-permute-start | bytes 331784 | tf_op jit(solution)/shard_map/ppermute | solution.py:483
  23.4 0.0 collective-permute-done.2.above
  23.4 5.8 %collective-permute-done.3.below = f32[216,128]{1,0:T(8,128)S(1)} collective-permute-done((f32[216,128]{1,0:T(8,128)S(1)}, f32[216,128]{1,0:T(8,128)S(1)}, u32[]{:S(2)}, u32[]{:S(2)}) %collective-permute-start.3) | collective-permute-done | bytes 110624 | tf_op jit(solution)/shard_map/ppermute | solution.py:483
  29.2 1.8 %coarse.1 = (f32[3,2,4,8,128]{4,3,2,1,0:T(8,128)S(1)}, f32[3,2,4,8,128]{4,3,2,1,0:T(8,128)S(1)}, f32[3,2,4,8,128]{4,3,2,1,0:T(8,128)S(1)}) custom-call(f32[3,2,4,8,128]{4,3,2,1,0:T(8,128)S(1)} %get-tuple-element.19.own, f32[216,128]{1,0:T(8,128)S(1)} %collective-permute-done.2.above, f32[216,128]{1,0:T(8,128)S(1)} %collective-permute-done.3.below, ...), custom_call_target="tpu_custom_call" | custom-call | tf_op jit(solution)/shard_map/coarse/pallas_call | solution.py:486
  31.0 3.5 %collective-permute-start.4 = (f32[3,2,4,8,128]{4,3,2,1,0:T(8,128)S(1)}, f32[3,2,4,8,128]{4,3,2,1,0:T(8,128)S(1)}, u32[]{:S(2)}, u32[]{:S(2)}) collective-permute-start(f32[3,2,4,8,128]{4,3,2,1,0:T(8,128)S(1)} %get-tuple-element.22), channel_id=1, source_target_pairs={{0,32},{32,64},{64,96},{1,33},{33,65},{65,97},{2,34},{34,66},{66,9... | collective-permute-start | bytes 294920 | tf_op jit(solution)/shard_map/ppermute | solution.py:498
  34.5 5.2 %collective-permute-start.5 = (f32[3,2,4,8,128]{4,3,2,1,0:T(8,128)S(1)}, f32[3,2,4,8,128]{4,3,2,1,0:T(8,128)S(1)}, u32[]{:S(2)}, u32[]{:S(2)}) collective-permute-start(f32[3,2,4,8,128]{4,3,2,1,0:T(8,128)S(1)} %get-tuple-element.23), channel_id=1, source_target_pairs={{0,64},{32,96},{1,65},{33,97},{2,66},{34,98},{3,67},{35,99},{4,68}... | collective-permute-start | bytes 294920 | tf_op jit(solution)/shard_map/ppermute | solution.py:498
  39.8 1.3 %collective-permute-start.6 = (f32[3,2,4,8,128]{4,3,2,1,0:T(8,128)S(1)}, f32[3,2,4,8,128]{4,3,2,1,0:T(8,128)S(1)}, u32[]{:S(2)}, u32[]{:S(2)}) collective-permute-start(f32[3,2,4,8,128]{4,3,2,1,0:T(8,128)S(1)} %get-tuple-element.24), channel_id=1, source_target_pairs={{0,96},{1,97},{2,98},{3,99},{4,100},{5,101},{6,102},{7,103},{8,104... | collective-permute-start | bytes 294920 | tf_op jit(solution)/shard_map/ppermute | solution.py:498
  41.1 0.0 copy-done.5
  41.1 0.0 copy-start.6
  41.1 0.4 natural.1.fine_end
  41.5 0.0 collective-permute-done.4.one
  41.5 0.0 collective-permute-done.5.two
  41.5 1.2 %collective-permute-done.6.three = f32[3,2,4,8,128]{4,3,2,1,0:T(8,128)S(1)} collective-permute-done((f32[3,2,4,8,128]{4,3,2,1,0:T(8,128)S(1)}, f32[3,2,4,8,128]{4,3,2,1,0:T(8,128)S(1)}, u32[]{:S(2)}, u32[]{:S(2)}) %collective-permute-start.6) | collective-permute-done | bytes 98336 | tf_op jit(solution)/shard_map/ppermute | solution.py:498
  42.7 0.0 copy-done.6
  42.7 1.0 %final.1 = f32[3,16,2048]{2,1,0:T(8,128)} custom-call(f32[3,16,2048]{2,1,0:T(8,128)S(1)} %natural.1.fine_end, f32[3,2,4,8,128]{4,3,2,1,0:T(8,128)S(1)} %get-tuple-element.18.propagated, f32[3,2,4,8,128]{4,3,2,1,0:T(8,128)S(1)} %collective-permute-done.4.one, f32[3,2,4,8,128]{4,3,2,1,0:T(8,128)S(1)} %collective-permute-done.5.two, ...), custom_call_target="tpu_custom_call" | custom-call | tf_op jit(solution)/shard_map/final/pallas_call | solution.py:501
  (6 shorter events, 0.0 us)
Async XLA Ops:
  0.0 14.6 %copy-start = (bf16[2,512,512]{2,1,0:T(8,128)(2,1)S(1)}, bf16[2,512,512]{2,1,0:T(8,128)(2,1)}, u32[]{:S(2)}) copy-start(bf16[2,512,512]{2,1,0:T(8,128)(2,1)} %constant.16.clone.coarse_inverse.inverse) | copy-start | bytes 3145732
  0.0 1.1 %copy-start.3 = (f32[1,3,16,2048]{3,2,1,0:T(8,128)S(1)}, f32[1,3,16,2048]{3,2,1,0:T(8,128)}, u32[]{:S(2)}) copy-start(f32[1,3,16,2048]{3,2,1,0:T(8,128)} %param.8) | copy-start | bytes 1179652
  1.1 7.0 %collective-permute-start = (f32[512,128]{1,0:T(8,128)S(1)}, f32[512,128]{1,0:T(8,128)S(1)}, u32[]{:S(2)}, u32[]{:S(2)}) collective-permute-start(f32[512,128]{1,0:T(8,128)S(1)} %get-tuple-element.15), channel_id=1, source_target_pairs={{0,1},{1,2},{2,3},{3,4},{4,5},{5,6},{6,7},{7,8},{8,9},{9,10},{10,1... | collective-permute-start | bytes 786440 | tf_op jit(solution)/shard_map/ppermute | solution.py:460
  4.8 9.8 %collective-permute-start.1 = (f32[512,128]{1,0:T(8,128)S(1)}, f32[512,128]{1,0:T(8,128)S(1)}, u32[]{:S(2)}, u32[]{:S(2)}) collective-permute-start(f32[512,128]{1,0:T(8,128)S(1)} %get-tuple-element.16), channel_id=1, source_target_pairs={{1,0},{2,1},{3,2},{4,3},{5,4},{6,5},{7,6},{8,7},{9,8},{10,9},{11,1... | collective-permute-start | bytes 786440 | tf_op jit(solution)/shard_map/ppermute | solution.py:461
  6.8 1.0 %copy-start.1 = (bf16[512,512]{1,0:T(8,128)(2,1)S(1)}, bf16[512,512]{1,0:T(8,128)(2,1)}, u32[]{:S(2)}) copy-start(bf16[512,512]{1,0:T(8,128)(2,1)} %constant.14.clone.matrix) | copy-start | bytes 1572868
  7.8 6.8 %copy-start.2 = (bf16[512,512]{1,0:T(8,128)(2,1)S(1)}, bf16[512,512]{1,0:T(8,128)(2,1)}, u32[]{:S(2)}) copy-start(bf16[512,512]{1,0:T(8,128)(2,1)} %constant.14.clone.matrix) | copy-start | bytes 1572868
  7.8 6.8 %copy-start.7 = (f32[36,128]{1,0:T(8,128)S(1)}, f32[36,128]{1,0:T(8,128)}, u32[]{:S(2)}) copy-start(f32[36,128]{1,0:T(8,128)} %constant.18.clone.coarse_table.table) | copy-start | bytes 55300
  7.8 6.8 %copy-start.8 = (f32[100,128]{1,0:T(8,128)S(1)}, f32[100,128]{1,0:T(8,128)}, u32[]{:S(2)}) copy-start(f32[100,128]{1,0:T(8,128)} %constant.17.clone.fine_table) | copy-start | bytes 153604
  14.7 1.2 %copy-start.4 = (bf16[2,512,512]{2,1,0:T(8,128)(2,1)S(1)}, bf16[2,512,512]{2,1,0:T(8,128)(2,1)}, u32[]{:S(2)}) copy-start(bf16[2,512,512]{2,1,0:T(8,128)(2,1)} %constant.15.clone.fine_inverse) | copy-start | bytes 3145732
  19.1 4.3 %collective-permute-start.2 = (f32[216,128]{1,0:T(8,128)S(1)}, f32[216,128]{1,0:T(8,128)S(1)}, u32[]{:S(2)}, u32[]{:S(2)}) collective-permute-start(f32[216,128]{1,0:T(8,128)S(1)} %get-tuple-element.20), channel_id=1, source_target_pairs={{0,1},{1,2},{2,3},{3,4},{4,5},{5,6},{6,7},{7,8},{8,9},{9,10},{10,1... | collective-permute-start | bytes 331784 | tf_op jit(solution)/shard_map/ppermute | solution.py:482
  21.0 8.2 %collective-permute-start.3 = (f32[216,128]{1,0:T(8,128)S(1)}, f32[216,128]{1,0:T(8,128)S(1)}, u32[]{:S(2)}, u32[]{:S(2)}) collective-permute-start(f32[216,128]{1,0:T(8,128)S(1)} %get-tuple-element.21), channel_id=1, source_target_pairs={{1,0},{2,1},{3,2},{4,3},{5,4},{6,5},{7,6},{8,7},{9,8},{10,9},{11,1... | collective-permute-start | bytes 331784 | tf_op jit(solution)/shard_map/ppermute | solution.py:483
  29.2 11.9 %copy-start.5 = (bf16[512,512]{1,0:T(8,128)(2,1)S(1)}, bf16[512,512]{1,0:T(8,128)(2,1)}, u32[]{:S(2)}) copy-start(bf16[512,512]{1,0:T(8,128)(2,1)} %constant.19.clone.matrix) | copy-start | bytes 1572868
  31.0 10.5 %collective-permute-start.4 = (f32[3,2,4,8,128]{4,3,2,1,0:T(8,128)S(1)}, f32[3,2,4,8,128]{4,3,2,1,0:T(8,128)S(1)}, u32[]{:S(2)}, u32[]{:S(2)}) collective-permute-start(f32[3,2,4,8,128]{4,3,2,1,0:T(8,128)S(1)} %get-tuple-element.22), channel_id=1, source_target_pairs={{0,32},{32,64},{64,96},{1,33},{33,65},{65,97},{2,34},{34,66},{66,9... | collective-permute-start | bytes 294920 | tf_op jit(solution)/shard_map/ppermute | solution.py:498
  34.5 6.9 %collective-permute-start.5 = (f32[3,2,4,8,128]{4,3,2,1,0:T(8,128)S(1)}, f32[3,2,4,8,128]{4,3,2,1,0:T(8,128)S(1)}, u32[]{:S(2)}, u32[]{:S(2)}) collective-permute-start(f32[3,2,4,8,128]{4,3,2,1,0:T(8,128)S(1)} %get-tuple-element.23), channel_id=1, source_target_pairs={{0,64},{32,96},{1,65},{33,97},{2,66},{34,98},{3,67},{35,99},{4,68}... | collective-permute-start | bytes 294920 | tf_op jit(solution)/shard_map/ppermute | solution.py:498
  39.8 2.9 %collective-permute-start.6 = (f32[3,2,4,8,128]{4,3,2,1,0:T(8,128)S(1)}, f32[3,2,4,8,128]{4,3,2,1,0:T(8,128)S(1)}, u32[]{:S(2)}, u32[]{:S(2)}) collective-permute-start(f32[3,2,4,8,128]{4,3,2,1,0:T(8,128)S(1)} %get-tuple-element.24), channel_id=1, source_target_pairs={{0,96},{1,97},{2,98},{3,99},{4,100},{5,101},{6,102},{7,103},{8,104... | collective-permute-start | bytes 294920 | tf_op jit(solution)/shard_map/ppermute | solution.py:498
  41.1 1.6 %copy-start.6 = (bf16[256,512]{1,0:T(8,128)(2,1)S(1)}, bf16[256,512]{1,0:T(8,128)(2,1)}, u32[]{:S(2)}) copy-start(bf16[256,512]{1,0:T(8,128)(2,1)} %constant.20.clone.matrix) | copy-start | bytes 786436

commit v2 on v1

--- a/solution.py
+++ b/solution.py
@@ -259,16 +259,33 @@
 COARSE_RATIO = COARSE_STEP / (2.0 * COARSE_SPACING)
 
 
-def pack_kernel(x, to_next, to_previous):
-    for s in range(16):
-        cols = slice(s * LANES, (s + 1) * LANES)
-        base = s * HALO_ROWS
-        for c, (start, count) in enumerate(((0, 10), (10, 11), (21, 11))):
-            to_next[base + start : base + start + count, :] = x[c, ROWS - count : ROWS, cols]
-            to_previous[base + start : base + start + count, :] = x[c, 0:count, cols]
-
-
-def own_kernel(x, matrix, out):
+def on_odd():
+    return lax.rem(lax.axis_index("tile"), 2) == 1
+
+
+def pack_kernel(source, x, to_far, to_near, sems):
+    copies = [pltpu.make_async_copy(source.at[c], x.at[c], sems.at[c]) for c in range(3)]
+    for copy in copies:
+        copy.start()
+    for copy in copies:
+        copy.wait()
+
+    def pack(to_next, to_previous):
+        for s in range(16):
+            cols = slice(s * LANES, (s + 1) * LANES)
+            base = s * HALO_ROWS
+            for c, (start, count) in enumerate(((0, 10), (10, 11), (21, 11))):
+                to_next[base + start : base + start + count, :] = x[c, ROWS - count : ROWS, cols]
+                to_previous[base + start : base + start + count, :] = x[c, 0:count, cols]
+
+    odd = on_odd()
+    pl.when(odd)(lambda: pack(to_far, to_near))
+    pl.when(jnp.logical_not(odd))(lambda: pack(to_near, to_far))
+
+
+def own_kernel(x, matrix, inverse, out, inverse_here, sem):
+    copy = pltpu.make_async_copy(inverse, inverse_here, sem)
+    copy.start()
     parts = []
     for a in range(BLOCKS):
         for c in range(3):
@@ -279,25 +296,29 @@
             base = (a * 3 + c) * ROWS
             for p in range(4):
                 out[c, p, a] = phased[base : base + ROWS, p * LANES : (p + 1) * LANES]
+    copy.wait()
 
 
 def fine_kernel(
-    own, above, below, matrix, fine_inverse, coarse_inverse, fine_table, coarse_table,
-    fine_end, u_own, u_next, u_previous, propagated,
+    own, far, near, matrix, fine_inverse, coarse_inverse, fine_table, coarse_table,
+    fine_end, u_own, u_far, u_near, propagated,
     height, height_new, flux, diff, c_height, c_height_new, c_flux, c_diff,
 ):
     tile = lax.axis_index("tile")
     cut = lax.axis_index("cuts")
     tiles = lax.axis_size("tile")
+    odd = on_odd()
     parts = []
     for a in range(BLOCKS):
-        for halo in (above, below):
-            parts.append(
+        ends = []
+        for halo in (far, near):
+            ends.append(
                 jnp.concatenate(
                     [halo[(4 * a + s) * HALO_ROWS : (4 * a + s + 1) * HALO_ROWS, :] for s in range(4)],
                     axis=1,
                 )
             )
+        parts += [jnp.where(odd, ends[1], ends[0]), jnp.where(odd, ends[0], ends[1])]
     phased = placed(jnp.concatenate(parts, axis=0), matrix[...])
 
     def field(c, p, a):
@@ -362,15 +383,25 @@
                 c_diff[0, p, a, 8:24, :] = u
                 u_own[c, p, a] = u[4:12]
                 base = ((c * 2 + p) * BLOCKS + a) * COARSE_HALO
-                u_next[base : base + COARSE_HALO, :] = c_diff[0, p, a, 11:20, :]
-                u_previous[base : base + COARSE_HALO, :] = c_diff[0, p, a, 12:21, :]
-
-
-def natural_kernel(fine_end, matrix, out):
+                to_next = c_diff[0, p, a, 11:20, :]
+                to_previous = c_diff[0, p, a, 12:21, :]
+                u_far[base : base + COARSE_HALO, :] = jnp.where(odd, to_next, to_previous)
+                u_near[base : base + COARSE_HALO, :] = jnp.where(odd, to_previous, to_next)
+
+
+def natural_kernel(fine_end, propagated, first, matrix, out, rows):
     parts = []
     for a in range(BLOCKS):
         for c in range(3):
-            parts.append(jnp.concatenate([fine_end[c, p, a] for p in range(4)], axis=1))
+            for p in range(2):
+                value = first[c, p, a] - propagated[c, p, a]
+                rows[c, p, a, pl.ds(0, 8, stride=2), :] = value
+                rows[c, p, a, pl.ds(1, 8, stride=2), :] = value
+    for a in range(BLOCKS):
+        for c in range(3):
+            parts.append(
+                jnp.concatenate([fine_end[c, p, a] + rows[c, p // 2, a] for p in range(4)], axis=1)
+            )
     natural = placed(jnp.concatenate(parts, axis=0), matrix[...])
     for a in range(BLOCKS):
         for c in range(3):
@@ -378,45 +409,61 @@
             out[c, :, a * 512 : (a + 1) * 512] = natural[base : base + ROWS]
 
 
-def coarse_kernel(own, above, below, inverse, table, one, two, three, height, height_new, flux, diff):
-    tile = lax.axis_index("tile")
-    tiles = lax.axis_size("tile")
-    for c in range(3):
-        for p in range(2):
-            for a in range(BLOCKS):
-                to = height.at[p, a] if c == 0 else flux.at[c - 1, p, a]
-                base = ((c * 2 + p) * BLOCKS + a) * COARSE_HALO
-                to[7:16, :] = above[base : base + COARSE_HALO, :]
-                to[16:24, :] = own[c, p, a]
-                to[24:33, :] = below[base : base + COARSE_HALO, :]
-    origin = tile * (ROWS // 2) - 16
-    total = tiles * (ROWS // 2)
+def coarse_origin(offset):
+    return lax.axis_index("tile") * (ROWS // 2) - offset, lax.axis_size("tile") * (ROWS // 2)
+
+
+def coarse_planes():
+    return [(c, p, a) for c in range(3) for p in range(2) for a in range(BLOCKS)]
+
+
+def first_kernel(own, far, near, inverse, table, one, wide, height, height_new, flux, diff):
+    odd = on_odd()
+    for c, p, a in coarse_planes():
+        to = height.at[p, a] if c == 0 else flux.at[c - 1, p, a]
+        base = ((c * 2 + p) * BLOCKS + a) * COARSE_HALO
+        distant = far[base : base + COARSE_HALO, :]
+        close = near[base : base + COARSE_HALO, :]
+        to[7:16, :] = jnp.where(odd, close, distant)
+        to[16:24, :] = own[c, p, a]
+        to[24:33, :] = jnp.where(odd, distant, close)
+    wave_step(
+        2, COARSE_NAMES, table, inverse, COARSE_RATIO, height, height_new, flux, diff,
+        ((8, 24), (8, 24), (8, 24)), *coarse_origin(16),
+    )
+    for c, p, a in coarse_planes():
+        result = height_new.at[p, a] if c == 0 else flux.at[c - 1, p, a]
+        one[c, p, a] = result[16:24, :]
+        wide[c, p, a] = result[8:32, :]
+
+
+def rest_kernel(wide, one, inverse, table, two, mixed, last, height, height_new, flux, diff):
+    for c, p, a in coarse_planes():
+        to = height.at[p, a] if c == 0 else flux.at[c - 1, p, a]
+        to[8:32, :] = wide[c, p, a]
     arguments = (2, COARSE_NAMES, table, inverse, COARSE_RATIO)
-
-    def keep(out, source):
-        for p in range(2):
-            for a in range(BLOCKS):
-                out[0, p, a] = source[p, a, 16:24, :]
-                for i in range(2):
-                    out[i + 1, p, a] = flux[i, p, a, 16:24, :]
-
-    wave_step(*arguments, height, height_new, flux, diff, ((8, 24), (8, 24), (8, 24)), origin, total)
-    keep(one, height_new)
-    wave_step(*arguments, height_new, height, flux, diff, ((8, 24), (12, 16), (12, 16)), origin, total)
-    keep(two, height)
-    wave_step(*arguments, height, height_new, flux, diff, ((12, 16), (12, 16), (16, 8)), origin, total)
-    keep(three, height_new)
-
-
-def final_kernel(fine_end, propagated, one, two, three, matrix, out, rows):
+    wave_step(*arguments, height, height_new, flux, diff, ((8, 24), (12, 16), (12, 16)), *coarse_origin(16))
+    for c, p, a in coarse_planes():
+        result = height_new.at[p, a] if c == 0 else flux.at[c - 1, p, a]
+        two[c, p, a] = result[16:24, :]
+    wave_step(*arguments, height_new, height, flux, diff, ((12, 16), (12, 16), (16, 8)), *coarse_origin(16))
+    start = lax.axis_index("cuts") == 0
+    for c, p, a in coarse_planes():
+        result = height.at[p, a] if c == 0 else flux.at[c - 1, p, a]
+        mixed[c, p, a] = jnp.where(start, result[16:24, :], one[c, p, a])
+        last[c, p, a] = one[c, p, a]
+
+
+def final_kernel(base_end, second, third, fourth, matrix, out, rows, staged, sems):
     parts = []
     for a in range(BLOCKS):
         for c in range(3):
             pair = []
             for p in range(2):
-                pair.append(one[c, p, a] + two[c, p, a] + three[c, p, a] - propagated[c, p, a])
+                pair.append(second[c, p, a] + (third[c, p, a] + fourth[c, p, a]))
             parts.append(jnp.concatenate(pair, axis=1))
     spread = placed(jnp.concatenate(parts, axis=0), matrix[...])
+    copies = []
     for a in range(BLOCKS):
         for c in range(3):
             base = (a * 3 + c) * 8
@@ -424,10 +471,15 @@
                 value = spread[base : base + 8, s * LANES : (s + 1) * LANES]
                 rows[c, a * 4 + s, pl.ds(0, 8, stride=2), :] = value
                 rows[c, a * 4 + s, pl.ds(1, 8, stride=2), :] = value
-    for c in range(3):
-        for s in range(16):
-            cols = slice(s * LANES, (s + 1) * LANES)
-            out[c, :, cols] = fine_end[c, :, cols] + rows[c, s]
+        for c in range(3):
+            for s in range(4 * a, 4 * a + 4):
+                cols = slice(s * LANES, (s + 1) * LANES)
+                staged[c, :, cols] = base_end[c, :, cols] + rows[c, s]
+        block = pl.ds(a * 512, 512)
+        copies.append(pltpu.make_async_copy(staged.at[:, :, block], out.at[:, :, block], sems.at[a]))
+        copies[-1].start()
+    for copy in copies:
+        copy.wait()
 
 
 def f32(*shape):
@@ -438,10 +490,20 @@
     return pltpu.VMEM(shape, jnp.float32)
 
 
-def call(kernel, outs, scratches=(), name=None):
+VMEM_SPEC = pl.BlockSpec(memory_space=pltpu.VMEM)
+HBM_SPEC = pl.BlockSpec(memory_space=pltpu.HBM)
+
+
+def in_hbm(array):
+    return pltpu.with_memory_space_constraint(array, pltpu.HBM)
+
+
+def call(kernel, ins, outs, scratches=(), name=None):
     return pl.pallas_call(
         kernel,
-        out_shape=outs,
+        in_specs=[HBM_SPEC if own else VMEM_SPEC for own in ins],
+        out_shape=[shape for shape, _ in outs],
+        out_specs=[HBM_SPEC if own else VMEM_SPEC for _, own in outs],
         scratch_shapes=scratches,
         name=name,
         compiler_params=pltpu.CompilerParams(vmem_limit_bytes=VMEM_LIMIT),
@@ -449,23 +511,29 @@
 
 
 def per_device(start_states):
-    x = start_states[0]
     tiles = lax.axis_size("tile")
-    slices = lax.axis_size("cuts")
-    forward = [(i, i + 1) for i in range(tiles - 1)]
-    backward = [(i + 1, i) for i in range(tiles - 1)]
-
-    halo = f32(16 * HALO_ROWS, LANES)
-    to_next, to_previous = call(pack_kernel, [halo, halo], name="pack")(x)
-    above = lax.ppermute(to_next, "tile", forward)
-    below = lax.ppermute(to_previous, "tile", backward)
-    own = call(own_kernel, f32(3, 4, BLOCKS, ROWS, LANES), name="phases")(x, PHASES)
-
-    coarse = f32(3, 2, BLOCKS, 8, LANES)
-    coarse_halo = f32(3 * 2 * BLOCKS * COARSE_HALO, LANES)
-    fine_end, u_own, u_next, u_previous, propagated = call(
+    far_pairs = [(i, j) for k in range(1, tiles - 1, 2) for i, j in ((k, k + 1), (k + 1, k))]
+    near_pairs = [(i, i ^ 1) for i in range(tiles)]
+    dma = pltpu.SemaphoreType.DMA
+
+    halo = (f32(16 * HALO_ROWS, LANES), False)
+    x, to_far, to_near = call(
+        pack_kernel, [True], [(f32(3, ROWS, NX), False), halo, halo], [dma((3,))], name="pack"
+    )(in_hbm(start_states[0]))
+    far = lax.ppermute(to_far, "tile", far_pairs)
+    near = lax.ppermute(to_near, "tile", near_pairs)
+    fine_shape = (f32(3, 4, BLOCKS, ROWS, LANES), False)
+    inverse_shape = (jax.ShapeDtypeStruct(FINE_INVERSE.shape, jnp.bfloat16), False)
+    own, fine_inverse = call(
+        own_kernel, [False, False, True], [fine_shape, inverse_shape], [dma(())], name="phases"
+    )(x, PHASES, in_hbm(FINE_INVERSE))
+
+    coarse = (f32(3, 2, BLOCKS, 8, LANES), False)
+    coarse_halo = (f32(3 * 2 * BLOCKS * COARSE_HALO, LANES), False)
+    fine_end, u_own, u_far, u_near, propagated = call(
         fine_kernel,
-        [f32(3, 4, BLOCKS, ROWS, LANES), coarse, coarse_halo, coarse_halo, coarse],
+        [False] * 8,
+        [fine_shape, coarse, coarse_halo, coarse_halo, coarse],
         [
             scratch(4, BLOCKS, 48, LANES),
             scratch(4, BLOCKS, 48, LANES),
@@ -477,30 +545,41 @@
             scratch(2, 2, BLOCKS, 32, LANES),
         ],
         name="fine",
-    )(own, above, below, PHASES, FINE_INVERSE, COARSE_INVERSE, FINE_TABLE, COARSE_TABLE)
-
-    u_above = lax.ppermute(u_next, "tile", forward)
-    u_below = lax.ppermute(u_previous, "tile", backward)
-    natural = call(natural_kernel, f32(3, ROWS, NX), name="natural")(fine_end, NATURAL)
-
-    powers = call(
-        coarse_kernel,
-        [coarse, coarse, coarse],
-        [
-            scratch(2, BLOCKS, 48, LANES),
-            scratch(2, BLOCKS, 48, LANES),
-            scratch(2, 2, BLOCKS, 48, LANES),
-            scratch(2, 2, BLOCKS, 48, LANES),
-        ],
-        name="coarse",
-    )(u_own, u_above, u_below, COARSE_INVERSE, COARSE_TABLE)
-    arrived = [
-        lax.ppermute(power, "cuts", [(i, i + m) for i in range(slices - m)])
-        for m, power in enumerate(powers, 1)
+    )(own, far, near, PHASES, fine_inverse, COARSE_INVERSE, FINE_TABLE, COARSE_TABLE)
+
+    u_far = lax.ppermute(u_far, "tile", far_pairs)
+    u_near = lax.ppermute(u_near, "tile", near_pairs)
+
+    state = [
+        scratch(2, BLOCKS, 48, LANES),
+        scratch(2, BLOCKS, 48, LANES),
+        scratch(2, 2, BLOCKS, 48, LANES),
+        scratch(2, 2, BLOCKS, 48, LANES),
     ]
-    out = call(final_kernel, f32(3, ROWS, NX), [scratch(3, 16, ROWS, LANES)], name="final")(
-        natural, propagated, *arrived, SPREAD
+    one, wide = call(
+        first_kernel, [False] * 5, [coarse, (f32(3, 2, BLOCKS, 24, LANES), False)], state, name="first"
+    )(u_own, u_far, u_near, COARSE_INVERSE, COARSE_TABLE)
+    first = lax.ppermute(one, "cuts", [(0, 1)])
+    two, mixed, last = call(rest_kernel, [False] * 4, [coarse] * 3, state, name="rest")(
+        wide, one, COARSE_INVERSE, COARSE_TABLE
     )
+    second = lax.ppermute(two, "cuts", [(0, 2), (1, 3)])
+    third = lax.ppermute(mixed, "cuts", [(0, 3), (1, 2)])
+    fourth = lax.ppermute(last, "cuts", [(2, 3)])
+    (natural,) = call(
+        natural_kernel,
+        [False] * 4,
+        [(f32(3, ROWS, NX), False)],
+        [scratch(3, 2, BLOCKS, ROWS, LANES)],
+        name="natural",
+    )(fine_end, propagated, first, NATURAL)
+    (out,) = call(
+        final_kernel,
+        [False] * 5,
+        [(f32(3, ROWS, NX), True)],
+        [scratch(3, 16, ROWS, LANES), scratch(3, ROWS, NX), dma((BLOCKS,))],
+        name="final",
+    )(natural, second, third, fourth, SPREAD)
     return out[None]
 
 

time: 44 us -> 35.8 us (0.81)
  the two profiles are of different devices: /device:TPU:15 before, /device:TPU:16 now
where the time goes in v2:
time: 35.8 us; the launch traced here: 35.4 us
  starting transfers between devices  16.9 us (47%)
  Pallas kernels  8.8 us (25%)
  waiting for transfers between devices  8.53 us (24%)
  local copies, waits for them, and re-layouts  1.07 us (3%)
    ppermute x1, starting transfers between devices, per_device(): far = lax.ppermute(to_far, 'tile', far_pairs)  4.12 us
    ppermute x1, waiting for transfers between devices, per_device(): u_far = lax.ppermute(u_far, 'tile', far_pairs)  4.08 us
    ppermute x1, starting transfers between devices, per_device(): u_far = lax.ppermute(u_far, 'tile', far_pairs)  4 us
    ppermute x1, starting transfers between devices, per_device(): first = lax.ppermute(one, 'cuts', [(0, 1)])  3.83 us
    ppermute x1, waiting for transfers between devices, per_device(): far = lax.ppermute(to_far, 'tile', far_pairs)  3.35 us
    pallas_call x1, Pallas kernels, per_device(): call(fine_kernel, [False] * 8, [fine_shape, coarse, coarse_halo, coarse_h...  3.21 us
    ppermute x1, starting transfers between devices, per_device(): second = lax.ppermute(two, 'cuts', [(0, 2), (1, 3)])  2.63 us
    ppermute x1, starting transfers between devices, per_device(): third = lax.ppermute(mixed, 'cuts', [(0, 3), (1, 2)])  1.45 us
  transfers between devices with their start and end apart: 8, of which 3 were waited for; matrix products, arithmetic and copies ran while one was open for 0% of the time, Pallas kernels for 8%

profile of v2, /device:TPU:16, one launch (start us, length us, event | category | flops | bytes accessed | tf_op | source)
XLA Modules:
  0.0 35.4 jit_solution(17372348445063579741)
XLA Ops:
  0.0 1.1 %pack.1 = (f32[3,16,2048]{2,1,0:T(8,128)S(1)}, f32[512,128]{1,0:T(8,128)S(1)}, f32[512,128]{1,0:T(8,128)S(1)}) custom-call(f32[3,16,2048]{2,1,0:T(8,128)} %bitcast.2), custom_call_target="tpu_custom_call" | custom-call | tf_op jit(solution)/shard_map/pack/pallas_call | solution.py:520
  1.1 0.0 copy-start
  1.1 4.1 %collective-permute-start = (f32[512,128]{1,0:T(8,128)S(1)}, f32[512,128]{1,0:T(8,128)S(1)}, u32[]{:S(2)}, u32[]{:S(2)}) collective-permute-start(f32[512,128]{1,0:T(8,128)S(1)} %get-tuple-element.22), channel_id=1, source_target_pairs={{1,2},{2,1},{3,4},{4,3},{5,6},{6,5},{7,8},{8,7},{9,10},{10,9},{11,... | collective-permute-start | bytes 786440 | tf_op jit(solution)/shard_map/ppermute | solution.py:523
  5.3 0.1 collective-permute-start.1
  5.4 0.0 copy-start.1
  5.4 1.0 %copy-done.1 = bf16[512,512]{1,0:T(8,128)(2,1)S(1)} copy-done((bf16[512,512]{1,0:T(8,128)(2,1)S(1)}, bf16[512,512]{1,0:T(8,128)(2,1)}, u32[]{:S(2)}) %copy-start.1) | copy-done | bytes 524312
  6.4 1.3 %phases.1 = (f32[3,4,4,16,128]{4,3,2,1,0:T(8,128)S(1)}, bf16[2,512,512]{2,1,0:T(8,128)(2,1)S(1)}) custom-call(f32[3,16,2048]{2,1,0:T(8,128)S(1)} %get-tuple-element.20.x, bf16[512,512]{1,0:T(8,128)(2,1)S(1)} %copy-done.1, bf16[2,512,512]{2,1,0:T(8,128)(2,1)} %constant.14.clone.inverse), custom_call_target="tpu_custom_call" | custom-call | tf_op jit(solution)/shard_map/phases/pallas_call | solution.py:527
  7.7 3.3 %collective-permute-done.far = f32[512,128]{1,0:T(8,128)S(1)} collective-permute-done((f32[512,128]{1,0:T(8,128)S(1)}, f32[512,128]{1,0:T(8,128)S(1)}, u32[]{:S(2)}, u32[]{:S(2)}) %collective-permute-start) | collective-permute-done | bytes 262176 | tf_op jit(solution)/shard_map/ppermute | solution.py:523
  11.1 0.0 collective-permute-done.1.near
  11.1 0.0 copy-done
  11.1 0.0 copy-done.2
  11.1 0.0 copy-done.5
  11.1 3.2 %fine.1 = (f32[3,4,4,16,128]{4,3,2,1,0:T(8,128)S(1)}, f32[3,2,4,8,128]{4,3,2,1,0:T(8,128)S(1)}, f32[216,128]{1,0:T(8,128)S(1)}, f32[216,128]{1,0:T(8,128)S(1)}, f32[3,2,4,8,128]{4,3,2,1,0:T(8,128)S(1)}) custom-call(f32[3,4,4,16,128]{4,3,2,1,0:T(8,128)S(1)} %get-tuple-element.21.own, f32[512,128]{1,0:T(8,128)S(1)} %collective-permute-done.far, ...), custom_call_target="tpu_custom_call" | custom-call | tf_op jit(solution)/shard_map/fine/pallas_call | solution.py:533
  14.3 4.0 %collective-permute-start.2 = (f32[216,128]{1,0:T(8,128)S(1)}, f32[216,128]{1,0:T(8,128)S(1)}, u32[]{:S(2)}, u32[]{:S(2)}) collective-permute-start(f32[216,128]{1,0:T(8,128)S(1)} %get-tuple-element.28), channel_id=1, source_target_pairs={{1,2},{2,1},{3,4},{4,3},{5,6},{6,5},{7,8},{8,7},{9,10},{10,9},{11,... | collective-permute-start | bytes 331784 | tf_op jit(solution)/shard_map/ppermute | solution.py:550
  18.3 0.1 collective-permute-start.3
  18.4 4.1 %collective-permute-done.2.far = f32[216,128]{1,0:T(8,128)S(1)} collective-permute-done((f32[216,128]{1,0:T(8,128)S(1)}, f32[216,128]{1,0:T(8,128)S(1)}, u32[]{:S(2)}, u32[]{:S(2)}) %collective-permute-start.2) | collective-permute-done | bytes 110624 | tf_op jit(solution)/shard_map/ppermute | solution.py:550
  22.5 0.0 collective-permute-done.3.near
  22.5 0.6 %first.1 = (f32[3,2,4,8,128]{4,3,2,1,0:T(8,128)S(1)}, f32[3,2,4,24,128]{4,3,2,1,0:T(8,128)S(1)}) custom-call(f32[3,2,4,8,128]{4,3,2,1,0:T(8,128)S(1)} %get-tuple-element.27.own, f32[216,128]{1,0:T(8,128)S(1)} %collective-permute-done.2.far, f32[216,128]{1,0:T(8,128)S(1)} %collective-permute-done.3.near, bf16[2,512,512]{2,1,0:T(8,128)(2,1)S(1)} %copy-done, ...), custom_call_target="tpu_custom_call" | custom-call | tf_op jit(solution)/shard_map/first/pallas_call | solution.py:559
  23.1 3.8 %collective-permute-start.4 = (f32[3,2,4,8,128]{4,3,2,1,0:T(8,128)S(1)}, f32[3,2,4,8,128]{4,3,2,1,0:T(8,128)S(1)}, u32[]{:S(2)}, u32[]{:S(2)}) collective-permute-start(f32[3,2,4,8,128]{4,3,2,1,0:T(8,128)S(1)} %get-tuple-element.30.one), channel_id=1, source_target_pairs={{0,32},{1,33},{2,34},{3,35},{4,36},{5,37},{6,38},{7,39},{8,40},{9,... | collective-permute-start | bytes 294920 | tf_op jit(solution)/shard_map/ppermute | solution.py:562
  27.0 0.0 copy-start.3
  27.0 1.2 %rest.1 = (f32[3,2,4,8,128]{4,3,2,1,0:T(8,128)S(1)}, f32[3,2,4,8,128]{4,3,2,1,0:T(8,128)S(1)}, f32[3,2,4,8,128]{4,3,2,1,0:T(8,128)S(1)}) custom-call(f32[3,2,4,24,128]{4,3,2,1,0:T(8,128)S(1)} %get-tuple-element.31.wide, f32[3,2,4,8,128]{4,3,2,1,0:T(8,128)S(1)} %get-tuple-element.30.one, bf16[2,512,512]{2,1,0:T(8,128)(2,1)S(1)} %copy-done, ...), custom_call_target="tpu_custom_call" | custom-call | tf_op jit(solution)/shard_map/rest/pallas_call | solution.py:563
  28.2 2.6 %collective-permute-start.5 = (f32[3,2,4,8,128]{4,3,2,1,0:T(8,128)S(1)}, f32[3,2,4,8,128]{4,3,2,1,0:T(8,128)S(1)}, u32[]{:S(2)}, u32[]{:S(2)}) collective-permute-start(f32[3,2,4,8,128]{4,3,2,1,0:T(8,128)S(1)} %get-tuple-element.32), channel_id=1, source_target_pairs={{0,64},{32,96},{1,65},{33,97},{2,66},{34,98},{3,67},{35,99},{4,68}... | collective-permute-start | bytes 294920 | tf_op jit(solution)/shard_map/ppermute | solution.py:566
  30.8 1.5 %collective-permute-start.6 = (f32[3,2,4,8,128]{4,3,2,1,0:T(8,128)S(1)}, f32[3,2,4,8,128]{4,3,2,1,0:T(8,128)S(1)}, u32[]{:S(2)}, u32[]{:S(2)}) collective-permute-start(f32[3,2,4,8,128]{4,3,2,1,0:T(8,128)S(1)} %get-tuple-element.33), channel_id=1, source_target_pairs={{0,96},{32,64},{1,97},{33,65},{2,98},{34,66},{3,99},{35,67},{4,100... | collective-permute-start | bytes 294920 | tf_op jit(solution)/shard_map/ppermute | solution.py:567
  32.3 0.7 %collective-permute-start.7 = (f32[3,2,4,8,128]{4,3,2,1,0:T(8,128)S(1)}, f32[3,2,4,8,128]{4,3,2,1,0:T(8,128)S(1)}, u32[]{:S(2)}, u32[]{:S(2)}) collective-permute-start(f32[3,2,4,8,128]{4,3,2,1,0:T(8,128)S(1)} %get-tuple-element.34), channel_id=1, source_target_pairs={{64,96},{65,97},{66,98},{67,99},{68,100},{69,101},{70,102},{71,103... | collective-permute-start | bytes 294920 | tf_op jit(solution)/shard_map/ppermute | solution.py:568
  32.9 0.0 collective-permute-done.4.first
  33.0 0.0 copy-done.3
  33.0 0.0 copy-start.4
  33.0 0.4 %natural.1.base_end = f32[3,16,2048]{2,1,0:T(8,128)S(1)} custom-call(f32[3,4,4,16,128]{4,3,2,1,0:T(8,128)S(1)} %get-tuple-element.25.fine_end, f32[3,2,4,8,128]{4,3,2,1,0:T(8,128)S(1)} %get-tuple-element.26.propagated, f32[3,2,4,8,128]{4,3,2,1,0:T(8,128)S(1)} %collective-permute-done.4.first, bf16[512,512]{1,0:T(8,128)(2,1)S(1)} %copy-done.3), custom_call_target="tpu_custom_call" | custom-call | tf_op jit(solution)/shard_map/natural/pallas_call | solution.py:569
  33.4 0.0 collective-permute-done.5.second
  33.4 1.1 %collective-permute-done.6.third = f32[3,2,4,8,128]{4,3,2,1,0:T(8,128)S(1)} collective-permute-done((f32[3,2,4,8,128]{4,3,2,1,0:T(8,128)S(1)}, f32[3,2,4,8,128]{4,3,2,1,0:T(8,128)S(1)}, u32[]{:S(2)}, u32[]{:S(2)}) %collective-permute-start.6) | collective-permute-done | bytes 98336 | tf_op jit(solution)/shard_map/ppermute | solution.py:567
  34.5 0.0 collective-permute-done.7.fourth
  34.5 1.0 %final.1 = f32[3,16,2048]{2,1,0:T(8,128)} custom-call(f32[3,16,2048]{2,1,0:T(8,128)S(1)} %natural.1.base_end, f32[3,2,4,8,128]{4,3,2,1,0:T(8,128)S(1)} %collective-permute-done.5.second, f32[3,2,4,8,128]{4,3,2,1,0:T(8,128)S(1)} %collective-permute-done.6.third, f32[3,2,4,8,128]{4,3,2,1,0:T(8,128)S(1)} %collective-permute-done.7.fourth, ...), custom_call_target="tpu_custom_call" | custom-call | tf_op jit(solution)/shard_map/final/pallas_call | solution.py:576
  (5 shorter events, 0.0 us)
Async XLA Ops:
  1.1 10.0 %copy-start = (bf16[2,512,512]{2,1,0:T(8,128)(2,1)S(1)}, bf16[2,512,512]{2,1,0:T(8,128)(2,1)}, u32[]{:S(2)}) copy-start(bf16[2,512,512]{2,1,0:T(8,128)(2,1)} %constant.16.clone.coarse_inverse.inverse) | copy-start | bytes 3145732
  1.1 9.9 %collective-permute-start = (f32[512,128]{1,0:T(8,128)S(1)}, f32[512,128]{1,0:T(8,128)S(1)}, u32[]{:S(2)}, u32[]{:S(2)}) collective-permute-start(f32[512,128]{1,0:T(8,128)S(1)} %get-tuple-element.22), channel_id=1, source_target_pairs={{1,2},{2,1},{3,4},{4,3},{5,6},{6,5},{7,8},{8,7},{9,10},{10,9},{11,... | collective-permute-start | bytes 786440 | tf_op jit(solution)/shard_map/ppermute | solution.py:523
  5.3 5.8 %collective-permute-start.1 = (f32[512,128]{1,0:T(8,128)S(1)}, f32[512,128]{1,0:T(8,128)S(1)}, u32[]{:S(2)}, u32[]{:S(2)}) collective-permute-start(f32[512,128]{1,0:T(8,128)S(1)} %get-tuple-element.23), channel_id=1, source_target_pairs={{0,1},{1,0},{2,3},{3,2},{4,5},{5,4},{6,7},{7,6},{8,9},{9,8},{10,11... | collective-permute-start | bytes 786440 | tf_op jit(solution)/shard_map/ppermute | solution.py:524
  5.4 1.0 %copy-start.1 = (bf16[512,512]{1,0:T(8,128)(2,1)S(1)}, bf16[512,512]{1,0:T(8,128)(2,1)}, u32[]{:S(2)}) copy-start(bf16[512,512]{1,0:T(8,128)(2,1)} %constant.15.clone.matrix) | copy-start | bytes 1572868
  6.4 4.7 %copy-start.2 = (bf16[512,512]{1,0:T(8,128)(2,1)S(1)}, bf16[512,512]{1,0:T(8,128)(2,1)}, u32[]{:S(2)}) copy-start(bf16[512,512]{1,0:T(8,128)(2,1)} %constant.15.clone.matrix) | copy-start | bytes 1572868
  6.4 4.7 %copy-start.5 = (f32[36,128]{1,0:T(8,128)S(1)}, f32[36,128]{1,0:T(8,128)}, u32[]{:S(2)}) copy-start(f32[36,128]{1,0:T(8,128)} %constant.18.clone.coarse_table.table) | copy-start | bytes 55300
  6.4 4.7 %copy-start.6 = (f32[100,128]{1,0:T(8,128)S(1)}, f32[100,128]{1,0:T(8,128)}, u32[]{:S(2)}) copy-start(f32[100,128]{1,0:T(8,128)} %constant.17.clone.fine_table) | copy-start | bytes 153604
  14.3 8.2 %collective-permute-start.2 = (f32[216,128]{1,0:T(8,128)S(1)}, f32[216,128]{1,0:T(8,128)S(1)}, u32[]{:S(2)}, u32[]{:S(2)}) collective-permute-start(f32[216,128]{1,0:T(8,128)S(1)} %get-tuple-element.28), channel_id=1, source_target_pairs={{1,2},{2,1},{3,4},{4,3},{5,6},{6,5},{7,8},{8,7},{9,10},{10,9},{11,... | collective-permute-start | bytes 331784 | tf_op jit(solution)/shard_map/ppermute | solution.py:550
  18.3 4.2 %collective-permute-start.3 = (f32[216,128]{1,0:T(8,128)S(1)}, f32[216,128]{1,0:T(8,128)S(1)}, u32[]{:S(2)}, u32[]{:S(2)}) collective-permute-start(f32[216,128]{1,0:T(8,128)S(1)} %get-tuple-element.29), channel_id=1, source_target_pairs={{0,1},{1,0},{2,3},{3,2},{4,5},{5,4},{6,7},{7,6},{8,9},{9,8},{10,11... | collective-permute-start | bytes 331784 | tf_op jit(solution)/shard_map/ppermute | solution.py:551
  23.1 9.8 %collective-permute-start.4 = (f32[3,2,4,8,128]{4,3,2,1,0:T(8,128)S(1)}, f32[3,2,4,8,128]{4,3,2,1,0:T(8,128)S(1)}, u32[]{:S(2)}, u32[]{:S(2)}) collective-permute-start(f32[3,2,4,8,128]{4,3,2,1,0:T(8,128)S(1)} %get-tuple-element.30.one), channel_id=1, source_target_pairs={{0,32},{1,33},{2,34},{3,35},{4,36},{5,37},{6,38},{7,39},{8,40},{9,... | collective-permute-start | bytes 294920 | tf_op jit(solution)/shard_map/ppermute | solution.py:562
  27.0 6.0 %copy-start.3 = (bf16[512,512]{1,0:T(8,128)(2,1)S(1)}, bf16[512,512]{1,0:T(8,128)(2,1)}, u32[]{:S(2)}) copy-start(bf16[512,512]{1,0:T(8,128)(2,1)} %constant.19.clone.matrix) | copy-start | bytes 1572868
  28.2 5.2 %collective-permute-start.5 = (f32[3,2,4,8,128]{4,3,2,1,0:T(8,128)S(1)}, f32[3,2,4,8,128]{4,3,2,1,0:T(8,128)S(1)}, u32[]{:S(2)}, u32[]{:S(2)}) collective-permute-start(f32[3,2,4,8,128]{4,3,2,1,0:T(8,128)S(1)} %get-tuple-element.32), channel_id=1, source_target_pairs={{0,64},{32,96},{1,65},{33,97},{2,66},{34,98},{3,67},{35,99},{4,68}... | collective-permute-start | bytes 294920 | tf_op jit(solution)/shard_map/ppermute | solution.py:566
  30.8 3.7 %collective-permute-start.6 = (f32[3,2,4,8,128]{4,3,2,1,0:T(8,128)S(1)}, f32[3,2,4,8,128]{4,3,2,1,0:T(8,128)S(1)}, u32[]{:S(2)}, u32[]{:S(2)}) collective-permute-start(f32[3,2,4,8,128]{4,3,2,1,0:T(8,128)S(1)} %get-tuple-element.33), channel_id=1, source_target_pairs={{0,96},{32,64},{1,97},{33,65},{2,98},{34,66},{3,99},{35,67},{4,100... | collective-permute-start | bytes 294920 | tf_op jit(solution)/shard_map/ppermute | solution.py:567
  32.3 2.2 %collective-permute-start.7 = (f32[3,2,4,8,128]{4,3,2,1,0:T(8,128)S(1)}, f32[3,2,4,8,128]{4,3,2,1,0:T(8,128)S(1)}, u32[]{:S(2)}, u32[]{:S(2)}) collective-permute-start(f32[3,2,4,8,128]{4,3,2,1,0:T(8,128)S(1)} %get-tuple-element.34), channel_id=1, source_target_pairs={{64,96},{65,97},{66,98},{67,99},{68,100},{69,101},{70,102},{71,103... | collective-permute-start | bytes 294920 | tf_op jit(solution)/shard_map/ppermute | solution.py:568
  33.0 1.5 %copy-start.4 = (bf16[256,512]{1,0:T(8,128)(2,1)S(1)}, bf16[256,512]{1,0:T(8,128)(2,1)}, u32[]{:S(2)}) copy-start(bf16[256,512]{1,0:T(8,128)(2,1)} %constant.20.clone.matrix) | copy-start | bytes 786436

commit v3 on v2

v3 whole, which is shorter than its diff:
```python
import jax
import jax.numpy as jnp
import ml_dtypes
import numpy as np
from jax import lax
from jax.experimental import pallas as pl
from jax.experimental.pallas import tpu as pltpu
from jax.sharding import PartitionSpec as P

STEPS = 3
FINE_SPACING = 0.05
COARSE_SPACING = 0.1
FINE_STEP = 0.015
COARSE_STEP = 0.045

NX = 2048
ROWS = 16
UNKNOWNS = 512
BLOCKS = 4
LANES = 128
VMEM_LIMIT = 48 * 1024 * 1024


def halves(values):
    high = values.astype(np.float32).astype(ml_dtypes.bfloat16)
    low = (values - high.astype(np.float64)).astype(np.float32).astype(ml_dtypes.bfloat16)
    return high, low


def shifted(values):
    return np.concatenate([[0.0], values[:-1]])


def eliminated(lower, middle, upper):
    lower_e, lower_o = lower[0::2], lower[1::2]
    middle_e, middle_o = middle[0::2], middle[1::2]
    upper_e, upper_o = upper[0::2], upper[1::2]
    middle_n = np.append(middle_e[1:], 1.0)
    lower_n = np.append(lower_e[1:], 0.0)
    upper_n = np.append(upper_e[1:], 0.0)
    alpha = -lower_o / middle_e
    gamma = -upper_o / middle_n
    reduced = (alpha * lower_e, middle_o + alpha * upper_e + gamma * lower_n, gamma * upper_n)
    return alpha, gamma, reduced


def operator_tables(phases, columns, spacing, time_step):
    stride = NX // columns
    centers = (np.arange(columns) + 0.5) * stride
    depth = 0.9 + 0.3 * np.sin(6.0 * np.pi * centers / NX)
    beta = depth * depth / 3.0
    coupling = beta / (spacing * spacing)
    lower = -coupling.copy()
    lower[0] = 0.0
    upper = -coupling.copy()
    upper[-1] = 0.0
    middle = 1.0 + 2.0 * coupling
    slope = time_step * depth / (2.0 * spacing)
    weight = beta / (spacing * spacing + 4.0 * beta)
    rows = {}
    for p in range(phases):
        rows["slope", p] = slope[p::phases]
        rows["weight", p] = weight[p::phases]
        rows["centre", p] = 1.0 - 2.0 * weight[p::phases]
    alpha, gamma, first = eliminated(lower, middle, upper)
    if phases == 4:
        alpha2, gamma2, last = eliminated(*first)
        a1, a3, g1, g3 = alpha[0::2], alpha[1::2], gamma[0::2], gamma[1::2]
        rows["s0"] = alpha2 * a1
        rows["s1"] = alpha2
        rows["s2"] = a3 + alpha2 * g1
        rows["n1"] = shifted(gamma2)
        rows["n0"] = shifted(gamma2) * a1 + shifted(g3)
        rows["n2"] = shifted(gamma2) * g1
        l1, m1, u1 = (v[0::2] for v in first)
        rows["b1"] = 1.0 / m1
        rows["b0"] = a1 / m1
        rows["b2"] = g1 / m1
        rows["bp"] = -l1 / m1
        rows["b3"] = -u1 / m1
        rows["c0"] = 1.0 / middle[0::4]
        rows["cp"] = -lower[0::4] / middle[0::4]
        rows["c1"] = -upper[0::4] / middle[0::4]
        rows["d2"] = 1.0 / middle[2::4]
        rows["d1"] = -lower[2::4] / middle[2::4]
        rows["d3"] = -upper[2::4] / middle[2::4]
    else:
        last = first
        rows["s0"] = alpha
        rows["n0"] = shifted(gamma)
        rows["c0"] = 1.0 / middle[0::2]
        rows["cp"] = -lower[0::2] / middle[0::2]
        rows["c1"] = -upper[0::2] / middle[0::2]
    low, mid, up = last
    matrix = np.diag(mid) + np.diag(low[1:], -1) + np.diag(up[:-1], 1)
    inverse = np.linalg.inv(matrix)
    names = {name: i for i, name in enumerate(rows)}
    table = np.stack(list(rows.values())).reshape(-1, LANES).astype(np.float32)
    return names, table, np.stack(halves(inverse.T))


FINE_NAMES, FINE_TABLE, FINE_INVERSE = operator_tables(4, NX, FINE_SPACING, FINE_STEP)
COARSE_NAMES, COARSE_TABLE, COARSE_INVERSE = operator_tables(2, NX // 2, COARSE_SPACING, COARSE_STEP)


def phase_matrix():
    matrix = np.zeros((512, 512), np.float32)
    j = np.arange(512)
    matrix[j, (j % 4) * LANES + j // 4] = 1.0
    return matrix


PHASES = phase_matrix().astype(ml_dtypes.bfloat16)
NATURAL = phase_matrix().T.copy().astype(ml_dtypes.bfloat16)


def spread_matrix():
    matrix = np.zeros((256, 512), np.float32)
    c = np.arange(512)
    coarse = c // 2
    matrix[(coarse % 2) * LANES + coarse // 2, c] = 1.0
    return matrix


SPREAD = spread_matrix().astype(ml_dtypes.bfloat16)


def split(values):
    high = values.astype(jnp.bfloat16)
    low = (values - high.astype(jnp.float32)).astype(jnp.bfloat16)
    return high, low


def dot(a, b):
    return jnp.dot(a, b, preferred_element_type=jnp.float32)


def placed(values, matrix):
    count = values.shape[0]
    high, low = split(values)
    both = dot(jnp.concatenate([high, low], axis=0), matrix)
    return both[:count] + both[count:]


def lane_index(rows):
    return lax.broadcasted_iota(jnp.int32, (rows, LANES), 1)


def following(tiles):
    lane = lane_index(tiles[0].shape[0])
    rolled = [pltpu.roll(t, LANES - 1, 1) for t in tiles] + [jnp.zeros_like(tiles[0])]
    return [jnp.where(lane == LANES - 1, rolled[a + 1], rolled[a]) for a in range(BLOCKS)]


def preceding(tiles):
    lane = lane_index(tiles[0].shape[0])
    rolled = [jnp.zeros_like(tiles[0])] + [pltpu.roll(t, 1, 1) for t in tiles]
    return [jnp.where(lane == 0, rolled[a], rolled[a + 1]) for a in range(BLOCKS)]


def inside(first, count, total):
    row = lax.broadcasted_iota(jnp.int32, (count, LANES), 0) + first
    return jnp.where((row >= 0) & (row < total), 1.0, 0.0).astype(jnp.float32)


def step_stages(phases, names, table, inverse, ratio, height, height_new, flux, diff, windows, origin, total):
    (h0, hn), (d0, dn), ends = windows
    last = phases - 1

    def coef(name, a):
        i = names[name] * BLOCKS + a
        return table[i : i + 1, :]

    mask = inside(origin + h0, hn, total)
    rows = pl.ds(h0, hn)
    before = preceding([flux[0, last, a, rows, :] for a in range(BLOCKS)])
    after = following([flux[0, 0, a, rows, :] for a in range(BLOCKS)])
    for p in range(phases):
        for a in range(BLOCKS):
            right = after[a] if p == last else flux[0, p + 1, a, rows, :]
            left = before[a] if p == 0 else flux[0, p - 1, a, rows, :]
            down = flux[1, p, a, pl.ds(h0 + 1, hn), :]
            upper = flux[1, p, a, pl.ds(h0 - 1, hn), :]
            change = (right - left) + (down - upper)
            height_new[p, a, rows, :] = (height[p, a, rows, :] - ratio * change) * mask
    yield

    rows = pl.ds(d0, dn)
    mask = inside(origin + d0, dn, total)

    def reduce(i):
        if i == 0:
            before = preceding([height_new[last, a, rows, :] for a in range(BLOCKS)])
            after = following([height_new[0, a, rows, :] for a in range(BLOCKS)])
        own, passed = [], []
        for a in range(BLOCKS):
            force = []
            for p in range(phases):
                if i == 0:
                    right = after[a] if p == last else height_new[p + 1, a, rows, :]
                    left = before[a] if p == 0 else height_new[p - 1, a, rows, :]
                    value = flux[0, p, a, rows, :] - coef(("slope", p), a) * (right - left)
                else:
                    down = height_new[p, a, pl.ds(d0 + 1, dn), :]
                    upper = height_new[p, a, pl.ds(d0 - 1, dn), :]
                    value = (flux[1, p, a, rows, :] - coef(("slope", p), a) * (down - upper)) * mask
                if p < last:
                    diff[i, p, a, rows, :] = value
                force.append(value)
            kept = force[last] + coef("s0", a) * force[0]
            sent = coef("n0", a) * force[0]
            if phases == 4:
                kept = kept + coef("s1", a) * force[1] + coef("s2", a) * force[2]
                sent = sent + coef("n1", a) * force[1] + coef("n2", a) * force[2]
            own.append(kept)
            passed.append(sent)
        arrived = following(passed)
        return jnp.concatenate([own[a] + arrived[a] for a in range(BLOCKS)], axis=1)

    def expand(i, solved):
        ends = [solved[:, a * LANES : (a + 1) * LANES] for a in range(BLOCKS)]
        before = preceding(ends)
        for a in range(BLOCKS):
            end, prior = ends[a], before[a]
            f0 = diff[i, 0, a, rows, :]
            if phases == 4:
                f1 = diff[i, 1, a, rows, :]
                f2 = diff[i, 2, a, rows, :]
                x1 = (
                    coef("b1", a) * f1
                    + coef("b0", a) * f0
                    + coef("b2", a) * f2
                    + coef("bp", a) * prior
                    + coef("b3", a) * end
                )
                x0 = coef("c0", a) * f0 + coef("cp", a) * prior + coef("c1", a) * x1
                x2 = coef("d2", a) * f2 + coef("d1", a) * x1 + coef("d3", a) * end
                trial = [x0, x1, x2, end]
            else:
                trial = [coef("c0", a) * f0 + coef("cp", a) * prior + coef("c1", a) * end, end]
            for p in range(phases):
                diff[i, p, a, rows, :] = trial[p] - flux[i, p, a, rows, :]

    pair = [reduce(0), reduce(1)]
    yield
    solved = solve(jnp.concatenate(pair, axis=0), inverse)
    yield
    expand(0, solved[:dn])
    expand(1, solved[dn:])
    yield

    for i in range(2):
        o0, on = ends[i]
        mask = inside(origin + o0, on, total)
        rows = pl.ds(o0, on)
        for p in range(phases):
            for a in range(BLOCKS):
                middle = diff[i, p, a, rows, :]
                down = diff[i, p, a, pl.ds(o0 + 1, on), :]
                upper = diff[i, p, a, pl.ds(o0 - 1, on), :]
                sides = coef(("weight", p), a) * (down + upper)
                flux[i, p, a, rows, :] = (flux[i, p, a, rows, :] + coef(("centre", p), a) * middle + sides) * mask
    yield


def solve(right, inverse):
    count = right.shape[0]
    high, low = split(right)
    both = dot(jnp.concatenate([high, low], axis=0), inverse[0])
    return both[:count] + both[count:] + dot(high, inverse[1])


def wave_step(*arguments):
    for _ in step_stages(*arguments):
        pass


def wave_steps_in_turn(*steps):
    for _ in zip(*[step_stages(*arguments) for arguments in steps]):
        pass


FINE_RATIO = FINE_STEP / (2.0 * FINE_SPACING)
COARSE_RATIO = COARSE_STEP / (2.0 * COARSE_SPACING)


def on_odd():
    return lax.rem(lax.axis_index("tile"), 2) == 1


def planes(phases):
    return [(c, p, a) for c in range(3) for p in range(phases) for a in range(BLOCKS)]


SPILL = ((0, 8), (8, 8), (16, 9))
SPILL_ROWS = 25
NEAR_START = 24 * 14
SPARE = 8


def fetch(pairs, sems):
    copies = [pltpu.make_async_copy(source, target, sems.at[i]) for i, (source, target) in enumerate(pairs)]
    for copy in copies:
        copy.start()
    return copies


def at_tile(tile_rows, offset):
    return lax.axis_index("tile") * tile_rows - offset, lax.axis_size("tile") * tile_rows


def fine_kernel(
    x_hbm, matrix_hbm, fine_inverse_hbm, fine_table_hbm, coarse_inverse_hbm, coarse_table_hbm,
    own, spill_far, u_wide, u_far, u_near, u_cross, coarse_inverse,
    x, matrix, fine_inverse, fine_table, coarse_table, sems,
    height, height_new, flux, diff, c_height, c_height_new, c_flux, c_diff,
):
    copies = fetch(
        (
            (x_hbm, x),
            (matrix_hbm, matrix),
            (fine_table_hbm, fine_table),
            (coarse_table_hbm, coarse_table),
            (fine_inverse_hbm, fine_inverse),
            (coarse_inverse_hbm, coarse_inverse),
        ),
        sems,
    )
    for ref in (height, height_new, flux, diff):
        for edge in (pl.ds(0, 16), pl.ds(32, 16)):
            target = ref.at[..., edge, :]
            target[...] = jnp.zeros(target.shape, jnp.float32)
    for ref in (c_height, c_height_new, c_flux, c_diff):
        ref[...] = jnp.zeros(ref.shape, jnp.float32)
    copies[0].wait()
    copies[1].wait()

    parts = []
    for a in range(BLOCKS):
        for c in range(3):
            parts.append(x[c, :, a * 512 : (a + 1) * 512])
    phased = placed(jnp.concatenate(parts, axis=0), matrix[...])
    for c, p, a in planes(4):
        to = height.at[p, a] if c == 0 else flux.at[c - 1, p, a]
        base = (a * 3 + c) * ROWS
        to[16:32, :] = phased[base : base + ROWS, p * LANES : (p + 1) * LANES]

    def restricted(ref, p, a, first, count):
        total = None
        for q in (2 * p, 2 * p + 1):
            for r in (first, first + 1):
                part = ref(q, a)[pl.ds(r, count, stride=2), :]
                total = part if total is None else total + part
        return 0.25 * total

    for p in range(2):
        for a in range(BLOCKS):
            c_height[p, a, 12:20, :] = restricted(lambda q, b: height.at[q, b], p, a, 16, 8)
            for i in range(2):
                c_flux[i, p, a, 12:20, :] = restricted(lambda q, b: flux.at[i, q, b], p, a, 16, 8)
    for copy in copies[2:]:
        copy.wait()

    coarse_arguments = (
        2, COARSE_NAMES, coarse_table, coarse_inverse, COARSE_RATIO, c_height, c_height_new, c_flux, c_diff,
        ((8, 16), (8, 16), ((8, 16), (8, 16))), *at_tile(ROWS // 2, 12),
    )
    fine_arguments = (4, FINE_NAMES, fine_table, fine_inverse, FINE_RATIO)
    place = at_tile(ROWS, 16)
    wave_steps_in_turn(
        (*fine_arguments, height, height_new, flux, diff, ((12, 24), (12, 24), ((12, 24), (12, 24))), *place),
        coarse_arguments,
    )
    wave_step(*fine_arguments, height_new, height, flux, diff, ((12, 24), (8, 32), ((8, 32), (8, 32))), *place)
    wave_step(*fine_arguments, height, height_new, flux, diff, ((8, 32), (8, 32), ((8, 32), (4, 40))), *place)

    odd = on_odd()
    later = jnp.where(lax.axis_index("cuts") > 0, 1.0, 0.0).astype(jnp.float32)
    for n, (c, p, a) in enumerate(planes(2)):
        if c == 0:
            end = restricted(lambda q, b: height_new.at[q, b], p, a, 0, 24)
            step = c_height_new[p, a, 4:28, :]
        else:
            end = restricted(lambda q, b: flux.at[c - 1, q, b], p, a, 0, 24)
            step = c_flux[c - 1, p, a, 4:28, :]
        step = later * step
        u = end - step
        u_wide[c, p, a] = u
        c_diff[0, p, a, 4:28, :] = u
        to_next = c_diff[0, p, a, 11:25, :]
        to_previous = c_diff[0, p, a, 7:21, :]
        u_far[n * 14 : n * 14 + 14, :] = jnp.where(odd, to_next, to_previous)
        u_near[n * 14 : n * 14 + 14, :] = jnp.where(odd, to_previous, to_next)
        forward = c_diff[0, p, a, 19:25, :]
        backward = c_diff[0, p, a, 7:13, :]
        u_cross[n * 6 : n * 6 + 6, :] = jnp.where(odd, forward, backward)
    for c, p, a in planes(4):
        source = height_new.at[p, a] if c == 0 else flux.at[c - 1, p, a]
        step = c_height_new.at[p // 2, a] if c == 0 else c_flux.at[c - 1, p // 2, a]
        start, count = SPILL[c]
        base = (p * BLOCKS + a) * SPILL_ROWS + start
        for q in (0, 1):
            lines = pl.ds(8 + q, 16, stride=2)
            source[lines, :] = source[lines, :] - later * step[8:24, :]
        own[c, p, a] = source[16:32, :]
        to_next = source[32 : 32 + count, :]
        to_previous = source[16 - count : 16, :]
        spill_far[base : base + count, :] = jnp.where(odd, to_next, to_previous)
        base += NEAR_START
        u_near[base : base + count, :] = jnp.where(odd, to_previous, to_next)


def join_kernel(own, near, out):
    odd = on_odd()

    @pl.when(odd)
    def _():
        for n in range(24):
            base = n * 14
            out[base + 6 : base + 14, :] = own[base + 6 : base + 14, :]
            out[base : base + 6, :] = own[base : base + 6, :] + near[base + 8 : base + 14, :]

    @pl.when(jnp.logical_not(odd))
    def _():
        for n in range(24):
            base = n * 14
            out[base : base + 8, :] = own[base : base + 8, :]
            out[base + 8 : base + 14, :] = own[base + 8 : base + 14, :] + near[base : base + 6, :]


def later_kernel(rows, arrived, out):
    out[...] = rows[...]


def first_kernel(
    own, far, near, cross, inverse, table, one, wide, height, height_new, flux, diff
):
    odd = on_odd()
    for n, (c, p, a) in enumerate(planes(2)):
        to = height.at[p, a] if c == 0 else flux.at[c - 1, p, a]
        distant = far[n * 14 : n * 14 + 14, :]
        close = near[n * 14 : n * 14 + 14, :]
        to[0:8, :] = jnp.zeros((8, LANES), jnp.float32)
        to[8:32, :] = own[c, p, a]
        to[32:40, :] = jnp.zeros((8, LANES), jnp.float32)
        to[7:21, :] = to[7:21, :] + jnp.where(odd, close, distant)
        to[19:33, :] = to[19:33, :] + jnp.where(odd, distant, close)
        beyond = cross[n * 6 : n * 6 + 6, :]
        to[7:13, :] = to[7:13, :] + jnp.where(odd, beyond, 0.0)
        to[27:33, :] = to[27:33, :] + jnp.where(odd, 0.0, beyond)
    window = (8, 24)
    wave_step(
        2, COARSE_NAMES, table, inverse, COARSE_RATIO, height, height_new, flux, diff,
        (window, window, (window, window)), *at_tile(ROWS // 2, 16),
    )
    for c, p, a in planes(2):
        result = height_new.at[p, a] if c == 0 else flux.at[c - 1, p, a]
        one[c, p, a] = result[16:24, :]
        wide[c, p, a] = result[8:32, :]


def rest_kernel(wide, one, inverse, table, early, two, mixed, last, height, height_new, flux, diff):
    for c, p, a in planes(2):
        to = height.at[p, a] if c == 0 else flux.at[c - 1, p, a]
        to[8:32, :] = wide[c, p, a]
    arguments = (2, COARSE_NAMES, table, inverse, COARSE_RATIO)
    wave_step(*arguments, height, height_new, flux, diff, ((8, 24), (12, 16), ((12, 16), (12, 16))), *at_tile(ROWS // 2, 16))
    for c, p, a in planes(2):
        result = height_new.at[p, a] if c == 0 else flux.at[c - 1, p, a]
        two[c, p, a] = result[16:24, :]
    wave_step(*arguments, height_new, height, flux, diff, ((12, 16), (12, 16), ((16, 8), (16, 8))), *at_tile(ROWS // 2, 16))
    start = lax.axis_index("cuts") == 0
    for c, p, a in planes(2):
        result = height.at[p, a] if c == 0 else flux.at[c - 1, p, a]
        mixed[c, p, a] = jnp.where(start, result[16:24, :], one[c, p, a])
        last[c, p, a] = one[c, p, a]
        early[c, p, a] = one[c, p, a]


def natural_kernel(own, far, near, first, matrix, out, rows, total):
    odd = on_odd()
    for c, p, a in planes(2):
        rows[c, p, a, pl.ds(0, 8, stride=2), :] = first[c, p, a]
        rows[c, p, a, pl.ds(1, 8, stride=2), :] = first[c, p, a]
    for c, p, a in planes(4):
        start, count = SPILL[c]
        base = (p * BLOCKS + a) * SPILL_ROWS + start
        distant = far[base : base + count, :]
        close = near[NEAR_START + base : NEAR_START + base + count, :]
        to = total.at[c, p, a]
        to[0:ROWS, :] = own[c, p, a] + rows[c, p // 2, a]
        to[0:count, :] = to[0:count, :] + jnp.where(odd, close, distant)
        to[ROWS - count : ROWS, :] = to[ROWS - count : ROWS, :] + jnp.where(odd, distant, close)
    parts = []
    for a in range(BLOCKS):
        for c in range(3):
            parts.append(jnp.concatenate([total[c, p, a, 0:ROWS, :] for p in range(4)], axis=1))
    natural = placed(jnp.concatenate(parts, axis=0), matrix[...])
    for a in range(BLOCKS):
        for c in range(3):
            base = (a * 3 + c) * ROWS
            out[c, :, a * 512 : (a + 1) * 512] = natural[base : base + ROWS]


def final_kernel(base_end, second, third, fourth, matrix, out, rows, staged, sems):
    parts = []
    for a in range(BLOCKS):
        for c in range(3):
            pair = []
            for p in range(2):
                pair.append(second[c, p, a] + (third[c, p, a] + fourth[c, p, a]))
            parts.append(jnp.concatenate(pair, axis=1))
    spread = placed(jnp.concatenate(parts, axis=0), matrix[...])
    copies = []
    for a in range(BLOCKS):
        for c in range(3):
            base = (a * 3 + c) * 8
            for s in range(4):
                value = spread[base : base + 8, s * LANES : (s + 1) * LANES]
                rows[c, a * 4 + s, pl.ds(0, 8, stride=2), :] = value
                rows[c, a * 4 + s, pl.ds(1, 8, stride=2), :] = value
        for c in range(3):
            for s in range(4 * a, 4 * a + 4):
                cols = slice(s * LANES, (s + 1) * LANES)
                staged[c, :, cols] = base_end[c, :, cols] + rows[c, s]
        block = pl.ds(a * 512, 512)
        copies.append(pltpu.make_async_copy(staged.at[:, :, block], out.at[:, :, block], sems.at[a]))
        copies[-1].start()
    for copy in copies:
        copy.wait()


def f32(*shape):
    return jax.ShapeDtypeStruct(shape, jnp.float32)


def scratch(*shape):
    return pltpu.VMEM(shape, jnp.float32)


VMEM_SPEC = pl.BlockSpec(memory_space=pltpu.VMEM)
HBM_SPEC = pl.BlockSpec(memory_space=pltpu.HBM)


def in_hbm(array):
    return pltpu.with_memory_space_constraint(array, pltpu.HBM)


def call(kernel, ins, outs, scratches=(), name=None):
    return pl.pallas_call(
        kernel,
        in_specs=[HBM_SPEC if own else VMEM_SPEC for own in ins],
        out_shape=[shape for shape, _ in outs],
        out_specs=[HBM_SPEC if own else VMEM_SPEC for _, own in outs],
        scratch_shapes=scratches,
        name=name,
        compiler_params=pltpu.CompilerParams(vmem_limit_bytes=VMEM_LIMIT),
    )


def per_device(start_states):
    tiles = lax.axis_size("tile")
    far_pairs = [(i, j) for k in range(1, tiles - 1, 2) for i, j in ((k, k + 1), (k + 1, k))]
    near_pairs = [(i, i ^ 1) for i in range(tiles)]
    cross_pairs = [(i, i + 2) if i % 2 else (i + 2, i) for i in range(tiles - 2)]
    dma = pltpu.SemaphoreType.DMA

    def bf16(array):
        return jax.ShapeDtypeStruct(array.shape, jnp.bfloat16)

    def here(array):
        return pltpu.VMEM(array.shape, array.dtype)

    coarse = (f32(3, 2, BLOCKS, 8, LANES), False)
    spilt = (f32(16 * SPILL_ROWS + SPARE, LANES), False)
    far_rows = (f32(NEAR_START + SPARE, LANES), False)
    next_rows = (f32(24 * 6 + SPARE, LANES), False)
    fetched = (start_states[0], PHASES, FINE_INVERSE, FINE_TABLE, COARSE_INVERSE, COARSE_TABLE)
    own, spill_far, u_wide, u_far, near, cross, coarse_inverse = call(
        fine_kernel,
        [True] * 6,
        [
            (f32(3, 4, BLOCKS, ROWS, LANES), False),
            spilt,
            (f32(3, 2, BLOCKS, 24, LANES), False),
            far_rows,
            (f32(NEAR_START + 16 * SPILL_ROWS + SPARE, LANES), False),
            next_rows,
            (bf16(COARSE_INVERSE), False),
        ],
        [
            scratch(3, ROWS, NX),
            here(PHASES),
            here(FINE_INVERSE),
            here(FINE_TABLE),
            here(COARSE_TABLE),
            dma((6,)),
            scratch(4, BLOCKS, 48, LANES),
            scratch(4, BLOCKS, 48, LANES),
            scratch(2, 4, BLOCKS, 48, LANES),
            scratch(2, 4, BLOCKS, 48, LANES),
            scratch(2, BLOCKS, 32, LANES),
            scratch(2, BLOCKS, 32, LANES),
            scratch(2, 2, BLOCKS, 32, LANES),
            scratch(2, 2, BLOCKS, 32, LANES),
        ],
        name="fine",
    )(*[in_hbm(array) for array in fetched])
    near = lax.ppermute(near, "tile", near_pairs)
    cross = lax.ppermute(cross, "tile", cross_pairs)
    (u_far,) = call(join_kernel, [False] * 2, [far_rows], name="join")(u_far, near)
    u_far = lax.ppermute(u_far, "tile", far_pairs)
    (spill_far,) = call(later_kernel, [False] * 2, [spilt], name="later")(spill_far, cross)
    spill_far = lax.ppermute(spill_far, "tile", far_pairs)

    state = [
        scratch(2, BLOCKS, 48, LANES),
        scratch(2, BLOCKS, 48, LANES),
        scratch(2, 2, BLOCKS, 48, LANES),
        scratch(2, 2, BLOCKS, 48, LANES),
    ]
    one, wide = call(
        first_kernel, [False] * 6, [coarse, (f32(3, 2, BLOCKS, 24, LANES), False)], state, name="first"
    )(u_wide, u_far, near, cross, coarse_inverse, COARSE_TABLE)
    early, two, mixed, last = call(rest_kernel, [False] * 4, [coarse] * 4, state, name="rest")(
        wide, one, coarse_inverse, COARSE_TABLE
    )
    first = lax.ppermute(early, "cuts", [(0, 1)])
    second = lax.ppermute(two, "cuts", [(0, 2), (1, 3)])
    third = lax.ppermute(mixed, "cuts", [(0, 3), (1, 2)])
    fourth = lax.ppermute(last, "cuts", [(2, 3)])
    (natural,) = call(
        natural_kernel,
        [False] * 5,
        [(f32(3, ROWS, NX), False)],
        [scratch(3, 2, BLOCKS, ROWS, LANES), scratch(3, 4, BLOCKS, ROWS + SPARE, LANES)],
        name="natural",
    )(own, spill_far, near, first, NATURAL)
    (out,) = call(
        final_kernel,
        [False] * 5,
        [(f32(3, ROWS, NX), True)],
        [scratch(3, 16, ROWS, LANES), scratch(3, ROWS, NX), dma((BLOCKS,))],
        name="final",
    )(natural, second, third, fourth, SPREAD)
    return out[None]


def solution(mesh):
    spec = P("cuts", None, "tile", None)
    return jax.shard_map(per_device, mesh=mesh, in_specs=(spec,), out_specs=spec, check_vma=False)
```

time: 35.8 us -> 31.8 us (0.89)
  waiting for transfers between devices: 8.53 us -> 2.19 us
  starting transfers between devices: 16.9 us -> 20.9 us
  local copies, waits for them, and re-layouts: 1.07 us -> 0.02 us
  Pallas kernels: 8.8 us -> 7.94 us
    ppermute x4, starting transfers between devices: 8.12 us -> 12.9 us  [the longest x1 4.55 us: per_device(): cross = lax.ppermute(cross, 'tile', cross_pairs)]
    ppermute x4, waiting for transfers between devices: 3.36 us -> 0.01 us  [the longest x1 0.01 us: per_device(): first = lax.ppermute(early, 'cuts', [(0, 1)])]
    ppermute x1, waiting for transfers between devices: 4.08 us -> 1.14 us  [per_device(): u_far = lax.ppermute(u_far, 'tile', far_pairs)]
    unnamed x14 -> x6, local copies, waits for them, and re-layouts: 1.07 us -> 0.02 us
    pallas_call x6, Pallas kernels: 7.82 us -> 6.96 us  [the longest x1 4.61 us: per_device(): call(fine_kernel, [True] * 6, [(f32(3, 4, BLOCKS, ROWS, LANES), False), s...]
    ppermute x1, starting transfers between devices: 4 us -> 3.21 us  [per_device(): u_far = lax.ppermute(u_far, 'tile', far_pairs)]
  transfers between devices with their start and end apart: 8 -> 8, of which waited for: 3 -> 2; matrix products, arithmetic and copies ran while one was open for 0% -> 0% of each run, Pallas kernels for 8% -> 8%
where the time goes in v3:
time: 31.8 us; the launch traced here: 31.2 us
  starting transfers between devices  20.9 us (66%)
  Pallas kernels  7.94 us (25%)
  waiting for transfers between devices  2.19 us (7%)
    pallas_call x1, Pallas kernels, per_device(): call(fine_kernel, [True] * 6, [(f32(3, 4, BLOCKS, ROWS, LANES), False), s...  4.61 us
    ppermute x1, starting transfers between devices, per_device(): cross = lax.ppermute(cross, 'tile', cross_pairs)  4.55 us
    ppermute x1, starting transfers between devices, per_device(): spill_far = lax.ppermute(spill_far, 'tile', far_pairs)  4.46 us
    ppermute x1, starting transfers between devices, per_device(): first = lax.ppermute(early, 'cuts', [(0, 1)])  3.84 us
    ppermute x1, starting transfers between devices, per_device(): u_far = lax.ppermute(u_far, 'tile', far_pairs)  3.21 us
    ppermute x1, starting transfers between devices, per_device(): second = lax.ppermute(two, 'cuts', [(0, 2), (1, 3)])  2.62 us
    ppermute x1, starting transfers between devices, per_device(): third = lax.ppermute(mixed, 'cuts', [(0, 3), (1, 2)])  1.46 us
    pallas_call x1, Pallas kernels, per_device(): call(rest_kernel, [False] * 4, [coarse] * 4, state, name='rest')  1.18 us
  transfers between devices with their start and end apart: 8, of which 2 were waited for; matrix products, arithmetic and copies ran while one was open for 0% of the time, Pallas kernels for 8%

profile of v3, /device:TPU:16, one launch (start us, length us, event | category | flops | bytes accessed | tf_op | source)
XLA Modules:
  0.0 31.2 jit_solution(3840939913412734885)
XLA Ops:
  0.0 4.6 %fine.1 = (f32[3,4,4,16,128]{4,3,2,1,0:T(8,128)S(1)}, f32[408,128]{1,0:T(8,128)S(1)}, f32[3,2,4,24,128]{4,3,2,1,0:T(8,128)S(1)}, f32[344,128]{1,0:T(8,128)S(1)},...) custom-call(f32[3,16,2048]{2,1,0:T(8,128)} %bitcast.2, ...), custom_call_target="tpu_custom_call" | custom-call | tf_op jit(solution)/shard_map/fine/pallas_call | solution.py:579
  4.6 0.1 collective-permute-start.2
  4.7 4.6 %collective-permute-start = (f32[152,128]{1,0:T(8,128)S(1)}, f32[152,128]{1,0:T(8,128)S(1)}, u32[]{:S(2)}, u32[]{:S(2)}) collective-permute-start(f32[152,128]{1,0:T(8,128)S(1)} %get-tuple-element.20), channel_id=1, source_target_pairs={{2,0},{1,3},{4,2},{3,5},{6,4},{5,7},{8,6},{7,9},{10,8},{9,11},{12,... | collective-permute-start | bytes 233480 | tf_op jit(solution)/shard_map/ppermute | solution.py:610
  9.3 0.0 collective-permute-done.2.near
  9.3 3.2 %collective-permute-start.3 = (f32[344,128]{1,0:T(8,128)S(1)}, f32[344,128]{1,0:T(8,128)S(1)}, u32[]{:S(2)}, u32[]{:S(2)}) collective-permute-start(f32[344,128]{1,0:T(8,128)S(1)} %join.1), channel_id=1, source_target_pairs={{1,2},{2,1},{3,4},{4,3},{5,6},{6,5},{7,8},{8,7},{9,10},{10,9},{11,... | collective-permute-start | bytes 528392 | tf_op jit(solution)/shard_map/ppermute | solution.py:612
  12.5 0.0 collective-permute-done.arrived.cross
  12.6 0.0 copy-start.2
  12.6 4.5 %collective-permute-start.1 = (f32[408,128]{1,0:T(8,128)S(1)}, f32[408,128]{1,0:T(8,128)S(1)}, u32[]{:S(2)}, u32[]{:S(2)}) collective-permute-start(f32[408,128]{1,0:T(8,128)S(1)} %later.1), channel_id=1, source_target_pairs={{1,2},{2,1},{3,4},{4,3},{5,6},{6,5},{7,8},{8,7},{9,10},{10,9},{11,... | collective-permute-start | bytes 626696 | tf_op jit(solution)/shard_map/ppermute | solution.py:614
  17.1 1.1 %collective-permute-done.3.far = f32[344,128]{1,0:T(8,128)S(1)} collective-permute-done((f32[344,128]{1,0:T(8,128)S(1)}, f32[344,128]{1,0:T(8,128)S(1)}, u32[]{:S(2)}, u32[]{:S(2)}) %collective-permute-start.3) | collective-permute-done | bytes 176160 | tf_op jit(solution)/shard_map/ppermute | solution.py:612
  18.2 0.0 copy-done.2
  18.2 0.7 %first.1 = (f32[3,2,4,8,128]{4,3,2,1,0:T(8,128)S(1)}, f32[3,2,4,24,128]{4,3,2,1,0:T(8,128)S(1)}) custom-call(f32[3,2,4,24,128]{4,3,2,1,0:T(8,128)S(1)} %get-tuple-element.22.own, f32[344,128]{1,0:T(8,128)S(1)} %collective-permute-done.3.far, f32[744,128]{1,0:T(8,128)S(1)} %collective-permute-done.2.near, f32[152,128]{1,0:T(8,128)S(1)} %collective-permute-done.arrived.cross, ...), custom_call_target="tpu_custom_call" | custom-call | tf_op jit(solution)/shard_map/first/pallas_call | solution.py:622
  18.9 0.0 copy-start
  18.9 1.2 %rest.1 = (f32[3,2,4,8,128]{4,3,2,1,0:T(8,128)S(1)}, f32[3,2,4,8,128]{4,3,2,1,0:T(8,128)S(1)}, f32[3,2,4,8,128]{4,3,2,1,0:T(8,128)S(1)}, f32[3,2,4,8,128]{4,3,2,1,0:T(8,128)S(1)}) custom-call(f32[3,2,4,24,128]{4,3,2,1,0:T(8,128)S(1)} %get-tuple-element.25.wide, f32[3,2,4,8,128]{4,3,2,1,0:T(8,128)S(1)} %get-tuple-element.26.one, ...), custom_call_target="tpu_custom_call" | custom-call | tf_op jit(solution)/shard_map/rest/pallas_call | solution.py:625
  20.1 3.8 %collective-permute-start.4 = (f32[3,2,4,8,128]{4,3,2,1,0:T(8,128)S(1)}, f32[3,2,4,8,128]{4,3,2,1,0:T(8,128)S(1)}, u32[]{:S(2)}, u32[]{:S(2)}) collective-permute-start(f32[3,2,4,8,128]{4,3,2,1,0:T(8,128)S(1)} %get-tuple-element.27), channel_id=1, source_target_pairs={{0,32},{1,33},{2,34},{3,35},{4,36},{5,37},{6,38},{7,39},{8,40},{9,... | collective-permute-start | bytes 294920 | tf_op jit(solution)/shard_map/ppermute | solution.py:628
  23.9 2.6 %collective-permute-start.5 = (f32[3,2,4,8,128]{4,3,2,1,0:T(8,128)S(1)}, f32[3,2,4,8,128]{4,3,2,1,0:T(8,128)S(1)}, u32[]{:S(2)}, u32[]{:S(2)}) collective-permute-start(f32[3,2,4,8,128]{4,3,2,1,0:T(8,128)S(1)} %get-tuple-element.28), channel_id=1, source_target_pairs={{0,64},{32,96},{1,65},{33,97},{2,66},{34,98},{3,67},{35,99},{4,68}... | collective-permute-start | bytes 294920 | tf_op jit(solution)/shard_map/ppermute | solution.py:629
  26.6 1.5 %collective-permute-start.6 = (f32[3,2,4,8,128]{4,3,2,1,0:T(8,128)S(1)}, f32[3,2,4,8,128]{4,3,2,1,0:T(8,128)S(1)}, u32[]{:S(2)}, u32[]{:S(2)}) collective-permute-start(f32[3,2,4,8,128]{4,3,2,1,0:T(8,128)S(1)} %get-tuple-element.29), channel_id=1, source_target_pairs={{0,96},{32,64},{1,97},{33,65},{2,98},{34,66},{3,99},{35,67},{4,100... | collective-permute-start | bytes 294920 | tf_op jit(solution)/shard_map/ppermute | solution.py:630
  28.0 0.7 %collective-permute-start.7 = (f32[3,2,4,8,128]{4,3,2,1,0:T(8,128)S(1)}, f32[3,2,4,8,128]{4,3,2,1,0:T(8,128)S(1)}, u32[]{:S(2)}, u32[]{:S(2)}) collective-permute-start(f32[3,2,4,8,128]{4,3,2,1,0:T(8,128)S(1)} %get-tuple-element.30), channel_id=1, source_target_pairs={{64,96},{65,97},{66,98},{67,99},{68,100},{69,101},{70,102},{71,103... | collective-permute-start | bytes 294920 | tf_op jit(solution)/shard_map/ppermute | solution.py:631
  28.7 0.0 collective-permute-done.1.far
  28.7 0.0 collective-permute-done.4.first
  28.7 0.0 copy-done
  28.7 0.0 copy-start.1
  28.8 0.4 %natural.1.base_end = f32[3,16,2048]{2,1,0:T(8,128)S(1)} custom-call(f32[3,4,4,16,128]{4,3,2,1,0:T(8,128)S(1)} %get-tuple-element.18.own, f32[408,128]{1,0:T(8,128)S(1)} %collective-permute-done.1.far, f32[744,128]{1,0:T(8,128)S(1)} %collective-permute-done.2.near, f32[3,2,4,8,128]{4,3,2,1,0:T(8,128)S(1)} %collective-permute-done.4.first, ...), custom_call_target="tpu_custom_call" | custom-call | tf_op jit(solution)/shard_map/natural/pallas_call | solution.py:632
  29.2 0.0 collective-permute-done.5.second
  29.2 1.0 %collective-permute-done.6.third = f32[3,2,4,8,128]{4,3,2,1,0:T(8,128)S(1)} collective-permute-done((f32[3,2,4,8,128]{4,3,2,1,0:T(8,128)S(1)}, f32[3,2,4,8,128]{4,3,2,1,0:T(8,128)S(1)}, u32[]{:S(2)}, u32[]{:S(2)}) %collective-permute-start.6) | collective-permute-done | bytes 98336 | tf_op jit(solution)/shard_map/ppermute | solution.py:630
  30.2 0.0 collective-permute-done.7.fourth
  30.2 0.0 copy-done.1
  30.2 1.0 %final.1 = f32[3,16,2048]{2,1,0:T(8,128)} custom-call(f32[3,16,2048]{2,1,0:T(8,128)S(1)} %natural.1.base_end, f32[3,2,4,8,128]{4,3,2,1,0:T(8,128)S(1)} %collective-permute-done.5.second, f32[3,2,4,8,128]{4,3,2,1,0:T(8,128)S(1)} %collective-permute-done.6.third, f32[3,2,4,8,128]{4,3,2,1,0:T(8,128)S(1)} %collective-permute-done.7.fourth, ...), custom_call_target="tpu_custom_call" | custom-call | tf_op jit(solution)/shard_map/final/pallas_call | solution.py:639
  (2 shorter events, 0.1 us)
Async XLA Ops:
  4.6 4.7 %collective-permute-start.2 = (f32[744,128]{1,0:T(8,128)S(1)}, f32[744,128]{1,0:T(8,128)S(1)}, u32[]{:S(2)}, u32[]{:S(2)}) collective-permute-start(f32[744,128]{1,0:T(8,128)S(1)} %get-tuple-element.21), channel_id=1, source_target_pairs={{0,1},{1,0},{2,3},{3,2},{4,5},{5,4},{6,7},{7,6},{8,9},{9,8},{10,11... | collective-permute-start | bytes 1142792 | tf_op jit(solution)/shard_map/ppermute | solution.py:609
  4.7 7.8 %collective-permute-start = (f32[152,128]{1,0:T(8,128)S(1)}, f32[152,128]{1,0:T(8,128)S(1)}, u32[]{:S(2)}, u32[]{:S(2)}) collective-permute-start(f32[152,128]{1,0:T(8,128)S(1)} %get-tuple-element.20), channel_id=1, source_target_pairs={{2,0},{1,3},{4,2},{3,5},{6,4},{5,7},{8,6},{7,9},{10,8},{9,11},{12,... | collective-permute-start | bytes 233480 | tf_op jit(solution)/shard_map/ppermute | solution.py:610
  9.3 8.9 %collective-permute-start.3 = (f32[344,128]{1,0:T(8,128)S(1)}, f32[344,128]{1,0:T(8,128)S(1)}, u32[]{:S(2)}, u32[]{:S(2)}) collective-permute-start(f32[344,128]{1,0:T(8,128)S(1)} %join.1), channel_id=1, source_target_pairs={{1,2},{2,1},{3,4},{4,3},{5,6},{6,5},{7,8},{8,7},{9,10},{10,9},{11,... | collective-permute-start | bytes 528392 | tf_op jit(solution)/shard_map/ppermute | solution.py:612
  12.6 5.7 %copy-start.2 = (f32[44,128]{1,0:T(8,128)S(1)}, f32[44,128]{1,0:T(8,128)}, u32[]{:S(2)}) copy-start(f32[44,128]{1,0:T(8,128)} %constant.18.clone.coarse_table_hbm.table) | copy-start | bytes 67588
  12.6 16.1 %collective-permute-start.1 = (f32[408,128]{1,0:T(8,128)S(1)}, f32[408,128]{1,0:T(8,128)S(1)}, u32[]{:S(2)}, u32[]{:S(2)}) collective-permute-start(f32[408,128]{1,0:T(8,128)S(1)} %later.1), channel_id=1, source_target_pairs={{1,2},{2,1},{3,4},{4,3},{5,6},{6,5},{7,8},{8,7},{9,10},{10,9},{11,... | collective-permute-start | bytes 626696 | tf_op jit(solution)/shard_map/ppermute | solution.py:614
  18.9 9.8 %copy-start = (bf16[512,512]{1,0:T(8,128)(2,1)S(1)}, bf16[512,512]{1,0:T(8,128)(2,1)}, u32[]{:S(2)}) copy-start(bf16[512,512]{1,0:T(8,128)(2,1)} %constant.19.clone.matrix) | copy-start | bytes 1572868
  20.1 8.6 %collective-permute-start.4 = (f32[3,2,4,8,128]{4,3,2,1,0:T(8,128)S(1)}, f32[3,2,4,8,128]{4,3,2,1,0:T(8,128)S(1)}, u32[]{:S(2)}, u32[]{:S(2)}) collective-permute-start(f32[3,2,4,8,128]{4,3,2,1,0:T(8,128)S(1)} %get-tuple-element.27), channel_id=1, source_target_pairs={{0,32},{1,33},{2,34},{3,35},{4,36},{5,37},{6,38},{7,39},{8,40},{9,... | collective-permute-start | bytes 294920 | tf_op jit(solution)/shard_map/ppermute | solution.py:628
  23.9 5.2 %collective-permute-start.5 = (f32[3,2,4,8,128]{4,3,2,1,0:T(8,128)S(1)}, f32[3,2,4,8,128]{4,3,2,1,0:T(8,128)S(1)}, u32[]{:S(2)}, u32[]{:S(2)}) collective-permute-start(f32[3,2,4,8,128]{4,3,2,1,0:T(8,128)S(1)} %get-tuple-element.28), channel_id=1, source_target_pairs={{0,64},{32,96},{1,65},{33,97},{2,66},{34,98},{3,67},{35,99},{4,68}... | collective-permute-start | bytes 294920 | tf_op jit(solution)/shard_map/ppermute | solution.py:629
  26.6 3.7 %collective-permute-start.6 = (f32[3,2,4,8,128]{4,3,2,1,0:T(8,128)S(1)}, f32[3,2,4,8,128]{4,3,2,1,0:T(8,128)S(1)}, u32[]{:S(2)}, u32[]{:S(2)}) collective-permute-start(f32[3,2,4,8,128]{4,3,2,1,0:T(8,128)S(1)} %get-tuple-element.29), channel_id=1, source_target_pairs={{0,96},{32,64},{1,97},{33,65},{2,98},{34,66},{3,99},{35,67},{4,100... | collective-permute-start | bytes 294920 | tf_op jit(solution)/shard_map/ppermute | solution.py:630
  28.0 2.2 %collective-permute-start.7 = (f32[3,2,4,8,128]{4,3,2,1,0:T(8,128)S(1)}, f32[3,2,4,8,128]{4,3,2,1,0:T(8,128)S(1)}, u32[]{:S(2)}, u32[]{:S(2)}) collective-permute-start(f32[3,2,4,8,128]{4,3,2,1,0:T(8,128)S(1)} %get-tuple-element.30), channel_id=1, source_target_pairs={{64,96},{65,97},{66,98},{67,99},{68,100},{69,101},{70,102},{71,103... | collective-permute-start | bytes 294920 | tf_op jit(solution)/shard_map/ppermute | solution.py:631
  28.7 1.5 %copy-start.1 = (bf16[256,512]{1,0:T(8,128)(2,1)S(1)}, bf16[256,512]{1,0:T(8,128)(2,1)}, u32[]{:S(2)}) copy-start(bf16[256,512]{1,0:T(8,128)(2,1)} %constant.20.clone.matrix) | copy-start | bytes 786436

commit v4 on v3

--- a/solution.py
+++ b/solution.py
@@ -18,6 +18,7 @@
 UNKNOWNS = 512
 BLOCKS = 4
 LANES = 128
+COST = 10**10
 VMEM_LIMIT = 48 * 1024 * 1024
 
 
@@ -110,7 +111,6 @@
     return matrix
 
 
-PHASES = phase_matrix().astype(ml_dtypes.bfloat16)
 NATURAL = phase_matrix().T.copy().astype(ml_dtypes.bfloat16)
 
 
@@ -275,11 +275,6 @@
         pass
 
 
-def wave_steps_in_turn(*steps):
-    for _ in zip(*[step_stages(*arguments) for arguments in steps]):
-        pass
-
-
 FINE_RATIO = FINE_STEP / (2.0 * FINE_SPACING)
 COARSE_RATIO = COARSE_STEP / (2.0 * COARSE_SPACING)
 
@@ -294,7 +289,8 @@
 
 SPILL = ((0, 8), (8, 8), (16, 9))
 SPILL_ROWS = 25
-NEAR_START = 24 * 14
+FAR_ROWS = 24 * 14
+NEXT_ROWS = 24 * 6
 SPARE = 8
 
 
@@ -310,15 +306,14 @@
 
 
 def fine_kernel(
-    x_hbm, matrix_hbm, fine_inverse_hbm, fine_table_hbm, coarse_inverse_hbm, coarse_table_hbm,
-    own, spill_far, u_wide, u_far, u_near, u_cross, coarse_inverse,
+    x_hbm, fine_inverse_hbm, fine_table_hbm, coarse_inverse_hbm, coarse_table_hbm,
+    wide_end, propagated, u_wide, u_far, u_near, coarse_inverse,
     x, matrix, fine_inverse, fine_table, coarse_table, sems,
     height, height_new, flux, diff, c_height, c_height_new, c_flux, c_diff,
 ):
     copies = fetch(
         (
             (x_hbm, x),
-            (matrix_hbm, matrix),
             (fine_table_hbm, fine_table),
             (coarse_table_hbm, coarse_table),
             (fine_inverse_hbm, fine_inverse),
@@ -332,8 +327,11 @@
             target[...] = jnp.zeros(target.shape, jnp.float32)
     for ref in (c_height, c_height_new, c_flux, c_diff):
         ref[...] = jnp.zeros(ref.shape, jnp.float32)
+    row = lax.broadcasted_iota(jnp.int32, (512, 512), 0)
+    column = lax.broadcasted_iota(jnp.int32, (512, 512), 1)
+    chosen = column == (row & 3) * LANES + (row >> 2)
+    matrix[...] = jnp.where(chosen, 1.0, 0.0).astype(jnp.bfloat16)
     copies[0].wait()
-    copies[1].wait()
 
     parts = []
     for a in range(BLOCKS):
@@ -358,7 +356,7 @@
             c_height[p, a, 12:20, :] = restricted(lambda q, b: height.at[q, b], p, a, 16, 8)
             for i in range(2):
                 c_flux[i, p, a, 12:20, :] = restricted(lambda q, b: flux.at[i, q, b], p, a, 16, 8)
-    for copy in copies[2:]:
+    for copy in copies[1:3]:
         copy.wait()
 
     coarse_arguments = (
@@ -367,10 +365,18 @@
     )
     fine_arguments = (4, FINE_NAMES, fine_table, fine_inverse, FINE_RATIO)
     place = at_tile(ROWS, 16)
-    wave_steps_in_turn(
-        (*fine_arguments, height, height_new, flux, diff, ((12, 24), (12, 24), ((12, 24), (12, 24))), *place),
-        coarse_arguments,
+    windows = ((12, 24), (12, 24), ((12, 24), (12, 24)))
+    stages = (
+        step_stages(*fine_arguments, height, height_new, flux, diff, windows, *place),
+        step_stages(*coarse_arguments),
     )
+    for _ in range(2):
+        for stage in stages:
+            next(stage)
+    for copy in copies[3:]:
+        copy.wait()
+    for _ in zip(*stages):
+        pass
     wave_step(*fine_arguments, height_new, height, flux, diff, ((12, 24), (8, 32), ((8, 32), (8, 32))), *place)
     wave_step(*fine_arguments, height, height_new, flux, diff, ((8, 32), (8, 32), ((8, 32), (4, 40))), *place)
 
@@ -384,6 +390,7 @@
             end = restricted(lambda q, b: flux.at[c - 1, q, b], p, a, 0, 24)
             step = c_flux[c - 1, p, a, 4:28, :]
         step = later * step
+        propagated[c, p, a] = step[4:20]
         u = end - step
         u_wide[c, p, a] = u
         c_diff[0, p, a, 4:28, :] = u
@@ -391,23 +398,27 @@
         to_previous = c_diff[0, p, a, 7:21, :]
         u_far[n * 14 : n * 14 + 14, :] = jnp.where(odd, to_next, to_previous)
         u_near[n * 14 : n * 14 + 14, :] = jnp.where(odd, to_previous, to_next)
-        forward = c_diff[0, p, a, 19:25, :]
-        backward = c_diff[0, p, a, 7:13, :]
-        u_cross[n * 6 : n * 6 + 6, :] = jnp.where(odd, forward, backward)
     for c, p, a in planes(4):
         source = height_new.at[p, a] if c == 0 else flux.at[c - 1, p, a]
-        step = c_height_new.at[p // 2, a] if c == 0 else c_flux.at[c - 1, p // 2, a]
+        wide_end[c, p, a] = source[4:44, :]
+
+
+def spill_kernel(wide_end, propagated, arrived, own, to_far, to_near, rows):
+    del arrived
+    odd = on_odd()
+    for c, p, a in planes(2):
+        value = propagated[c, p, a]
+        rows[c, p, a, pl.ds(0, 16, stride=2), :] = value
+        rows[c, p, a, pl.ds(1, 16, stride=2), :] = value
+    for c, p, a in planes(4):
         start, count = SPILL[c]
         base = (p * BLOCKS + a) * SPILL_ROWS + start
-        for q in (0, 1):
-            lines = pl.ds(8 + q, 16, stride=2)
-            source[lines, :] = source[lines, :] - later * step[8:24, :]
-        own[c, p, a] = source[16:32, :]
-        to_next = source[32 : 32 + count, :]
-        to_previous = source[16 - count : 16, :]
-        spill_far[base : base + count, :] = jnp.where(odd, to_next, to_previous)
-        base += NEAR_START
-        u_near[base : base + count, :] = jnp.where(odd, to_previous, to_next)
+        wide_end[c, p, a, 4:36, :] = wide_end[c, p, a, 4:36, :] - rows[c, p // 2, a]
+        own[c, p, a] = wide_end[c, p, a, 12:28, :]
+        to_next = wide_end[c, p, a, 28 : 28 + count, :]
+        to_previous = wide_end[c, p, a, 12 - count : 12, :]
+        to_far[base : base + count, :] = jnp.where(odd, to_next, to_previous)
+        to_near[base : base + count, :] = jnp.where(odd, to_previous, to_next)
 
 
 def join_kernel(own, near, out):
@@ -428,16 +439,19 @@
             out[base + 8 : base + 14, :] = own[base + 8 : base + 14, :] + near[base : base + 6, :]
 
 
-def later_kernel(rows, arrived, out):
-    out[...] = rows[...]
-
-
-def first_kernel(
-    own, far, near, cross, inverse, table, one, wide, height, height_new, flux, diff
-):
+def forward_kernel(far, rows, out):
+    odd = on_odd()
+    for n in range(24):
+        low = far[n * 14 : n * 14 + 6, :]
+        high = far[n * 14 + 8 : n * 14 + 14, :]
+        out[n * 6 : n * 6 + 6, :] = jnp.where(odd, low, high)
+    out[NEXT_ROWS : NEXT_ROWS + 16 * SPILL_ROWS, :] = rows[0 : 16 * SPILL_ROWS, :]
+
+
+def assemble_kernel(own, far, near, out):
     odd = on_odd()
     for n, (c, p, a) in enumerate(planes(2)):
-        to = height.at[p, a] if c == 0 else flux.at[c - 1, p, a]
+        to = out.at[c, p, a]
         distant = far[n * 14 : n * 14 + 14, :]
         close = near[n * 14 : n * 14 + 14, :]
         to[0:8, :] = jnp.zeros((8, LANES), jnp.float32)
@@ -445,7 +459,14 @@
         to[32:40, :] = jnp.zeros((8, LANES), jnp.float32)
         to[7:21, :] = to[7:21, :] + jnp.where(odd, close, distant)
         to[19:33, :] = to[19:33, :] + jnp.where(odd, distant, close)
+
+
+def first_kernel(assembled, cross, inverse, table, one, wide, height, height_new, flux, diff):
+    odd = on_odd()
+    for n, (c, p, a) in enumerate(planes(2)):
+        to = height.at[p, a] if c == 0 else flux.at[c - 1, p, a]
         beyond = cross[n * 6 : n * 6 + 6, :]
+        to[0:40, :] = assembled[c, p, a, 0:40, :]
         to[7:13, :] = to[7:13, :] + jnp.where(odd, beyond, 0.0)
         to[27:33, :] = to[27:33, :] + jnp.where(odd, 0.0, beyond)
     window = (8, 24)
@@ -486,7 +507,7 @@
         start, count = SPILL[c]
         base = (p * BLOCKS + a) * SPILL_ROWS + start
         distant = far[base : base + count, :]
-        close = near[NEAR_START + base : NEAR_START + base + count, :]
+        close = near[NEXT_ROWS + base : NEXT_ROWS + base + count, :]
         to = total.at[c, p, a]
         to[0:ROWS, :] = own[c, p, a] + rows[c, p // 2, a]
         to[0:count, :] = to[0:count, :] + jnp.where(odd, close, distant)
@@ -546,7 +567,7 @@
     return pltpu.with_memory_space_constraint(array, pltpu.HBM)
 
 
-def call(kernel, ins, outs, scratches=(), name=None):
+def call(kernel, ins, outs, scratches=(), name=None, cost=None):
     return pl.pallas_call(
         kernel,
         in_specs=[HBM_SPEC if own else VMEM_SPEC for own in ins],
@@ -554,6 +575,7 @@
         out_specs=[HBM_SPEC if own else VMEM_SPEC for _, own in outs],
         scratch_shapes=scratches,
         name=name,
+        cost_estimate=cost,
         compiler_params=pltpu.CompilerParams(vmem_limit_bytes=VMEM_LIMIT),
     )
 
@@ -562,7 +584,6 @@
     tiles = lax.axis_size("tile")
     far_pairs = [(i, j) for k in range(1, tiles - 1, 2) for i, j in ((k, k + 1), (k + 1, k))]
     near_pairs = [(i, i ^ 1) for i in range(tiles)]
-    cross_pairs = [(i, i + 2) if i % 2 else (i + 2, i) for i in range(tiles - 2)]
     dma = pltpu.SemaphoreType.DMA
 
     def bf16(array):
@@ -573,28 +594,27 @@
 
     coarse = (f32(3, 2, BLOCKS, 8, LANES), False)
     spilt = (f32(16 * SPILL_ROWS + SPARE, LANES), False)
-    far_rows = (f32(NEAR_START + SPARE, LANES), False)
-    next_rows = (f32(24 * 6 + SPARE, LANES), False)
-    fetched = (start_states[0], PHASES, FINE_INVERSE, FINE_TABLE, COARSE_INVERSE, COARSE_TABLE)
-    own, spill_far, u_wide, u_far, near, cross, coarse_inverse = call(
+    far_rows = (f32(FAR_ROWS + SPARE, LANES), False)
+    last_rows = (f32(NEXT_ROWS + 16 * SPILL_ROWS + SPARE, LANES), False)
+    fetched = (start_states[0], FINE_INVERSE, FINE_TABLE, COARSE_INVERSE, COARSE_TABLE)
+    wide_end, propagated, u_wide, u_far, u_near, coarse_inverse = call(
         fine_kernel,
-        [True] * 6,
+        [True] * 5,
         [
-            (f32(3, 4, BLOCKS, ROWS, LANES), False),
-            spilt,
+            (f32(3, 4, BLOCKS, 40, LANES), False),
+            (f32(3, 2, BLOCKS, 16, LANES), False),
             (f32(3, 2, BLOCKS, 24, LANES), False),
             far_rows,
-            (f32(NEAR_START + 16 * SPILL_ROWS + SPARE, LANES), False),
-            next_rows,
+            far_rows,
             (bf16(COARSE_INVERSE), False),
         ],
         [
             scratch(3, ROWS, NX),
-            here(PHASES),
+            pltpu.VMEM((512, 512), jnp.bfloat16),
             here(FINE_INVERSE),
             here(FINE_TABLE),
             here(COARSE_TABLE),
-            dma((6,)),
+            dma((5,)),
             scratch(4, BLOCKS, 48, LANES),
             scratch(4, BLOCKS, 48, LANES),
             scratch(2, 4, BLOCKS, 48, LANES),
@@ -606,12 +626,19 @@
         ],
         name="fine",
     )(*[in_hbm(array) for array in fetched])
+    u_near = lax.ppermute(u_near, "tile", near_pairs)
+    (u_far,) = call(join_kernel, [False] * 2, [far_rows], name="join")(u_far, u_near)
+    own, spill_far, spill_near = call(
+        spill_kernel,
+        [False] * 3,
+        [(f32(3, 4, BLOCKS, ROWS, LANES), False), spilt, spilt],
+        [scratch(3, 2, BLOCKS, 32, LANES)],
+        name="spill",
+    )(wide_end, propagated, u_far)
+    u_far = lax.ppermute(u_far, "tile", far_pairs)
+    spill_far = lax.ppermute(spill_far, "tile", far_pairs)
+    (near,) = call(forward_kernel, [False] * 2, [last_rows], name="forward")(u_far, spill_near)
     near = lax.ppermute(near, "tile", near_pairs)
-    cross = lax.ppermute(cross, "tile", cross_pairs)
-    (u_far,) = call(join_kernel, [False] * 2, [far_rows], name="join")(u_far, near)
-    u_far = lax.ppermute(u_far, "tile", far_pairs)
-    (spill_far,) = call(later_kernel, [False] * 2, [spilt], name="later")(spill_far, cross)
-    spill_far = lax.ppermute(spill_far, "tile", far_pairs)
 
     state = [
         scratch(2, BLOCKS, 48, LANES),
@@ -619,9 +646,16 @@
         scratch(2, 2, BLOCKS, 48, LANES),
         scratch(2, 2, BLOCKS, 48, LANES),
     ]
+    (assembled,) = call(
+        assemble_kernel,
+        [False] * 3,
+        [(f32(3, 2, BLOCKS, 48, LANES), False)],
+        name="assemble",
+        cost=pl.CostEstimate(flops=COST, bytes_accessed=COST // 100, transcendentals=0),
+    )(u_wide, u_far, u_near)
     one, wide = call(
-        first_kernel, [False] * 6, [coarse, (f32(3, 2, BLOCKS, 24, LANES), False)], state, name="first"
-    )(u_wide, u_far, near, cross, coarse_inverse, COARSE_TABLE)
+        first_kernel, [False] * 4, [coarse, (f32(3, 2, BLOCKS, 24, LANES), False)], state, name="first"
+    )(assembled, near, coarse_inverse, COARSE_TABLE)
     early, two, mixed, last = call(rest_kernel, [False] * 4, [coarse] * 4, state, name="rest")(
         wide, one, coarse_inverse, COARSE_TABLE
     )

time: 31.8 us -> 30.9 us (0.972)
  starting transfers between devices: 20.9 us -> 16.4 us
  waiting for transfers between devices: 2.19 us -> 6.15 us
    ppermute x1, starting transfers between devices: 4.55 us -> 0.09 us  [per_device(): u_near = lax.ppermute(u_near, 'tile', near_pairs)]
    ppermute x1, waiting for transfers between devices: 0.01 us -> 1.44 us  [per_device(): near = lax.ppermute(near, 'tile', near_pairs)]
    ppermute x1, waiting for transfers between devices: 0.01 us -> 1.4 us  [per_device(): u_near = lax.ppermute(u_near, 'tile', near_pairs)]
    ppermute x1, waiting for transfers between devices: 1.03 us -> 2.28 us  [per_device(): third = lax.ppermute(mixed, 'cuts', [(0, 3), (1, 2)])]
    ppermute x1, starting transfers between devices: 4.46 us -> 3.37 us  [per_device(): spill_far = lax.ppermute(spill_far, 'tile', far_pairs)]
    ppermute x1, starting transfers between devices: 3.21 us -> 4.3 us  [per_device(): u_far = lax.ppermute(u_far, 'tile', far_pairs)]
    pallas_call x4 -> x6, Pallas kernels: 5.36 us -> 5.09 us  [the longest x1 4.11 us: per_device(): call(fine_kernel, [True] * 5, [(f32(3, 4, BLOCKS, 40, LANES), False), (f3...]
  transfers between devices with their start and end apart: 8 -> 8, of which waited for: 2 -> 4; matrix products, arithmetic and copies ran while one was open for 0% -> 0% of each run, Pallas kernels for 8% -> 8%
where the time goes in v4:
time: 30.9 us; the launch traced here: 30.4 us
  starting transfers between devices  16.4 us (53%)
  Pallas kernels  7.67 us (25%)
  waiting for transfers between devices  6.15 us (20%)
    ppermute x1, starting transfers between devices, per_device(): u_far = lax.ppermute(u_far, 'tile', far_pairs)  4.3 us
    pallas_call x1, Pallas kernels, per_device(): call(fine_kernel, [True] * 5, [(f32(3, 4, BLOCKS, 40, LANES), False), (f3...  4.11 us
    ppermute x1, starting transfers between devices, per_device(): first = lax.ppermute(early, 'cuts', [(0, 1)])  3.82 us
    ppermute x1, starting transfers between devices, per_device(): spill_far = lax.ppermute(spill_far, 'tile', far_pairs)  3.37 us
    ppermute x1, starting transfers between devices, per_device(): second = lax.ppermute(two, 'cuts', [(0, 2), (1, 3)])  2.63 us
    ppermute x1, waiting for transfers between devices, per_device(): third = lax.ppermute(mixed, 'cuts', [(0, 3), (1, 2)])  2.28 us
    ppermute x1, starting transfers between devices, per_device(): third = lax.ppermute(mixed, 'cuts', [(0, 3), (1, 2)])  1.45 us
    ppermute x1, waiting for transfers between devices, per_device(): near = lax.ppermute(near, 'tile', near_pairs)  1.44 us
  transfers between devices with their start and end apart: 8, of which 4 were waited for; matrix products, arithmetic and copies ran while one was open for 0% of the time, Pallas kernels for 8%

profile of v4, /device:TPU:16, one launch (start us, length us, event | category | flops | bytes accessed | tf_op | source)
XLA Modules:
  0.0 30.4 jit_solution(11879840814400314831)
XLA Ops:
  0.0 4.1 %fine.1 = (f32[3,4,4,40,128]{4,3,2,1,0:T(8,128)S(1)}, f32[3,2,4,16,128]{4,3,2,1,0:T(8,128)S(1)}, f32[3,2,4,24,128]{4,3,2,1,0:T(8,128)S(1)}, f32[344,128]{1,0:T(8...) custom-call(f32[3,16,2048]{2,1,0:T(8,128)} %bitcast.2, ...), custom_call_target="tpu_custom_call" | custom-call | tf_op jit(solution)/shard_map/fine/pallas_call | solution.py:600
  4.1 0.1 collective-permute-start
  4.2 1.4 %collective-permute-done.near = f32[344,128]{1,0:T(8,128)S(1)} collective-permute-done((f32[344,128]{1,0:T(8,128)S(1)}, f32[344,128]{1,0:T(8,128)S(1)}, u32[]{:S(2)}, u32[]{:S(2)}) %collective-permute-start) | collective-permute-done | bytes 176160 | tf_op jit(solution)/shard_map/ppermute | solution.py:629
  5.6 4.3 %collective-permute-start.2 = (f32[344,128]{1,0:T(8,128)S(1)}, f32[344,128]{1,0:T(8,128)S(1)}, u32[]{:S(2)}, u32[]{:S(2)}) collective-permute-start(f32[344,128]{1,0:T(8,128)S(1)} %join.1.arrived), channel_id=1, source_target_pairs={{1,2},{2,1},{3,4},{4,3},{5,6},{6,5},{7,8},{8,7},{9,10},{10,9},{11,... | collective-permute-start | bytes 528392 | tf_op jit(solution)/shard_map/ppermute | solution.py:638
  9.9 0.2 spill.1
  10.1 3.4 %collective-permute-start.1 = (f32[408,128]{1,0:T(8,128)S(1)}, f32[408,128]{1,0:T(8,128)S(1)}, u32[]{:S(2)}, u32[]{:S(2)}) collective-permute-start(f32[408,128]{1,0:T(8,128)S(1)} %get-tuple-element.25), channel_id=1, source_target_pairs={{1,2},{2,1},{3,4},{4,3},{5,6},{6,5},{7,8},{8,7},{9,10},{10,9},{11,... | collective-permute-start | bytes 626696 | tf_op jit(solution)/shard_map/ppermute | solution.py:639
  13.5 1.0 %collective-permute-done.2.far = f32[344,128]{1,0:T(8,128)S(1)} collective-permute-done((f32[344,128]{1,0:T(8,128)S(1)}, f32[344,128]{1,0:T(8,128)S(1)}, u32[]{:S(2)}, u32[]{:S(2)}) %collective-permute-start.2) | collective-permute-done | bytes 176160 | tf_op jit(solution)/shard_map/ppermute | solution.py:638
  14.6 0.1 collective-permute-start.3
  14.6 0.0 copy-start.2
  14.7 0.1 assemble.1.assembled
  14.8 1.4 %collective-permute-done.3.cross.near = f32[552,128]{1,0:T(8,128)S(1)} collective-permute-done((f32[552,128]{1,0:T(8,128)S(1)}, f32[552,128]{1,0:T(8,128)S(1)}, u32[]{:S(2)}, u32[]{:S(2)}) %collective-permute-start.3) | collective-permute-done | bytes 282656 | tf_op jit(solution)/shard_map/ppermute | solution.py:641
  16.2 0.0 copy-done.2
  16.2 0.7 %first.1 = (f32[3,2,4,8,128]{4,3,2,1,0:T(8,128)S(1)}, f32[3,2,4,24,128]{4,3,2,1,0:T(8,128)S(1)}) custom-call(f32[3,2,4,48,128]{4,3,2,1,0:T(8,128)S(1)} %assemble.1.assembled, f32[552,128]{1,0:T(8,128)S(1)} %collective-permute-done.3.cross.near, bf16[2,512,512]{2,1,0:T(8,128)(2,1)S(1)} %get-tuple-element.28.inverse, f32[44,128]{1,0:T(8,128)S(1)} %copy-done.2), custom_call_target="tpu_custom_call" | custom-call | tf_op jit(solution)/shard_map/first/pallas_call | solution.py:656
  16.9 0.0 copy-start
  16.9 1.2 %rest.1 = (f32[3,2,4,8,128]{4,3,2,1,0:T(8,128)S(1)}, f32[3,2,4,8,128]{4,3,2,1,0:T(8,128)S(1)}, f32[3,2,4,8,128]{4,3,2,1,0:T(8,128)S(1)}, f32[3,2,4,8,128]{4,3,2,1,0:T(8,128)S(1)}) custom-call(f32[3,2,4,24,128]{4,3,2,1,0:T(8,128)S(1)} %get-tuple-element.29.wide, f32[3,2,4,8,128]{4,3,2,1,0:T(8,128)S(1)} %get-tuple-element.30.one, ...), custom_call_target="tpu_custom_call" | custom-call | tf_op jit(solution)/shard_map/rest/pallas_call | solution.py:659
  18.1 3.8 %collective-permute-start.4 = (f32[3,2,4,8,128]{4,3,2,1,0:T(8,128)S(1)}, f32[3,2,4,8,128]{4,3,2,1,0:T(8,128)S(1)}, u32[]{:S(2)}, u32[]{:S(2)}) collective-permute-start(f32[3,2,4,8,128]{4,3,2,1,0:T(8,128)S(1)} %get-tuple-element.31), channel_id=1, source_target_pairs={{0,32},{1,33},{2,34},{3,35},{4,36},{5,37},{6,38},{7,39},{8,40},{9,... | collective-permute-start | bytes 294920 | tf_op jit(solution)/shard_map/ppermute | solution.py:662
  21.9 2.6 %collective-permute-start.5 = (f32[3,2,4,8,128]{4,3,2,1,0:T(8,128)S(1)}, f32[3,2,4,8,128]{4,3,2,1,0:T(8,128)S(1)}, u32[]{:S(2)}, u32[]{:S(2)}) collective-permute-start(f32[3,2,4,8,128]{4,3,2,1,0:T(8,128)S(1)} %get-tuple-element.32), channel_id=1, source_target_pairs={{0,64},{32,96},{1,65},{33,97},{2,66},{34,98},{3,67},{35,99},{4,68}... | collective-permute-start | bytes 294920 | tf_op jit(solution)/shard_map/ppermute | solution.py:663
  24.5 1.4 %collective-permute-start.6 = (f32[3,2,4,8,128]{4,3,2,1,0:T(8,128)S(1)}, f32[3,2,4,8,128]{4,3,2,1,0:T(8,128)S(1)}, u32[]{:S(2)}, u32[]{:S(2)}) collective-permute-start(f32[3,2,4,8,128]{4,3,2,1,0:T(8,128)S(1)} %get-tuple-element.33), channel_id=1, source_target_pairs={{0,96},{32,64},{1,97},{33,65},{2,98},{34,66},{3,99},{35,67},{4,100... | collective-permute-start | bytes 294920 | tf_op jit(solution)/shard_map/ppermute | solution.py:664
  26.0 0.7 %collective-permute-start.7 = (f32[3,2,4,8,128]{4,3,2,1,0:T(8,128)S(1)}, f32[3,2,4,8,128]{4,3,2,1,0:T(8,128)S(1)}, u32[]{:S(2)}, u32[]{:S(2)}) collective-permute-start(f32[3,2,4,8,128]{4,3,2,1,0:T(8,128)S(1)} %get-tuple-element.34), channel_id=1, source_target_pairs={{64,96},{65,97},{66,98},{67,99},{68,100},{69,101},{70,102},{71,103... | collective-permute-start | bytes 294920 | tf_op jit(solution)/shard_map/ppermute | solution.py:665
  26.7 0.0 collective-permute-done.1.far
  26.7 0.0 collective-permute-done.4.first
  26.7 0.0 copy-done
  26.7 0.0 copy-start.1
  26.7 0.4 %natural.1.base_end = f32[3,16,2048]{2,1,0:T(8,128)S(1)} custom-call(f32[3,4,4,16,128]{4,3,2,1,0:T(8,128)S(1)} %get-tuple-element.24.own, f32[408,128]{1,0:T(8,128)S(1)} %collective-permute-done.1.far, f32[552,128]{1,0:T(8,128)S(1)} %collective-permute-done.3.cross.near, f32[3,2,4,8,128]{4,3,2,1,0:T(8,128)S(1)} %collective-permute-done.4.first, ...), custom_call_target="tpu_custom_call" | custom-call | tf_op jit(solution)/shard_map/natural/pallas_call | solution.py:666
  27.1 0.0 collective-permute-done.5.second
  27.1 2.3 %collective-permute-done.6.third = f32[3,2,4,8,128]{4,3,2,1,0:T(8,128)S(1)} collective-permute-done((f32[3,2,4,8,128]{4,3,2,1,0:T(8,128)S(1)}, f32[3,2,4,8,128]{4,3,2,1,0:T(8,128)S(1)}, u32[]{:S(2)}, u32[]{:S(2)}) %collective-permute-start.6) | collective-permute-done | bytes 98336 | tf_op jit(solution)/shard_map/ppermute | solution.py:664
  29.4 0.0 collective-permute-done.7.fourth
  29.4 0.0 copy-done.1
  29.4 1.0 %final.1 = f32[3,16,2048]{2,1,0:T(8,128)} custom-call(f32[3,16,2048]{2,1,0:T(8,128)S(1)} %natural.1.base_end, f32[3,2,4,8,128]{4,3,2,1,0:T(8,128)S(1)} %collective-permute-done.5.second, f32[3,2,4,8,128]{4,3,2,1,0:T(8,128)S(1)} %collective-permute-done.6.third, f32[3,2,4,8,128]{4,3,2,1,0:T(8,128)S(1)} %collective-permute-done.7.fourth, ...), custom_call_target="tpu_custom_call" | custom-call | tf_op jit(solution)/shard_map/final/pallas_call | solution.py:673
  (2 shorter events, 0.1 us)
Async XLA Ops:
  4.1 1.5 %collective-permute-start = (f32[344,128]{1,0:T(8,128)S(1)}, f32[344,128]{1,0:T(8,128)S(1)}, u32[]{:S(2)}, u32[]{:S(2)}) collective-permute-start(f32[344,128]{1,0:T(8,128)S(1)} %get-tuple-element.23), channel_id=1, source_target_pairs={{0,1},{1,0},{2,3},{3,2},{4,5},{5,4},{6,7},{7,6},{8,9},{9,8},{10,11... | collective-permute-start | bytes 528392 | tf_op jit(solution)/shard_map/ppermute | solution.py:629
  5.6 8.9 %collective-permute-start.2 = (f32[344,128]{1,0:T(8,128)S(1)}, f32[344,128]{1,0:T(8,128)S(1)}, u32[]{:S(2)}, u32[]{:S(2)}) collective-permute-start(f32[344,128]{1,0:T(8,128)S(1)} %join.1.arrived), channel_id=1, source_target_pairs={{1,2},{2,1},{3,4},{4,3},{5,6},{6,5},{7,8},{8,7},{9,10},{10,9},{11,... | collective-permute-start | bytes 528392 | tf_op jit(solution)/shard_map/ppermute | solution.py:638
  10.1 16.6 %collective-permute-start.1 = (f32[408,128]{1,0:T(8,128)S(1)}, f32[408,128]{1,0:T(8,128)S(1)}, u32[]{:S(2)}, u32[]{:S(2)}) collective-permute-start(f32[408,128]{1,0:T(8,128)S(1)} %get-tuple-element.25), channel_id=1, source_target_pairs={{1,2},{2,1},{3,4},{4,3},{5,6},{6,5},{7,8},{8,7},{9,10},{10,9},{11,... | collective-permute-start | bytes 626696 | tf_op jit(solution)/shard_map/ppermute | solution.py:639
  14.6 1.6 %collective-permute-start.3 = (f32[552,128]{1,0:T(8,128)S(1)}, f32[552,128]{1,0:T(8,128)S(1)}, u32[]{:S(2)}, u32[]{:S(2)}) collective-permute-start(f32[552,128]{1,0:T(8,128)S(1)} %forward.1), channel_id=1, source_target_pairs={{0,1},{1,0},{2,3},{3,2},{4,5},{5,4},{6,7},{7,6},{8,9},{9,8},{10,11... | collective-permute-start | bytes 847880 | tf_op jit(solution)/shard_map/ppermute | solution.py:641
  14.6 1.6 %copy-start.2 = (f32[44,128]{1,0:T(8,128)S(1)}, f32[44,128]{1,0:T(8,128)}, u32[]{:S(2)}) copy-start(f32[44,128]{1,0:T(8,128)} %constant.15.clone.coarse_table_hbm.table) | copy-start | bytes 67588
  16.9 9.8 %copy-start = (bf16[512,512]{1,0:T(8,128)(2,1)S(1)}, bf16[512,512]{1,0:T(8,128)(2,1)}, u32[]{:S(2)}) copy-start(bf16[512,512]{1,0:T(8,128)(2,1)} %constant.16.clone.matrix) | copy-start | bytes 1572868
  18.1 8.6 %collective-permute-start.4 = (f32[3,2,4,8,128]{4,3,2,1,0:T(8,128)S(1)}, f32[3,2,4,8,128]{4,3,2,1,0:T(8,128)S(1)}, u32[]{:S(2)}, u32[]{:S(2)}) collective-permute-start(f32[3,2,4,8,128]{4,3,2,1,0:T(8,128)S(1)} %get-tuple-element.31), channel_id=1, source_target_pairs={{0,32},{1,33},{2,34},{3,35},{4,36},{5,37},{6,38},{7,39},{8,40},{9,... | collective-permute-start | bytes 294920 | tf_op jit(solution)/shard_map/ppermute | solution.py:662
  21.9 5.2 %collective-permute-start.5 = (f32[3,2,4,8,128]{4,3,2,1,0:T(8,128)S(1)}, f32[3,2,4,8,128]{4,3,2,1,0:T(8,128)S(1)}, u32[]{:S(2)}, u32[]{:S(2)}) collective-permute-start(f32[3,2,4,8,128]{4,3,2,1,0:T(8,128)S(1)} %get-tuple-element.32), channel_id=1, source_target_pairs={{0,64},{32,96},{1,65},{33,97},{2,66},{34,98},{3,67},{35,99},{4,68}... | collective-permute-start | bytes 294920 | tf_op jit(solution)/shard_map/ppermute | solution.py:663
  24.5 4.9 %collective-permute-start.6 = (f32[3,2,4,8,128]{4,3,2,1,0:T(8,128)S(1)}, f32[3,2,4,8,128]{4,3,2,1,0:T(8,128)S(1)}, u32[]{:S(2)}, u32[]{:S(2)}) collective-permute-start(f32[3,2,4,8,128]{4,3,2,1,0:T(8,128)S(1)} %get-tuple-element.33), channel_id=1, source_target_pairs={{0,96},{32,64},{1,97},{33,65},{2,98},{34,66},{3,99},{35,67},{4,100... | collective-permute-start | bytes 294920 | tf_op jit(solution)/shard_map/ppermute | solution.py:664
  26.0 3.4 %collective-permute-start.7 = (f32[3,2,4,8,128]{4,3,2,1,0:T(8,128)S(1)}, f32[3,2,4,8,128]{4,3,2,1,0:T(8,128)S(1)}, u32[]{:S(2)}, u32[]{:S(2)}) collective-permute-start(f32[3,2,4,8,128]{4,3,2,1,0:T(8,128)S(1)} %get-tuple-element.34), channel_id=1, source_target_pairs={{64,96},{65,97},{66,98},{67,99},{68,100},{69,101},{70,102},{71,103... | collective-permute-start | bytes 294920 | tf_op jit(solution)/shard_map/ppermute | solution.py:665
  26.7 2.7 %copy-start.1 = (bf16[256,512]{1,0:T(8,128)(2,1)S(1)}, bf16[256,512]{1,0:T(8,128)(2,1)}, u32[]{:S(2)}) copy-start(bf16[256,512]{1,0:T(8,128)(2,1)} %constant.17.clone.matrix) | copy-start | bytes 786436

commit v5 on v4

--- a/solution.py
+++ b/solution.py
@@ -463,39 +463,51 @@
 
 def first_kernel(assembled, cross, inverse, table, one, wide, height, height_new, flux, diff):
     odd = on_odd()
-    for n, (c, p, a) in enumerate(planes(2)):
-        to = height.at[p, a] if c == 0 else flux.at[c - 1, p, a]
-        beyond = cross[n * 6 : n * 6 + 6, :]
-        to[0:40, :] = assembled[c, p, a, 0:40, :]
-        to[7:13, :] = to[7:13, :] + jnp.where(odd, beyond, 0.0)
-        to[27:33, :] = to[27:33, :] + jnp.where(odd, 0.0, beyond)
-    window = (8, 24)
-    wave_step(
-        2, COARSE_NAMES, table, inverse, COARSE_RATIO, height, height_new, flux, diff,
-        (window, window, (window, window)), *at_tile(ROWS // 2, 16),
-    )
+
+    @pl.when(lax.axis_index("cuts") < lax.axis_size("cuts") - 1)
+    def _():
+        for n, (c, p, a) in enumerate(planes(2)):
+            to = height.at[p, a] if c == 0 else flux.at[c - 1, p, a]
+            beyond = cross[n * 6 : n * 6 + 6, :]
+            to[0:40, :] = assembled[c, p, a, 0:40, :]
+            to[7:13, :] = to[7:13, :] + jnp.where(odd, beyond, 0.0)
+            to[27:33, :] = to[27:33, :] + jnp.where(odd, 0.0, beyond)
+        window = (8, 24)
+        wave_step(
+            2, COARSE_NAMES, table, inverse, COARSE_RATIO, height, height_new, flux, diff,
+            (window, window, (window, window)), *at_tile(ROWS // 2, 16),
+        )
+        for c, p, a in planes(2):
+            result = height_new.at[p, a] if c == 0 else flux.at[c - 1, p, a]
+            one[c, p, a] = result[16:24, :]
+            wide[c, p, a] = result[8:32, :]
+
+
+def rest_kernel(wide, one, inverse, table, early, two, three, last, height, height_new, flux, diff):
+    cut = lax.axis_index("cuts")
+    arguments = (2, COARSE_NAMES, table, inverse, COARSE_RATIO)
     for c, p, a in planes(2):
-        result = height_new.at[p, a] if c == 0 else flux.at[c - 1, p, a]
-        one[c, p, a] = result[16:24, :]
-        wide[c, p, a] = result[8:32, :]
-
-
-def rest_kernel(wide, one, inverse, table, early, two, mixed, last, height, height_new, flux, diff):
-    for c, p, a in planes(2):
-        to = height.at[p, a] if c == 0 else flux.at[c - 1, p, a]
-        to[8:32, :] = wide[c, p, a]
-    arguments = (2, COARSE_NAMES, table, inverse, COARSE_RATIO)
-    wave_step(*arguments, height, height_new, flux, diff, ((8, 24), (12, 16), ((12, 16), (12, 16))), *at_tile(ROWS // 2, 16))
-    for c, p, a in planes(2):
-        result = height_new.at[p, a] if c == 0 else flux.at[c - 1, p, a]
-        two[c, p, a] = result[16:24, :]
-    wave_step(*arguments, height_new, height, flux, diff, ((12, 16), (12, 16), ((16, 8), (16, 8))), *at_tile(ROWS // 2, 16))
-    start = lax.axis_index("cuts") == 0
-    for c, p, a in planes(2):
-        result = height.at[p, a] if c == 0 else flux.at[c - 1, p, a]
-        mixed[c, p, a] = jnp.where(start, result[16:24, :], one[c, p, a])
+        early[c, p, a] = one[c, p, a]
         last[c, p, a] = one[c, p, a]
-        early[c, p, a] = one[c, p, a]
+
+    @pl.when(cut < 2)
+    def _():
+        for c, p, a in planes(2):
+            to = height.at[p, a] if c == 0 else flux.at[c - 1, p, a]
+            to[8:32, :] = wide[c, p, a]
+        windows = ((8, 24), (12, 16), ((12, 16), (12, 16)))
+        wave_step(*arguments, height, height_new, flux, diff, windows, *at_tile(ROWS // 2, 16))
+        for c, p, a in planes(2):
+            result = height_new.at[p, a] if c == 0 else flux.at[c - 1, p, a]
+            two[c, p, a] = result[16:24, :]
+
+    @pl.when(cut == 0)
+    def _():
+        windows = ((12, 16), (12, 16), ((16, 8), (16, 8)))
+        wave_step(*arguments, height_new, height, flux, diff, windows, *at_tile(ROWS // 2, 16))
+        for c, p, a in planes(2):
+            result = height.at[p, a] if c == 0 else flux.at[c - 1, p, a]
+            three[c, p, a] = result[16:24, :]
 
 
 def natural_kernel(own, far, near, first, matrix, out, rows, total):
@@ -626,6 +638,11 @@
         ],
         name="fine",
     )(*[in_hbm(array) for array in fetched])
+    senders = range(lax.axis_size("cuts") - 1)
+
+    def of_senders(pairs):
+        return [(k * tiles + i, k * tiles + j) for k in senders for i, j in pairs]
+
     u_near = lax.ppermute(u_near, "tile", near_pairs)
     (u_far,) = call(join_kernel, [False] * 2, [far_rows], name="join")(u_far, u_near)
     own, spill_far, spill_near = call(
@@ -635,7 +652,7 @@
         [scratch(3, 2, BLOCKS, 32, LANES)],
         name="spill",
     )(wide_end, propagated, u_far)
-    u_far = lax.ppermute(u_far, "tile", far_pairs)
+    u_far = lax.ppermute(u_far, ("cuts", "tile"), of_senders(far_pairs))
     spill_far = lax.ppermute(spill_far, "tile", far_pairs)
     (near,) = call(forward_kernel, [False] * 2, [last_rows], name="forward")(u_far, spill_near)
     near = lax.ppermute(near, "tile", near_pairs)
@@ -656,12 +673,12 @@
     one, wide = call(
         first_kernel, [False] * 4, [coarse, (f32(3, 2, BLOCKS, 24, LANES), False)], state, name="first"
     )(assembled, near, coarse_inverse, COARSE_TABLE)
-    early, two, mixed, last = call(rest_kernel, [False] * 4, [coarse] * 4, state, name="rest")(
+    early, two, three, last = call(rest_kernel, [False] * 4, [coarse] * 4, state, name="rest")(
         wide, one, coarse_inverse, COARSE_TABLE
     )
-    first = lax.ppermute(early, "cuts", [(0, 1)])
+    first = lax.ppermute(early, "cuts", [(0, 1), (1, 2)])
     second = lax.ppermute(two, "cuts", [(0, 2), (1, 3)])
-    third = lax.ppermute(mixed, "cuts", [(0, 3), (1, 2)])
+    third = lax.ppermute(three, "cuts", [(0, 3)])
     fourth = lax.ppermute(last, "cuts", [(2, 3)])
     (natural,) = call(
         natural_kernel,
@@ -676,7 +693,7 @@
         [(f32(3, ROWS, NX), True)],
         [scratch(3, 16, ROWS, LANES), scratch(3, ROWS, NX), dma((BLOCKS,))],
         name="final",
-    )(natural, second, third, fourth, SPREAD)
+    )(natural, third, second, fourth, SPREAD)
     return out[None]
 
 

time: 30.9 us -> 28.5 us (0.922)
  starting transfers between devices: 16.4 us -> 15.2 us
  waiting for transfers between devices: 6.15 us -> 5.06 us
    ppermute x3, waiting for transfers between devices: 3.31 us -> 2.2 us  [the longest x1 1.17 us: per_device(): third = lax.ppermute(three, 'cuts', [(0, 3)])]
    ppermute x3, starting transfers between devices: 9.57 us -> 8.84 us  [the longest x1 4.3 us: per_device(): u_far = lax.ppermute(u_far, ('cuts', 'tile'), of_senders(far_pairs))]
    ppermute x1, starting transfers between devices: 2.63 us -> 2.15 us  [per_device(): second = lax.ppermute(two, 'cuts', [(0, 2), (1, 3)])]
  transfers between devices with their start and end apart: 8 -> 8, of which waited for: 4 -> 4; matrix products, arithmetic and copies ran while one was open for 0% -> 0% of each run, Pallas kernels for 8% -> 9%
where the time goes in v5:
time: 28.5 us; the launch traced here: 28.1 us
  starting transfers between devices  15.2 us (53%)
  Pallas kernels  7.7 us (27%)
  waiting for transfers between devices  5.06 us (18%)
    ppermute x1, starting transfers between devices, per_device(): u_far = lax.ppermute(u_far, ('cuts', 'tile'), of_senders(far_pairs))  4.3 us
    pallas_call x1, Pallas kernels, per_device(): call(fine_kernel, [True] * 5, [(f32(3, 4, BLOCKS, 40, LANES), False), (f3...  4.11 us
    ppermute x1, starting transfers between devices, per_device(): spill_far = lax.ppermute(spill_far, 'tile', far_pairs)  3.37 us
    ppermute x1, starting transfers between devices, per_device(): first = lax.ppermute(early, 'cuts', [(0, 1), (1, 2)])  3.24 us
    ppermute x1, starting transfers between devices, per_device(): second = lax.ppermute(two, 'cuts', [(0, 2), (1, 3)])  2.15 us
    ppermute x1, waiting for transfers between devices, per_device(): near = lax.ppermute(near, 'tile', near_pairs)  1.44 us
    ppermute x1, waiting for transfers between devices, per_device(): u_near = lax.ppermute(u_near, 'tile', near_pairs)  1.4 us
    ppermute x1, starting transfers between devices, per_device(): third = lax.ppermute(three, 'cuts', [(0, 3)])  1.3 us
  transfers between devices with their start and end apart: 8, of which 4 were waited for; matrix products, arithmetic and copies ran while one was open for 0% of the time, Pallas kernels for 9%

profile of v5, /device:TPU:16, one launch (start us, length us, event | category | flops | bytes accessed | tf_op | source)
XLA Modules:
  0.0 28.1 jit_solution(13332472818093632370)
XLA Ops:
  0.0 4.1 %fine.1 = (f32[3,4,4,40,128]{4,3,2,1,0:T(8,128)S(1)}, f32[3,2,4,16,128]{4,3,2,1,0:T(8,128)S(1)}, f32[3,2,4,24,128]{4,3,2,1,0:T(8,128)S(1)}, f32[344,128]{1,0:T(8...) custom-call(f32[3,16,2048]{2,1,0:T(8,128)} %bitcast.2, ...), custom_call_target="tpu_custom_call" | custom-call | tf_op jit(solution)/shard_map/fine/pallas_call | solution.py:612
  4.1 0.1 collective-permute-start
  4.2 1.4 %collective-permute-done.near = f32[344,128]{1,0:T(8,128)S(1)} collective-permute-done((f32[344,128]{1,0:T(8,128)S(1)}, f32[344,128]{1,0:T(8,128)S(1)}, u32[]{:S(2)}, u32[]{:S(2)}) %collective-permute-start) | collective-permute-done | bytes 176160 | tf_op jit(solution)/shard_map/ppermute | solution.py:646
  5.6 4.3 %collective-permute-start.2 = (f32[344,128]{1,0:T(8,128)S(1)}, f32[344,128]{1,0:T(8,128)S(1)}, u32[]{:S(2)}, u32[]{:S(2)}) collective-permute-start(f32[344,128]{1,0:T(8,128)S(1)} %join.1.arrived), channel_id=1, source_target_pairs={{1,2},{2,1},{3,4},{4,3},{5,6},{6,5},{7,8},{8,7},{9,10},{10,9},{11,... | collective-permute-start | bytes 528392 | tf_op jit(solution)/shard_map/ppermute | solution.py:655
  9.9 0.2 spill.1
  10.1 3.4 %collective-permute-start.1 = (f32[408,128]{1,0:T(8,128)S(1)}, f32[408,128]{1,0:T(8,128)S(1)}, u32[]{:S(2)}, u32[]{:S(2)}) collective-permute-start(f32[408,128]{1,0:T(8,128)S(1)} %get-tuple-element.25), channel_id=1, source_target_pairs={{1,2},{2,1},{3,4},{4,3},{5,6},{6,5},{7,8},{8,7},{9,10},{10,9},{11,... | collective-permute-start | bytes 626696 | tf_op jit(solution)/shard_map/ppermute | solution.py:656
  13.5 1.0 %collective-permute-done.2.far = f32[344,128]{1,0:T(8,128)S(1)} collective-permute-done((f32[344,128]{1,0:T(8,128)S(1)}, f32[344,128]{1,0:T(8,128)S(1)}, u32[]{:S(2)}, u32[]{:S(2)}) %collective-permute-start.2) | collective-permute-done | bytes 176160 | tf_op jit(solution)/shard_map/ppermute | solution.py:655
  14.6 0.1 collective-permute-start.3
  14.6 0.0 copy-start.2
  14.7 0.1 assemble.1.assembled
  14.8 1.4 %collective-permute-done.3.cross.near = f32[552,128]{1,0:T(8,128)S(1)} collective-permute-done((f32[552,128]{1,0:T(8,128)S(1)}, f32[552,128]{1,0:T(8,128)S(1)}, u32[]{:S(2)}, u32[]{:S(2)}) %collective-permute-start.3) | collective-permute-done | bytes 282656 | tf_op jit(solution)/shard_map/ppermute | solution.py:658
  16.2 0.0 copy-done.2
  16.2 0.7 %first.1 = (f32[3,2,4,8,128]{4,3,2,1,0:T(8,128)S(1)}, f32[3,2,4,24,128]{4,3,2,1,0:T(8,128)S(1)}) custom-call(f32[3,2,4,48,128]{4,3,2,1,0:T(8,128)S(1)} %assemble.1.assembled, f32[552,128]{1,0:T(8,128)S(1)} %collective-permute-done.3.cross.near, bf16[2,512,512]{2,1,0:T(8,128)(2,1)S(1)} %get-tuple-element.28.inverse, f32[44,128]{1,0:T(8,128)S(1)} %copy-done.2), custom_call_target="tpu_custom_call" | custom-call | tf_op jit(solution)/shard_map/first/pallas_call | solution.py:673
  16.9 0.0 copy-start
  16.9 1.2 %rest.1 = (f32[3,2,4,8,128]{4,3,2,1,0:T(8,128)S(1)}, f32[3,2,4,8,128]{4,3,2,1,0:T(8,128)S(1)}, f32[3,2,4,8,128]{4,3,2,1,0:T(8,128)S(1)}, f32[3,2,4,8,128]{4,3,2,1,0:T(8,128)S(1)}) custom-call(f32[3,2,4,24,128]{4,3,2,1,0:T(8,128)S(1)} %get-tuple-element.29.wide, f32[3,2,4,8,128]{4,3,2,1,0:T(8,128)S(1)} %get-tuple-element.30.one, ...), custom_call_target="tpu_custom_call" | custom-call | tf_op jit(solution)/shard_map/rest/pallas_call | solution.py:676
  18.1 3.2 %collective-permute-start.4 = (f32[3,2,4,8,128]{4,3,2,1,0:T(8,128)S(1)}, f32[3,2,4,8,128]{4,3,2,1,0:T(8,128)S(1)}, u32[]{:S(2)}, u32[]{:S(2)}) collective-permute-start(f32[3,2,4,8,128]{4,3,2,1,0:T(8,128)S(1)} %get-tuple-element.31), channel_id=1, source_target_pairs={{0,32},{32,64},{1,33},{33,65},{2,34},{34,66},{3,35},{35,67},{4,36}... | collective-permute-start | bytes 294920 | tf_op jit(solution)/shard_map/ppermute | solution.py:679
  21.3 1.3 %collective-permute-start.5 = (f32[3,2,4,8,128]{4,3,2,1,0:T(8,128)S(1)}, f32[3,2,4,8,128]{4,3,2,1,0:T(8,128)S(1)}, u32[]{:S(2)}, u32[]{:S(2)}) collective-permute-start(f32[3,2,4,8,128]{4,3,2,1,0:T(8,128)S(1)} %get-tuple-element.32), channel_id=1, source_target_pairs={{0,96},{1,97},{2,98},{3,99},{4,100},{5,101},{6,102},{7,103},{8,104... | collective-permute-start | bytes 294920 | tf_op jit(solution)/shard_map/ppermute | solution.py:681
  22.6 2.2 %collective-permute-start.6 = (f32[3,2,4,8,128]{4,3,2,1,0:T(8,128)S(1)}, f32[3,2,4,8,128]{4,3,2,1,0:T(8,128)S(1)}, u32[]{:S(2)}, u32[]{:S(2)}) collective-permute-start(f32[3,2,4,8,128]{4,3,2,1,0:T(8,128)S(1)} %get-tuple-element.33), channel_id=1, source_target_pairs={{0,64},{32,96},{1,65},{33,97},{2,66},{34,98},{3,67},{35,99},{4,68}... | collective-permute-start | bytes 294920 | tf_op jit(solution)/shard_map/ppermute | solution.py:680
  24.8 0.7 %collective-permute-start.7 = (f32[3,2,4,8,128]{4,3,2,1,0:T(8,128)S(1)}, f32[3,2,4,8,128]{4,3,2,1,0:T(8,128)S(1)}, u32[]{:S(2)}, u32[]{:S(2)}) collective-permute-start(f32[3,2,4,8,128]{4,3,2,1,0:T(8,128)S(1)} %get-tuple-element.34), channel_id=1, source_target_pairs={{64,96},{65,97},{66,98},{67,99},{68,100},{69,101},{70,102},{71,103... | collective-permute-start | bytes 294920 | tf_op jit(solution)/shard_map/ppermute | solution.py:682
  25.5 0.0 collective-permute-done.1.far
  25.5 0.0 collective-permute-done.4.first
  25.5 0.0 copy-done
  25.5 0.0 copy-start.1
  25.5 0.4 %natural.1.base_end = f32[3,16,2048]{2,1,0:T(8,128)S(1)} custom-call(f32[3,4,4,16,128]{4,3,2,1,0:T(8,128)S(1)} %get-tuple-element.24.own, f32[408,128]{1,0:T(8,128)S(1)} %collective-permute-done.1.far, f32[552,128]{1,0:T(8,128)S(1)} %collective-permute-done.3.cross.near, f32[3,2,4,8,128]{4,3,2,1,0:T(8,128)S(1)} %collective-permute-done.4.first, ...), custom_call_target="tpu_custom_call" | custom-call | tf_op jit(solution)/shard_map/natural/pallas_call | solution.py:683
  26.0 1.2 %collective-permute-done.5.second = f32[3,2,4,8,128]{4,3,2,1,0:T(8,128)S(1)} collective-permute-done((f32[3,2,4,8,128]{4,3,2,1,0:T(8,128)S(1)}, f32[3,2,4,8,128]{4,3,2,1,0:T(8,128)S(1)}, u32[]{:S(2)}, u32[]{:S(2)}) %collective-permute-start.5) | collective-permute-done | bytes 98336 | tf_op jit(solution)/shard_map/ppermute | solution.py:681
  27.1 0.0 collective-permute-done.6.third
  27.1 0.0 collective-permute-done.7.fourth
  27.1 0.0 copy-done.1
  27.1 1.0 %final.1 = f32[3,16,2048]{2,1,0:T(8,128)} custom-call(f32[3,16,2048]{2,1,0:T(8,128)S(1)} %natural.1.base_end, f32[3,2,4,8,128]{4,3,2,1,0:T(8,128)S(1)} %collective-permute-done.5.second, f32[3,2,4,8,128]{4,3,2,1,0:T(8,128)S(1)} %collective-permute-done.6.third, f32[3,2,4,8,128]{4,3,2,1,0:T(8,128)S(1)} %collective-permute-done.7.fourth, ...), custom_call_target="tpu_custom_call" | custom-call | tf_op jit(solution)/shard_map/final/pallas_call | solution.py:690
  (2 shorter events, 0.1 us)
Async XLA Ops:
  4.1 1.5 %collective-permute-start = (f32[344,128]{1,0:T(8,128)S(1)}, f32[344,128]{1,0:T(8,128)S(1)}, u32[]{:S(2)}, u32[]{:S(2)}) collective-permute-start(f32[344,128]{1,0:T(8,128)S(1)} %get-tuple-element.23), channel_id=1, source_target_pairs={{0,1},{1,0},{2,3},{3,2},{4,5},{5,4},{6,7},{7,6},{8,9},{9,8},{10,11... | collective-permute-start | bytes 528392 | tf_op jit(solution)/shard_map/ppermute | solution.py:646
  5.6 8.9 %collective-permute-start.2 = (f32[344,128]{1,0:T(8,128)S(1)}, f32[344,128]{1,0:T(8,128)S(1)}, u32[]{:S(2)}, u32[]{:S(2)}) collective-permute-start(f32[344,128]{1,0:T(8,128)S(1)} %join.1.arrived), channel_id=1, source_target_pairs={{1,2},{2,1},{3,4},{4,3},{5,6},{6,5},{7,8},{8,7},{9,10},{10,9},{11,... | collective-permute-start | bytes 528392 | tf_op jit(solution)/shard_map/ppermute | solution.py:655
  10.1 15.4 %collective-permute-start.1 = (f32[408,128]{1,0:T(8,128)S(1)}, f32[408,128]{1,0:T(8,128)S(1)}, u32[]{:S(2)}, u32[]{:S(2)}) collective-permute-start(f32[408,128]{1,0:T(8,128)S(1)} %get-tuple-element.25), channel_id=1, source_target_pairs={{1,2},{2,1},{3,4},{4,3},{5,6},{6,5},{7,8},{8,7},{9,10},{10,9},{11,... | collective-permute-start | bytes 626696 | tf_op jit(solution)/shard_map/ppermute | solution.py:656
  14.6 1.6 %collective-permute-start.3 = (f32[552,128]{1,0:T(8,128)S(1)}, f32[552,128]{1,0:T(8,128)S(1)}, u32[]{:S(2)}, u32[]{:S(2)}) collective-permute-start(f32[552,128]{1,0:T(8,128)S(1)} %forward.1), channel_id=1, source_target_pairs={{0,1},{1,0},{2,3},{3,2},{4,5},{5,4},{6,7},{7,6},{8,9},{9,8},{10,11... | collective-permute-start | bytes 847880 | tf_op jit(solution)/shard_map/ppermute | solution.py:658
  14.6 1.6 %copy-start.2 = (f32[44,128]{1,0:T(8,128)S(1)}, f32[44,128]{1,0:T(8,128)}, u32[]{:S(2)}) copy-start(f32[44,128]{1,0:T(8,128)} %constant.15.clone.coarse_table_hbm.table) | copy-start | bytes 67588
  16.9 8.6 %copy-start = (bf16[512,512]{1,0:T(8,128)(2,1)S(1)}, bf16[512,512]{1,0:T(8,128)(2,1)}, u32[]{:S(2)}) copy-start(bf16[512,512]{1,0:T(8,128)(2,1)} %constant.16.clone.matrix) | copy-start | bytes 1572868
  18.1 7.4 %collective-permute-start.4 = (f32[3,2,4,8,128]{4,3,2,1,0:T(8,128)S(1)}, f32[3,2,4,8,128]{4,3,2,1,0:T(8,128)S(1)}, u32[]{:S(2)}, u32[]{:S(2)}) collective-permute-start(f32[3,2,4,8,128]{4,3,2,1,0:T(8,128)S(1)} %get-tuple-element.31), channel_id=1, source_target_pairs={{0,32},{32,64},{1,33},{33,65},{2,34},{34,66},{3,35},{35,67},{4,36}... | collective-permute-start | bytes 294920 | tf_op jit(solution)/shard_map/ppermute | solution.py:679
  21.3 5.8 %collective-permute-start.5 = (f32[3,2,4,8,128]{4,3,2,1,0:T(8,128)S(1)}, f32[3,2,4,8,128]{4,3,2,1,0:T(8,128)S(1)}, u32[]{:S(2)}, u32[]{:S(2)}) collective-permute-start(f32[3,2,4,8,128]{4,3,2,1,0:T(8,128)S(1)} %get-tuple-element.32), channel_id=1, source_target_pairs={{0,96},{1,97},{2,98},{3,99},{4,100},{5,101},{6,102},{7,103},{8,104... | collective-permute-start | bytes 294920 | tf_op jit(solution)/shard_map/ppermute | solution.py:681
  22.6 4.5 %collective-permute-start.6 = (f32[3,2,4,8,128]{4,3,2,1,0:T(8,128)S(1)}, f32[3,2,4,8,128]{4,3,2,1,0:T(8,128)S(1)}, u32[]{:S(2)}, u32[]{:S(2)}) collective-permute-start(f32[3,2,4,8,128]{4,3,2,1,0:T(8,128)S(1)} %get-tuple-element.33), channel_id=1, source_target_pairs={{0,64},{32,96},{1,65},{33,97},{2,66},{34,98},{3,67},{35,99},{4,68}... | collective-permute-start | bytes 294920 | tf_op jit(solution)/shard_map/ppermute | solution.py:680
  24.8 2.3 %collective-permute-start.7 = (f32[3,2,4,8,128]{4,3,2,1,0:T(8,128)S(1)}, f32[3,2,4,8,128]{4,3,2,1,0:T(8,128)S(1)}, u32[]{:S(2)}, u32[]{:S(2)}) collective-permute-start(f32[3,2,4,8,128]{4,3,2,1,0:T(8,128)S(1)} %get-tuple-element.34), channel_id=1, source_target_pairs={{64,96},{65,97},{66,98},{67,99},{68,100},{69,101},{70,102},{71,103... | collective-permute-start | bytes 294920 | tf_op jit(solution)/shard_map/ppermute | solution.py:682
  25.5 1.6 %copy-start.1 = (bf16[256,512]{1,0:T(8,128)(2,1)S(1)}, bf16[256,512]{1,0:T(8,128)(2,1)}, u32[]{:S(2)}) copy-start(bf16[256,512]{1,0:T(8,128)(2,1)} %constant.17.clone.matrix) | copy-start | bytes 786436

commit v6 on v5

--- a/solution.py
+++ b/solution.py
@@ -439,13 +439,12 @@
             out[base + 8 : base + 14, :] = own[base + 8 : base + 14, :] + near[base : base + 6, :]
 
 
-def forward_kernel(far, rows, out):
+def forward_kernel(far, out):
     odd = on_odd()
     for n in range(24):
         low = far[n * 14 : n * 14 + 6, :]
         high = far[n * 14 + 8 : n * 14 + 14, :]
         out[n * 6 : n * 6 + 6, :] = jnp.where(odd, low, high)
-    out[NEXT_ROWS : NEXT_ROWS + 16 * SPILL_ROWS, :] = rows[0 : 16 * SPILL_ROWS, :]
 
 
 def assemble_kernel(own, far, near, out):
@@ -519,7 +518,7 @@
         start, count = SPILL[c]
         base = (p * BLOCKS + a) * SPILL_ROWS + start
         distant = far[base : base + count, :]
-        close = near[NEXT_ROWS + base : NEXT_ROWS + base + count, :]
+        close = near[base : base + count, :]
         to = total.at[c, p, a]
         to[0:ROWS, :] = own[c, p, a] + rows[c, p // 2, a]
         to[0:count, :] = to[0:count, :] + jnp.where(odd, close, distant)
@@ -607,7 +606,7 @@
     coarse = (f32(3, 2, BLOCKS, 8, LANES), False)
     spilt = (f32(16 * SPILL_ROWS + SPARE, LANES), False)
     far_rows = (f32(FAR_ROWS + SPARE, LANES), False)
-    last_rows = (f32(NEXT_ROWS + 16 * SPILL_ROWS + SPARE, LANES), False)
+    last_rows = (f32(NEXT_ROWS + SPARE, LANES), False)
     fetched = (start_states[0], FINE_INVERSE, FINE_TABLE, COARSE_INVERSE, COARSE_TABLE)
     wide_end, propagated, u_wide, u_far, u_near, coarse_inverse = call(
         fine_kernel,
@@ -654,8 +653,9 @@
     )(wide_end, propagated, u_far)
     u_far = lax.ppermute(u_far, ("cuts", "tile"), of_senders(far_pairs))
     spill_far = lax.ppermute(spill_far, "tile", far_pairs)
-    (near,) = call(forward_kernel, [False] * 2, [last_rows], name="forward")(u_far, spill_near)
-    near = lax.ppermute(near, "tile", near_pairs)
+    spill_near = lax.ppermute(spill_near, "tile", near_pairs)
+    (cross,) = call(forward_kernel, [False], [last_rows], name="forward")(u_far)
+    cross = lax.ppermute(cross, "tile", near_pairs)
 
     state = [
         scratch(2, BLOCKS, 48, LANES),
@@ -672,7 +672,7 @@
     )(u_wide, u_far, u_near)
     one, wide = call(
         first_kernel, [False] * 4, [coarse, (f32(3, 2, BLOCKS, 24, LANES), False)], state, name="first"
-    )(assembled, near, coarse_inverse, COARSE_TABLE)
+    )(assembled, cross, coarse_inverse, COARSE_TABLE)
     early, two, three, last = call(rest_kernel, [False] * 4, [coarse] * 4, state, name="rest")(
         wide, one, coarse_inverse, COARSE_TABLE
     )
@@ -686,7 +686,7 @@
         [(f32(3, ROWS, NX), False)],
         [scratch(3, 2, BLOCKS, ROWS, LANES), scratch(3, 4, BLOCKS, ROWS + SPARE, LANES)],
         name="natural",
-    )(own, spill_far, near, first, NATURAL)
+    )(own, spill_far, spill_near, first, NATURAL)
     (out,) = call(
         final_kernel,
         [False] * 5,

time: 28.5 us -> 28.2 us (0.989)
  waiting for transfers between devices: 5.06 us -> 4.68 us
    ppermute x1 -> x2, waiting for transfers between devices: 1.44 us -> 1.14 us  [the longest x1 1.14 us: per_device(): cross = lax.ppermute(cross, 'tile', near_pairs)]
  transfers between devices with their start and end apart: 8 -> 9, of which waited for: 4 -> 4; matrix products, arithmetic and copies ran while one was open for 0% -> 0% of each run, Pallas kernels for 9% -> 9%
where the time goes in v6:
time: 28.2 us; the launch traced here: 27.8 us
  starting transfers between devices  15.3 us (54%)
  Pallas kernels  7.69 us (27%)
  waiting for transfers between devices  4.68 us (17%)
    ppermute x1, starting transfers between devices, per_device(): u_far = lax.ppermute(u_far, ('cuts', 'tile'), of_senders(far_pairs))  4.3 us
    pallas_call x1, Pallas kernels, per_device(): call(fine_kernel, [True] * 5, [(f32(3, 4, BLOCKS, 40, LANES), False), (f3...  4.12 us
    ppermute x1, starting transfers between devices, per_device(): spill_far = lax.ppermute(spill_far, 'tile', far_pairs)  3.37 us
    ppermute x1, starting transfers between devices, per_device(): first = lax.ppermute(early, 'cuts', [(0, 1), (1, 2)])  3.25 us
    ppermute x1, starting transfers between devices, per_device(): second = lax.ppermute(two, 'cuts', [(0, 2), (1, 3)])  2.15 us
    ppermute x1, waiting for transfers between devices, per_device(): u_near = lax.ppermute(u_near, 'tile', near_pairs)  1.4 us
    ppermute x1, starting transfers between devices, per_device(): third = lax.ppermute(three, 'cuts', [(0, 3)])  1.3 us
    pallas_call x1, Pallas kernels, per_device(): call(rest_kernel, [False] * 4, [coarse] * 4, state, name='rest')  1.21 us
  transfers between devices with their start and end apart: 9, of which 4 were waited for; matrix products, arithmetic and copies ran while one was open for 0% of the time, Pallas kernels for 9%

profile of v6, /device:TPU:16, one launch (start us, length us, event | category | flops | bytes accessed | tf_op | source)
XLA Modules:
  0.0 27.8 jit_solution(10144814397473888270)
XLA Ops:
  0.0 4.1 %fine.1 = (f32[3,4,4,40,128]{4,3,2,1,0:T(8,128)S(1)}, f32[3,2,4,16,128]{4,3,2,1,0:T(8,128)S(1)}, f32[3,2,4,24,128]{4,3,2,1,0:T(8,128)S(1)}, f32[344,128]{1,0:T(8...) custom-call(f32[3,16,2048]{2,1,0:T(8,128)} %bitcast.2, ...), custom_call_target="tpu_custom_call" | custom-call | tf_op jit(solution)/shard_map/fine/pallas_call | solution.py:611
  4.1 0.1 collective-permute-start
  4.2 1.4 %collective-permute-done.near = f32[344,128]{1,0:T(8,128)S(1)} collective-permute-done((f32[344,128]{1,0:T(8,128)S(1)}, f32[344,128]{1,0:T(8,128)S(1)}, u32[]{:S(2)}, u32[]{:S(2)}) %collective-permute-start) | collective-permute-done | bytes 176160 | tf_op jit(solution)/shard_map/ppermute | solution.py:645
  5.6 4.3 %collective-permute-start.3 = (f32[344,128]{1,0:T(8,128)S(1)}, f32[344,128]{1,0:T(8,128)S(1)}, u32[]{:S(2)}, u32[]{:S(2)}) collective-permute-start(f32[344,128]{1,0:T(8,128)S(1)} %join.1.arrived), channel_id=1, source_target_pairs={{1,2},{2,1},{3,4},{4,3},{5,6},{6,5},{7,8},{8,7},{9,10},{10,9},{11,... | collective-permute-start | bytes 528392 | tf_op jit(solution)/shard_map/ppermute | solution.py:654
  10.0 0.2 spill.1
  10.1 3.4 %collective-permute-start.1 = (f32[408,128]{1,0:T(8,128)S(1)}, f32[408,128]{1,0:T(8,128)S(1)}, u32[]{:S(2)}, u32[]{:S(2)}) collective-permute-start(f32[408,128]{1,0:T(8,128)S(1)} %get-tuple-element.25), channel_id=1, source_target_pairs={{1,2},{2,1},{3,4},{4,3},{5,6},{6,5},{7,8},{8,7},{9,10},{10,9},{11,... | collective-permute-start | bytes 626696 | tf_op jit(solution)/shard_map/ppermute | solution.py:655
  13.5 0.1 collective-permute-start.2
  13.6 0.9 %collective-permute-done.3.far = f32[344,128]{1,0:T(8,128)S(1)} collective-permute-done((f32[344,128]{1,0:T(8,128)S(1)}, f32[344,128]{1,0:T(8,128)S(1)}, u32[]{:S(2)}, u32[]{:S(2)}) %collective-permute-start.3) | collective-permute-done | bytes 176160 | tf_op jit(solution)/shard_map/ppermute | solution.py:654
  14.5 0.1 collective-permute-start.4
  14.6 0.0 copy-start.2
  14.7 0.1 assemble.1.assembled
  14.8 1.1 %collective-permute-done.4.cross = f32[152,128]{1,0:T(8,128)S(1)} collective-permute-done((f32[152,128]{1,0:T(8,128)S(1)}, f32[152,128]{1,0:T(8,128)S(1)}, u32[]{:S(2)}, u32[]{:S(2)}) %collective-permute-start.4) | collective-permute-done | bytes 77856 | tf_op jit(solution)/shard_map/ppermute | solution.py:658
  15.9 0.0 copy-done.2
  15.9 0.6 %first.1 = (f32[3,2,4,8,128]{4,3,2,1,0:T(8,128)S(1)}, f32[3,2,4,24,128]{4,3,2,1,0:T(8,128)S(1)}) custom-call(f32[3,2,4,48,128]{4,3,2,1,0:T(8,128)S(1)} %assemble.1.assembled, f32[152,128]{1,0:T(8,128)S(1)} %collective-permute-done.4.cross, bf16[2,512,512]{2,1,0:T(8,128)(2,1)S(1)} %get-tuple-element.28.inverse, f32[44,128]{1,0:T(8,128)S(1)} %copy-done.2), custom_call_target="tpu_custom_call" | custom-call | tf_op jit(solution)/shard_map/first/pallas_call | solution.py:673
  16.6 0.0 copy-start
  16.6 1.2 %rest.1 = (f32[3,2,4,8,128]{4,3,2,1,0:T(8,128)S(1)}, f32[3,2,4,8,128]{4,3,2,1,0:T(8,128)S(1)}, f32[3,2,4,8,128]{4,3,2,1,0:T(8,128)S(1)}, f32[3,2,4,8,128]{4,3,2,1,0:T(8,128)S(1)}) custom-call(f32[3,2,4,24,128]{4,3,2,1,0:T(8,128)S(1)} %get-tuple-element.29.wide, f32[3,2,4,8,128]{4,3,2,1,0:T(8,128)S(1)} %get-tuple-element.30.one, ...), custom_call_target="tpu_custom_call" | custom-call | tf_op jit(solution)/shard_map/rest/pallas_call | solution.py:676
  17.8 3.2 %collective-permute-start.5 = (f32[3,2,4,8,128]{4,3,2,1,0:T(8,128)S(1)}, f32[3,2,4,8,128]{4,3,2,1,0:T(8,128)S(1)}, u32[]{:S(2)}, u32[]{:S(2)}) collective-permute-start(f32[3,2,4,8,128]{4,3,2,1,0:T(8,128)S(1)} %get-tuple-element.31), channel_id=1, source_target_pairs={{0,32},{32,64},{1,33},{33,65},{2,34},{34,66},{3,35},{35,67},{4,36}... | collective-permute-start | bytes 294920 | tf_op jit(solution)/shard_map/ppermute | solution.py:679
  21.0 1.3 %collective-permute-start.6 = (f32[3,2,4,8,128]{4,3,2,1,0:T(8,128)S(1)}, f32[3,2,4,8,128]{4,3,2,1,0:T(8,128)S(1)}, u32[]{:S(2)}, u32[]{:S(2)}) collective-permute-start(f32[3,2,4,8,128]{4,3,2,1,0:T(8,128)S(1)} %get-tuple-element.32), channel_id=1, source_target_pairs={{0,96},{1,97},{2,98},{3,99},{4,100},{5,101},{6,102},{7,103},{8,104... | collective-permute-start | bytes 294920 | tf_op jit(solution)/shard_map/ppermute | solution.py:681
  22.3 2.1 %collective-permute-start.7 = (f32[3,2,4,8,128]{4,3,2,1,0:T(8,128)S(1)}, f32[3,2,4,8,128]{4,3,2,1,0:T(8,128)S(1)}, u32[]{:S(2)}, u32[]{:S(2)}) collective-permute-start(f32[3,2,4,8,128]{4,3,2,1,0:T(8,128)S(1)} %get-tuple-element.33), channel_id=1, source_target_pairs={{0,64},{32,96},{1,65},{33,97},{2,66},{34,98},{3,67},{35,99},{4,68}... | collective-permute-start | bytes 294920 | tf_op jit(solution)/shard_map/ppermute | solution.py:680
  24.5 0.0 collective-permute-done.1.far
  24.5 0.7 %collective-permute-start.8 = (f32[3,2,4,8,128]{4,3,2,1,0:T(8,128)S(1)}, f32[3,2,4,8,128]{4,3,2,1,0:T(8,128)S(1)}, u32[]{:S(2)}, u32[]{:S(2)}) collective-permute-start(f32[3,2,4,8,128]{4,3,2,1,0:T(8,128)S(1)} %get-tuple-element.34), channel_id=1, source_target_pairs={{64,96},{65,97},{66,98},{67,99},{68,100},{69,101},{70,102},{71,103... | collective-permute-start | bytes 294920 | tf_op jit(solution)/shard_map/ppermute | solution.py:682
  25.2 0.0 collective-permute-done.2.near
  25.2 0.0 collective-permute-done.5.first
  25.2 0.0 copy-done
  25.2 0.0 copy-start.1
  25.2 0.4 %natural.1.base_end = f32[3,16,2048]{2,1,0:T(8,128)S(1)} custom-call(f32[3,4,4,16,128]{4,3,2,1,0:T(8,128)S(1)} %get-tuple-element.24.own, f32[408,128]{1,0:T(8,128)S(1)} %collective-permute-done.1.far, f32[408,128]{1,0:T(8,128)S(1)} %collective-permute-done.2.near, f32[3,2,4,8,128]{4,3,2,1,0:T(8,128)S(1)} %collective-permute-done.5.first, ...), custom_call_target="tpu_custom_call" | custom-call | tf_op jit(solution)/shard_map/natural/pallas_call | solution.py:683
  25.7 1.2 %collective-permute-done.6.second = f32[3,2,4,8,128]{4,3,2,1,0:T(8,128)S(1)} collective-permute-done((f32[3,2,4,8,128]{4,3,2,1,0:T(8,128)S(1)}, f32[3,2,4,8,128]{4,3,2,1,0:T(8,128)S(1)}, u32[]{:S(2)}, u32[]{:S(2)}) %collective-permute-start.6) | collective-permute-done | bytes 98336 | tf_op jit(solution)/shard_map/ppermute | solution.py:681
  26.8 0.0 collective-permute-done.7.third
  26.9 0.0 collective-permute-done.8.fourth
  26.9 0.0 copy-done.1
  26.9 1.0 %final.1 = f32[3,16,2048]{2,1,0:T(8,128)} custom-call(f32[3,16,2048]{2,1,0:T(8,128)S(1)} %natural.1.base_end, f32[3,2,4,8,128]{4,3,2,1,0:T(8,128)S(1)} %collective-permute-done.6.second, f32[3,2,4,8,128]{4,3,2,1,0:T(8,128)S(1)} %collective-permute-done.7.third, f32[3,2,4,8,128]{4,3,2,1,0:T(8,128)S(1)} %collective-permute-done.8.fourth, ...), custom_call_target="tpu_custom_call" | custom-call | tf_op jit(solution)/shard_map/final/pallas_call | solution.py:690
  (2 shorter events, 0.0 us)
Async XLA Ops:
  4.1 1.5 %collective-permute-start = (f32[344,128]{1,0:T(8,128)S(1)}, f32[344,128]{1,0:T(8,128)S(1)}, u32[]{:S(2)}, u32[]{:S(2)}) collective-permute-start(f32[344,128]{1,0:T(8,128)S(1)} %get-tuple-element.23), channel_id=1, source_target_pairs={{0,1},{1,0},{2,3},{3,2},{4,5},{5,4},{6,7},{7,6},{8,9},{9,8},{10,11... | collective-permute-start | bytes 528392 | tf_op jit(solution)/shard_map/ppermute | solution.py:645
  5.6 8.9 %collective-permute-start.3 = (f32[344,128]{1,0:T(8,128)S(1)}, f32[344,128]{1,0:T(8,128)S(1)}, u32[]{:S(2)}, u32[]{:S(2)}) collective-permute-start(f32[344,128]{1,0:T(8,128)S(1)} %join.1.arrived), channel_id=1, source_target_pairs={{1,2},{2,1},{3,4},{4,3},{5,6},{6,5},{7,8},{8,7},{9,10},{10,9},{11,... | collective-permute-start | bytes 528392 | tf_op jit(solution)/shard_map/ppermute | solution.py:654
  10.1 14.4 %collective-permute-start.1 = (f32[408,128]{1,0:T(8,128)S(1)}, f32[408,128]{1,0:T(8,128)S(1)}, u32[]{:S(2)}, u32[]{:S(2)}) collective-permute-start(f32[408,128]{1,0:T(8,128)S(1)} %get-tuple-element.25), channel_id=1, source_target_pairs={{1,2},{2,1},{3,4},{4,3},{5,6},{6,5},{7,8},{8,7},{9,10},{10,9},{11,... | collective-permute-start | bytes 626696 | tf_op jit(solution)/shard_map/ppermute | solution.py:655
  13.5 11.7 %collective-permute-start.2 = (f32[408,128]{1,0:T(8,128)S(1)}, f32[408,128]{1,0:T(8,128)S(1)}, u32[]{:S(2)}, u32[]{:S(2)}) collective-permute-start(f32[408,128]{1,0:T(8,128)S(1)} %get-tuple-element.26), channel_id=1, source_target_pairs={{0,1},{1,0},{2,3},{3,2},{4,5},{5,4},{6,7},{7,6},{8,9},{9,8},{10,11... | collective-permute-start | bytes 626696 | tf_op jit(solution)/shard_map/ppermute | solution.py:656
  14.5 1.4 %collective-permute-start.4 = (f32[152,128]{1,0:T(8,128)S(1)}, f32[152,128]{1,0:T(8,128)S(1)}, u32[]{:S(2)}, u32[]{:S(2)}) collective-permute-start(f32[152,128]{1,0:T(8,128)S(1)} %forward.1), channel_id=1, source_target_pairs={{0,1},{1,0},{2,3},{3,2},{4,5},{5,4},{6,7},{7,6},{8,9},{9,8},{10,11... | collective-permute-start | bytes 233480 | tf_op jit(solution)/shard_map/ppermute | solution.py:658
  14.6 1.3 %copy-start.2 = (f32[44,128]{1,0:T(8,128)S(1)}, f32[44,128]{1,0:T(8,128)}, u32[]{:S(2)}) copy-start(f32[44,128]{1,0:T(8,128)} %constant.15.clone.coarse_table_hbm.table) | copy-start | bytes 67588
  16.6 8.7 %copy-start = (bf16[512,512]{1,0:T(8,128)(2,1)S(1)}, bf16[512,512]{1,0:T(8,128)(2,1)}, u32[]{:S(2)}) copy-start(bf16[512,512]{1,0:T(8,128)(2,1)} %constant.16.clone.matrix) | copy-start | bytes 1572868
  17.8 7.4 %collective-permute-start.5 = (f32[3,2,4,8,128]{4,3,2,1,0:T(8,128)S(1)}, f32[3,2,4,8,128]{4,3,2,1,0:T(8,128)S(1)}, u32[]{:S(2)}, u32[]{:S(2)}) collective-permute-start(f32[3,2,4,8,128]{4,3,2,1,0:T(8,128)S(1)} %get-tuple-element.31), channel_id=1, source_target_pairs={{0,32},{32,64},{1,33},{33,65},{2,34},{34,66},{3,35},{35,67},{4,36}... | collective-permute-start | bytes 294920 | tf_op jit(solution)/shard_map/ppermute | solution.py:679
  21.0 5.8 %collective-permute-start.6 = (f32[3,2,4,8,128]{4,3,2,1,0:T(8,128)S(1)}, f32[3,2,4,8,128]{4,3,2,1,0:T(8,128)S(1)}, u32[]{:S(2)}, u32[]{:S(2)}) collective-permute-start(f32[3,2,4,8,128]{4,3,2,1,0:T(8,128)S(1)} %get-tuple-element.32), channel_id=1, source_target_pairs={{0,96},{1,97},{2,98},{3,99},{4,100},{5,101},{6,102},{7,103},{8,104... | collective-permute-start | bytes 294920 | tf_op jit(solution)/shard_map/ppermute | solution.py:681
  22.3 4.5 %collective-permute-start.7 = (f32[3,2,4,8,128]{4,3,2,1,0:T(8,128)S(1)}, f32[3,2,4,8,128]{4,3,2,1,0:T(8,128)S(1)}, u32[]{:S(2)}, u32[]{:S(2)}) collective-permute-start(f32[3,2,4,8,128]{4,3,2,1,0:T(8,128)S(1)} %get-tuple-element.33), channel_id=1, source_target_pairs={{0,64},{32,96},{1,65},{33,97},{2,66},{34,98},{3,67},{35,99},{4,68}... | collective-permute-start | bytes 294920 | tf_op jit(solution)/shard_map/ppermute | solution.py:680
  24.5 2.3 %collective-permute-start.8 = (f32[3,2,4,8,128]{4,3,2,1,0:T(8,128)S(1)}, f32[3,2,4,8,128]{4,3,2,1,0:T(8,128)S(1)}, u32[]{:S(2)}, u32[]{:S(2)}) collective-permute-start(f32[3,2,4,8,128]{4,3,2,1,0:T(8,128)S(1)} %get-tuple-element.34), channel_id=1, source_target_pairs={{64,96},{65,97},{66,98},{67,99},{68,100},{69,101},{70,102},{71,103... | collective-permute-start | bytes 294920 | tf_op jit(solution)/shard_map/ppermute | solution.py:682
  25.2 1.6 %copy-start.1 = (bf16[256,512]{1,0:T(8,128)(2,1)S(1)}, bf16[256,512]{1,0:T(8,128)(2,1)}, u32[]{:S(2)}) copy-start(bf16[256,512]{1,0:T(8,128)(2,1)} %constant.17.clone.matrix) | copy-start | bytes 786436

commit v7 on v6

--- a/solution.py
+++ b/solution.py
@@ -403,7 +403,7 @@
         wide_end[c, p, a] = source[4:44, :]
 
 
-def spill_kernel(wide_end, propagated, arrived, own, to_far, to_near, rows):
+def spill_kernel(wide_end, propagated, arrived, own, to_far, to_near, rows, total):
     del arrived
     odd = on_odd()
     for c, p, a in planes(2):
@@ -413,10 +413,12 @@
     for c, p, a in planes(4):
         start, count = SPILL[c]
         base = (p * BLOCKS + a) * SPILL_ROWS + start
-        wide_end[c, p, a, 4:36, :] = wide_end[c, p, a, 4:36, :] - rows[c, p // 2, a]
-        own[c, p, a] = wide_end[c, p, a, 12:28, :]
-        to_next = wide_end[c, p, a, 28 : 28 + count, :]
-        to_previous = wide_end[c, p, a, 12 - count : 12, :]
+        to = total.at[c, p, a]
+        to[0:40, :] = wide_end[c, p, a]
+        to[4:36, :] = to[4:36, :] - rows[c, p // 2, a]
+        own[c, p, a] = to[12:28, :]
+        to_next = to[28 : 28 + count, :]
+        to_previous = to[12 - count : 12, :]
         to_far[base : base + count, :] = jnp.where(odd, to_next, to_previous)
         to_near[base : base + count, :] = jnp.where(odd, to_previous, to_next)
 
@@ -648,7 +650,7 @@
         spill_kernel,
         [False] * 3,
         [(f32(3, 4, BLOCKS, ROWS, LANES), False), spilt, spilt],
-        [scratch(3, 2, BLOCKS, 32, LANES)],
+        [scratch(3, 2, BLOCKS, 32, LANES), scratch(3, 4, BLOCKS, 48, LANES)],
         name="spill",
     )(wide_end, propagated, u_far)
     u_far = lax.ppermute(u_far, ("cuts", "tile"), of_senders(far_pairs))

time: 28.2 us -> 28.2 us (level)
  transfers between devices with their start and end apart: 9 -> 9, of which waited for: 4 -> 4; matrix products, arithmetic and copies ran while one was open for 0% -> 0% of each run, Pallas kernels for 9% -> 10%
where the time goes in v7:
time: 28.2 us; the launch traced here: 27.8 us
  starting transfers between devices  15.3 us (54%)
  Pallas kernels  7.8 us (28%)
  waiting for transfers between devices  4.56 us (16%)
    ppermute x1, starting transfers between devices, per_device(): u_far = lax.ppermute(u_far, ('cuts', 'tile'), of_senders(far_pairs))  4.3 us
    pallas_call x1, Pallas kernels, per_device(): call(fine_kernel, [True] * 5, [(f32(3, 4, BLOCKS, 40, LANES), False), (f3...  4.12 us
    ppermute x1, starting transfers between devices, per_device(): spill_far = lax.ppermute(spill_far, 'tile', far_pairs)  3.37 us
    ppermute x1, starting transfers between devices, per_device(): first = lax.ppermute(early, 'cuts', [(0, 1), (1, 2)])  3.25 us
    ppermute x1, starting transfers between devices, per_device(): second = lax.ppermute(two, 'cuts', [(0, 2), (1, 3)])  2.15 us
    ppermute x1, waiting for transfers between devices, per_device(): u_near = lax.ppermute(u_near, 'tile', near_pairs)  1.4 us
    ppermute x1, starting transfers between devices, per_device(): third = lax.ppermute(three, 'cuts', [(0, 3)])  1.3 us
    pallas_call x1, Pallas kernels, per_device(): call(rest_kernel, [False] * 4, [coarse] * 4, state, name='rest')  1.21 us
  transfers between devices with their start and end apart: 9, of which 4 were waited for; matrix products, arithmetic and copies ran while one was open for 0% of the time, Pallas kernels for 10%

profile of v7, /device:TPU:16, one launch (start us, length us, event | category | flops | bytes accessed | tf_op | source)
XLA Modules:
  0.0 27.8 jit_solution(9219097213375044957)
XLA Ops:
  0.0 4.1 %fine.1 = (f32[3,4,4,40,128]{4,3,2,1,0:T(8,128)S(1)}, f32[3,2,4,16,128]{4,3,2,1,0:T(8,128)S(1)}, f32[3,2,4,24,128]{4,3,2,1,0:T(8,128)S(1)}, f32[344,128]{1,0:T(8...) custom-call(f32[3,16,2048]{2,1,0:T(8,128)} %bitcast.2, ...), custom_call_target="tpu_custom_call" | custom-call | tf_op jit(solution)/shard_map/fine/pallas_call | solution.py:613
  4.1 0.1 collective-permute-start
  4.2 1.4 %collective-permute-done.near = f32[344,128]{1,0:T(8,128)S(1)} collective-permute-done((f32[344,128]{1,0:T(8,128)S(1)}, f32[344,128]{1,0:T(8,128)S(1)}, u32[]{:S(2)}, u32[]{:S(2)}) %collective-permute-start) | collective-permute-done | bytes 176160 | tf_op jit(solution)/shard_map/ppermute | solution.py:647
  5.6 4.3 %collective-permute-start.3 = (f32[344,128]{1,0:T(8,128)S(1)}, f32[344,128]{1,0:T(8,128)S(1)}, u32[]{:S(2)}, u32[]{:S(2)}) collective-permute-start(f32[344,128]{1,0:T(8,128)S(1)} %join.1.arrived), channel_id=1, source_target_pairs={{1,2},{2,1},{3,4},{4,3},{5,6},{6,5},{7,8},{8,7},{9,10},{10,9},{11,... | collective-permute-start | bytes 528392 | tf_op jit(solution)/shard_map/ppermute | solution.py:656
  10.0 0.3 spill.1
  10.2 3.4 %collective-permute-start.1 = (f32[408,128]{1,0:T(8,128)S(1)}, f32[408,128]{1,0:T(8,128)S(1)}, u32[]{:S(2)}, u32[]{:S(2)}) collective-permute-start(f32[408,128]{1,0:T(8,128)S(1)} %get-tuple-element.25), channel_id=1, source_target_pairs={{1,2},{2,1},{3,4},{4,3},{5,6},{6,5},{7,8},{8,7},{9,10},{10,9},{11,... | collective-permute-start | bytes 626696 | tf_op jit(solution)/shard_map/ppermute | solution.py:657
  13.6 0.1 collective-permute-start.2
  13.7 0.8 %collective-permute-done.3.far = f32[344,128]{1,0:T(8,128)S(1)} collective-permute-done((f32[344,128]{1,0:T(8,128)S(1)}, f32[344,128]{1,0:T(8,128)S(1)}, u32[]{:S(2)}, u32[]{:S(2)}) %collective-permute-start.3) | collective-permute-done | bytes 176160 | tf_op jit(solution)/shard_map/ppermute | solution.py:656
  14.5 0.1 collective-permute-start.4
  14.6 0.0 copy-start.2
  14.7 0.1 assemble.1.assembled
  14.8 1.1 %collective-permute-done.4.cross = f32[152,128]{1,0:T(8,128)S(1)} collective-permute-done((f32[152,128]{1,0:T(8,128)S(1)}, f32[152,128]{1,0:T(8,128)S(1)}, u32[]{:S(2)}, u32[]{:S(2)}) %collective-permute-start.4) | collective-permute-done | bytes 77856 | tf_op jit(solution)/shard_map/ppermute | solution.py:660
  15.9 0.0 copy-done.2
  15.9 0.6 %first.1 = (f32[3,2,4,8,128]{4,3,2,1,0:T(8,128)S(1)}, f32[3,2,4,24,128]{4,3,2,1,0:T(8,128)S(1)}) custom-call(f32[3,2,4,48,128]{4,3,2,1,0:T(8,128)S(1)} %assemble.1.assembled, f32[152,128]{1,0:T(8,128)S(1)} %collective-permute-done.4.cross, bf16[2,512,512]{2,1,0:T(8,128)(2,1)S(1)} %get-tuple-element.28.inverse, f32[44,128]{1,0:T(8,128)S(1)} %copy-done.2), custom_call_target="tpu_custom_call" | custom-call | tf_op jit(solution)/shard_map/first/pallas_call | solution.py:675
  16.6 0.0 copy-start
  16.6 1.2 %rest.1 = (f32[3,2,4,8,128]{4,3,2,1,0:T(8,128)S(1)}, f32[3,2,4,8,128]{4,3,2,1,0:T(8,128)S(1)}, f32[3,2,4,8,128]{4,3,2,1,0:T(8,128)S(1)}, f32[3,2,4,8,128]{4,3,2,1,0:T(8,128)S(1)}) custom-call(f32[3,2,4,24,128]{4,3,2,1,0:T(8,128)S(1)} %get-tuple-element.29.wide, f32[3,2,4,8,128]{4,3,2,1,0:T(8,128)S(1)} %get-tuple-element.30.one, ...), custom_call_target="tpu_custom_call" | custom-call | tf_op jit(solution)/shard_map/rest/pallas_call | solution.py:678
  17.8 3.2 %collective-permute-start.5 = (f32[3,2,4,8,128]{4,3,2,1,0:T(8,128)S(1)}, f32[3,2,4,8,128]{4,3,2,1,0:T(8,128)S(1)}, u32[]{:S(2)}, u32[]{:S(2)}) collective-permute-start(f32[3,2,4,8,128]{4,3,2,1,0:T(8,128)S(1)} %get-tuple-element.31), channel_id=1, source_target_pairs={{0,32},{32,64},{1,33},{33,65},{2,34},{34,66},{3,35},{35,67},{4,36}... | collective-permute-start | bytes 294920 | tf_op jit(solution)/shard_map/ppermute | solution.py:681
  21.0 1.3 %collective-permute-start.6 = (f32[3,2,4,8,128]{4,3,2,1,0:T(8,128)S(1)}, f32[3,2,4,8,128]{4,3,2,1,0:T(8,128)S(1)}, u32[]{:S(2)}, u32[]{:S(2)}) collective-permute-start(f32[3,2,4,8,128]{4,3,2,1,0:T(8,128)S(1)} %get-tuple-element.32), channel_id=1, source_target_pairs={{0,96},{1,97},{2,98},{3,99},{4,100},{5,101},{6,102},{7,103},{8,104... | collective-permute-start | bytes 294920 | tf_op jit(solution)/shard_map/ppermute | solution.py:683
  22.3 2.1 %collective-permute-start.7 = (f32[3,2,4,8,128]{4,3,2,1,0:T(8,128)S(1)}, f32[3,2,4,8,128]{4,3,2,1,0:T(8,128)S(1)}, u32[]{:S(2)}, u32[]{:S(2)}) collective-permute-start(f32[3,2,4,8,128]{4,3,2,1,0:T(8,128)S(1)} %get-tuple-element.33), channel_id=1, source_target_pairs={{0,64},{32,96},{1,65},{33,97},{2,66},{34,98},{3,67},{35,99},{4,68}... | collective-permute-start | bytes 294920 | tf_op jit(solution)/shard_map/ppermute | solution.py:682
  24.5 0.0 collective-permute-done.1.far
  24.5 0.7 %collective-permute-start.8 = (f32[3,2,4,8,128]{4,3,2,1,0:T(8,128)S(1)}, f32[3,2,4,8,128]{4,3,2,1,0:T(8,128)S(1)}, u32[]{:S(2)}, u32[]{:S(2)}) collective-permute-start(f32[3,2,4,8,128]{4,3,2,1,0:T(8,128)S(1)} %get-tuple-element.34), channel_id=1, source_target_pairs={{64,96},{65,97},{66,98},{67,99},{68,100},{69,101},{70,102},{71,103... | collective-permute-start | bytes 294920 | tf_op jit(solution)/shard_map/ppermute | solution.py:684
  25.2 0.0 collective-permute-done.2.near
  25.2 0.0 collective-permute-done.5.first
  25.2 0.0 copy-done
  25.2 0.0 copy-start.1
  25.2 0.4 %natural.1.base_end = f32[3,16,2048]{2,1,0:T(8,128)S(1)} custom-call(f32[3,4,4,16,128]{4,3,2,1,0:T(8,128)S(1)} %get-tuple-element.24.own, f32[408,128]{1,0:T(8,128)S(1)} %collective-permute-done.1.far, f32[408,128]{1,0:T(8,128)S(1)} %collective-permute-done.2.near, f32[3,2,4,8,128]{4,3,2,1,0:T(8,128)S(1)} %collective-permute-done.5.first, ...), custom_call_target="tpu_custom_call" | custom-call | tf_op jit(solution)/shard_map/natural/pallas_call | solution.py:685
  25.7 1.2 %collective-permute-done.6.second = f32[3,2,4,8,128]{4,3,2,1,0:T(8,128)S(1)} collective-permute-done((f32[3,2,4,8,128]{4,3,2,1,0:T(8,128)S(1)}, f32[3,2,4,8,128]{4,3,2,1,0:T(8,128)S(1)}, u32[]{:S(2)}, u32[]{:S(2)}) %collective-permute-start.6) | collective-permute-done | bytes 98336 | tf_op jit(solution)/shard_map/ppermute | solution.py:683
  26.8 0.0 collective-permute-done.7.third
  26.9 0.0 collective-permute-done.8.fourth
  26.9 0.0 copy-done.1
  26.9 1.0 %final.1 = f32[3,16,2048]{2,1,0:T(8,128)} custom-call(f32[3,16,2048]{2,1,0:T(8,128)S(1)} %natural.1.base_end, f32[3,2,4,8,128]{4,3,2,1,0:T(8,128)S(1)} %collective-permute-done.6.second, f32[3,2,4,8,128]{4,3,2,1,0:T(8,128)S(1)} %collective-permute-done.7.third, f32[3,2,4,8,128]{4,3,2,1,0:T(8,128)S(1)} %collective-permute-done.8.fourth, ...), custom_call_target="tpu_custom_call" | custom-call | tf_op jit(solution)/shard_map/final/pallas_call | solution.py:692
  (2 shorter events, 0.0 us)
Async XLA Ops:
  4.1 1.5 %collective-permute-start = (f32[344,128]{1,0:T(8,128)S(1)}, f32[344,128]{1,0:T(8,128)S(1)}, u32[]{:S(2)}, u32[]{:S(2)}) collective-permute-start(f32[344,128]{1,0:T(8,128)S(1)} %get-tuple-element.23), channel_id=1, source_target_pairs={{0,1},{1,0},{2,3},{3,2},{4,5},{5,4},{6,7},{7,6},{8,9},{9,8},{10,11... | collective-permute-start | bytes 528392 | tf_op jit(solution)/shard_map/ppermute | solution.py:647
  5.6 8.9 %collective-permute-start.3 = (f32[344,128]{1,0:T(8,128)S(1)}, f32[344,128]{1,0:T(8,128)S(1)}, u32[]{:S(2)}, u32[]{:S(2)}) collective-permute-start(f32[344,128]{1,0:T(8,128)S(1)} %join.1.arrived), channel_id=1, source_target_pairs={{1,2},{2,1},{3,4},{4,3},{5,6},{6,5},{7,8},{8,7},{9,10},{10,9},{11,... | collective-permute-start | bytes 528392 | tf_op jit(solution)/shard_map/ppermute | solution.py:656
  10.2 14.3 %collective-permute-start.1 = (f32[408,128]{1,0:T(8,128)S(1)}, f32[408,128]{1,0:T(8,128)S(1)}, u32[]{:S(2)}, u32[]{:S(2)}) collective-permute-start(f32[408,128]{1,0:T(8,128)S(1)} %get-tuple-element.25), channel_id=1, source_target_pairs={{1,2},{2,1},{3,4},{4,3},{5,6},{6,5},{7,8},{8,7},{9,10},{10,9},{11,... | collective-permute-start | bytes 626696 | tf_op jit(solution)/shard_map/ppermute | solution.py:657
  13.6 11.6 %collective-permute-start.2 = (f32[408,128]{1,0:T(8,128)S(1)}, f32[408,128]{1,0:T(8,128)S(1)}, u32[]{:S(2)}, u32[]{:S(2)}) collective-permute-start(f32[408,128]{1,0:T(8,128)S(1)} %get-tuple-element.26), channel_id=1, source_target_pairs={{0,1},{1,0},{2,3},{3,2},{4,5},{5,4},{6,7},{7,6},{8,9},{9,8},{10,11... | collective-permute-start | bytes 626696 | tf_op jit(solution)/shard_map/ppermute | solution.py:658
  14.5 1.4 %collective-permute-start.4 = (f32[152,128]{1,0:T(8,128)S(1)}, f32[152,128]{1,0:T(8,128)S(1)}, u32[]{:S(2)}, u32[]{:S(2)}) collective-permute-start(f32[152,128]{1,0:T(8,128)S(1)} %forward.1), channel_id=1, source_target_pairs={{0,1},{1,0},{2,3},{3,2},{4,5},{5,4},{6,7},{7,6},{8,9},{9,8},{10,11... | collective-permute-start | bytes 233480 | tf_op jit(solution)/shard_map/ppermute | solution.py:660
  14.6 1.3 %copy-start.2 = (f32[44,128]{1,0:T(8,128)S(1)}, f32[44,128]{1,0:T(8,128)}, u32[]{:S(2)}) copy-start(f32[44,128]{1,0:T(8,128)} %constant.15.clone.coarse_table_hbm.table) | copy-start | bytes 67588
  16.6 8.7 %copy-start = (bf16[512,512]{1,0:T(8,128)(2,1)S(1)}, bf16[512,512]{1,0:T(8,128)(2,1)}, u32[]{:S(2)}) copy-start(bf16[512,512]{1,0:T(8,128)(2,1)} %constant.16.clone.matrix) | copy-start | bytes 1572868
  17.8 7.4 %collective-permute-start.5 = (f32[3,2,4,8,128]{4,3,2,1,0:T(8,128)S(1)}, f32[3,2,4,8,128]{4,3,2,1,0:T(8,128)S(1)}, u32[]{:S(2)}, u32[]{:S(2)}) collective-permute-start(f32[3,2,4,8,128]{4,3,2,1,0:T(8,128)S(1)} %get-tuple-element.31), channel_id=1, source_target_pairs={{0,32},{32,64},{1,33},{33,65},{2,34},{34,66},{3,35},{35,67},{4,36}... | collective-permute-start | bytes 294920 | tf_op jit(solution)/shard_map/ppermute | solution.py:681
  21.0 5.8 %collective-permute-start.6 = (f32[3,2,4,8,128]{4,3,2,1,0:T(8,128)S(1)}, f32[3,2,4,8,128]{4,3,2,1,0:T(8,128)S(1)}, u32[]{:S(2)}, u32[]{:S(2)}) collective-permute-start(f32[3,2,4,8,128]{4,3,2,1,0:T(8,128)S(1)} %get-tuple-element.32), channel_id=1, source_target_pairs={{0,96},{1,97},{2,98},{3,99},{4,100},{5,101},{6,102},{7,103},{8,104... | collective-permute-start | bytes 294920 | tf_op jit(solution)/shard_map/ppermute | solution.py:683
  22.3 4.5 %collective-permute-start.7 = (f32[3,2,4,8,128]{4,3,2,1,0:T(8,128)S(1)}, f32[3,2,4,8,128]{4,3,2,1,0:T(8,128)S(1)}, u32[]{:S(2)}, u32[]{:S(2)}) collective-permute-start(f32[3,2,4,8,128]{4,3,2,1,0:T(8,128)S(1)} %get-tuple-element.33), channel_id=1, source_target_pairs={{0,64},{32,96},{1,65},{33,97},{2,66},{34,98},{3,67},{35,99},{4,68}... | collective-permute-start | bytes 294920 | tf_op jit(solution)/shard_map/ppermute | solution.py:682
  24.5 2.3 %collective-permute-start.8 = (f32[3,2,4,8,128]{4,3,2,1,0:T(8,128)S(1)}, f32[3,2,4,8,128]{4,3,2,1,0:T(8,128)S(1)}, u32[]{:S(2)}, u32[]{:S(2)}) collective-permute-start(f32[3,2,4,8,128]{4,3,2,1,0:T(8,128)S(1)} %get-tuple-element.34), channel_id=1, source_target_pairs={{64,96},{65,97},{66,98},{67,99},{68,100},{69,101},{70,102},{71,103... | collective-permute-start | bytes 294920 | tf_op jit(solution)/shard_map/ppermute | solution.py:684
  25.2 1.6 %copy-start.1 = (bf16[256,512]{1,0:T(8,128)(2,1)S(1)}, bf16[256,512]{1,0:T(8,128)(2,1)}, u32[]{:S(2)}) copy-start(bf16[256,512]{1,0:T(8,128)(2,1)} %constant.17.clone.matrix) | copy-start | bytes 786436
